TPU v7x, 256 devices: a whole 4x4x8 slice. The times are simulated.
256 devices in a mesh: row: 16 (over y, x), col: 16 (over z, core).
Axes of the slice: x: 4, y: 4, z: 8, core: 2. Of those that a mesh axis runs over, the one named last changes fastest.
Arguments:
- matrix: bfloat16 [8192, 8192], P('row', 'col'), may hold values from -0.1875 to 0.1875
- pattern: int32 [128, 128], P('row', 'col'), may hold values 0 or 1
Outputs:
- sign_step: bfloat16 [8192, 8192], P('row', 'col')
All inputs are finite; a program needn't handle non-finite values. No bound on the sum of `pattern` on one device may be relied on, other than what follows from the above.
Results may differ from a plain program's by a relative error of at most 0.0042.
Values may be sent and summed in bfloat16 or wider, within the bound.
No kernel may reach another device: no remote copies, remote signals or barrier semaphores. Data moves between devices by JAX's collectives and lax.ppermute only.
A program may use at most 64 MiB of HBM per device.

v0:
```python
import jax
import jax.numpy as jnp
from jax import lax
from jax.sharding import PartitionSpec as P

BLK = 64


def gather_right(operand):
    return lax.all_gather(operand, "row", axis=0, tiled=True)


def multiply_passed(left, right):
    gathered = gather_right(right)
    return jnp.dot(
        lax.all_gather(left, "col", axis=1, tiled=True),
        gathered,
        preferred_element_type=jnp.float32,
    )


def local(matrix, pattern):
    keep = jnp.repeat(jnp.repeat(pattern, BLK, axis=0), BLK, axis=1)
    keep_float = keep.astype(jnp.float32)
    masked = jnp.where(keep == 1, matrix, jnp.zeros_like(matrix))
    rows_local = matrix.shape[0]
    cols_local = matrix.shape[1]
    row_ids = lax.axis_index("row") * rows_local + jnp.arange(rows_local, dtype=jnp.int32)
    col_ids = lax.axis_index("col") * cols_local + jnp.arange(cols_local, dtype=jnp.int32)
    identity = (row_ids[:, None] == col_ids[None, :]).astype(jnp.float32)
    square = keep_float * multiply_passed(masked, masked)
    middle = (1.5 * identity - 0.5 * square).astype(jnp.bfloat16)
    product = multiply_passed(masked, middle)
    return (keep_float * product).astype(jnp.bfloat16)


def solution(mesh):
    in_specs = (P("row", "col"), P("row", "col"))
    out_specs = P("row", "col")
    return jax.shard_map(local, mesh=mesh, in_specs=in_specs, out_specs=out_specs, check_vma=False)
```

profile of v0, /device:TPU:1, one launch (start us, length us, event | category | flops | bytes accessed | tf_op | source)
XLA Modules:
  0.0 264.8 jit_solution(9871183105975283187)
XLA Ops:
  6.5 0.0 all-gather.4.cloned.1.call-start
  6.5 0.7 broadcast_compare_fusion
  7.2 0.1 copy.4
  7.3 0.1 broadcast_in_dim.17
  7.4 0.1 eq.29
  7.5 1.3 copy.5
  8.8 0.8 bitcast_select_fusion
  9.6 0.0 all-gather.4.cloned.1.call-update
  9.6 0.0 all-gather.6.cloned.1.call-start
  9.7 0.7 all-gather.6.cloned.1.call-update
  10.4 0.0 all-gather.8.cloned.1.call-start
  10.4 0.7 convert_element_type.18
  11.1 0.1 copy.3
  11.2 0.1 broadcast_in_dim.15
  11.3 0.1 convert_element_type.19
  11.3 58.6 %all-gather.4.cloned.1.call-done = bf16[512,8192]{0,1:T(8,128)(2,1)} async-done(((bf16[512,512]{0,1:T(8,128)(2,1)}), bf16[512,8192]{0,1:T(8,128)(2,1)}) %all-gather.4.cloned.1.call-update) | async-done | bytes 8388624 | tf_op jit(solution)/shard_map/all_gather | solution.py:16
  69.9 83.1 %all-gather.6.cloned.1.call-done = bf16[8192,512]{0,1:T(8,128)(2,1)} async-done(((bf16[512,512]{0,1:T(8,128)(2,1)}), bf16[8192,512]{0,1:T(8,128)(2,1)}) %all-gather.6.cloned.1.call-update) | async-done | bytes 8388624 | tf_op jit(solution)/shard_map/all_gather | solution.py:10
  153.0 0.1 broadcast_in_dim.16
  153.1 11.1 %fusion.3 = bf16[512,512]{0,1:T(8,128)(2,1)} fusion(f32[512,512]{0,1:T(8,128)S(1)} %bitcast.11, bf16[8192,512]{0,1:T(8,128)(2,1)} %all-gather.6.cloned.1.call-done, bf16[512,8192]{0,1:T(8,128)(2,1)} %all-gather.4.cloned.1.call-done, s32[512]{0:T(512)S(1)} %get-tuple-element.6, s32[512]{0:T(512)S(1)} %get-tuple-element.5), kind=kOutput, calls=%fused_computation.5 | convolution fusion | flops 4296540160 | bytes 18354176 | tf_op jit(solution)/shard_map/dot_general | solution.py:15
  164.2 0.0 all-gather.8.cloned.1.call-update
  164.2 0.3 copy.6
  164.5 82.6 %all-gather.8.cloned.1.call-done = bf16[8192,512]{0,1:T(8,128)(2,1)} async-done(((bf16[512,512]{0,1:T(8,128)(2,1)}), bf16[8192,512]{0,1:T(8,128)(2,1)}) %all-gather.8.cloned.1.call-update) | async-done | bytes 8388624 | tf_op jit(solution)/shard_map/all_gather | solution.py:10
  247.2 11.1 %fusion.2 = bf16[512,512]{1,0:T(8,128)(2,1)} fusion(f32[512,512]{1,0:T(8,128)S(1)} %copy.6, bf16[512,8192]{0,1:T(8,128)(2,1)} %all-gather.4.cloned.1.call-done, bf16[8192,512]{0,1:T(8,128)(2,1)} %all-gather.8.cloned.1.call-done), kind=kOutput, calls=%fused_computation.4 | convolution fusion | flops 4295491584 | bytes 18350080 | tf_op jit(solution)/shard_map/dot_general | solution.py:15
  (1 shorter events, 0.0 us)
Async XLA Ops:
  6.5 63.4 %all-gather.4.cloned.1.call-start = ((), (), s32[]{:S(2)}) async-start(), calls=%async_computation | async-start | bytes 8912896 | tf_op jit(solution)/shard_map/all_gather | solution.py:16
  9.6 143.4 %all-gather.6.cloned.1.call-start = ((), (), s32[]{:S(2)}) async-start(), calls=%async_computation.1 | async-start | bytes 8912896 | tf_op jit(solution)/shard_map/all_gather | solution.py:10
  10.4 236.8 %all-gather.8.cloned.1.call-start = ((), (), s32[]{:S(2)}) async-start(), calls=%async_computation.2 | async-start | bytes 8912896 | tf_op jit(solution)/shard_map/all_gather | solution.py:10
Sparse Core Ops, SparseCore 0:
  9.7 60.1 all-gather.3
  72.3 80.6 all-gather.5
  164.3 82.7 all-gather.7
where the time goes:
time: 265 us
  waiting for transfers between devices  225 us (85%)
  matrix products  22.2 us (8%)
  between operations  13.1 us (5%)
    all_gather x2, waiting for transfers between devices, gather_right(): return lax.all_gather(operand, 'row', axis=0, tiled=True)  166 us
    all_gather x1, waiting for transfers between devices, multiply_passed(): lax.all_gather(left, 'col', axis=1, tiled=True)  58.6 us
    dot_general x2, matrix products, multiply_passed(): jnp.dot(lax.all_gather(left, 'col', axis=1, tiled=True), gathered, prefer...  22.2 us
  transfers between devices with their start and end apart: 3, of which 3 were waited for; matrix products, arithmetic and copies ran while one was open for 0% of the time, Pallas kernels for 0%

commit v1 on v0

v1 whole, which is shorter than its diff:
```python
import functools

import jax
import jax.numpy as jnp
from jax import lax
from jax.experimental import pallas as pl
from jax.experimental.pallas import tpu as pltpu
from jax.sharding import PartitionSpec as P

BLK = 64
SIDE = 4
CHUNKS = 2
AXES = ("row", "col")
F32 = jnp.float32
BF16 = jnp.bfloat16


def device(y, x, z, c):
    return ((y % SIDE) * SIDE + x % SIDE) * 16 + z * 2 + c


def shift_perm(dy, dx):
    return [
        (device(y, x, z, c), device(y + dy, x + dx, z, c))
        for y in range(SIDE) for x in range(SIDE) for z in range(8) for c in range(2)
    ]


def exchange_perm():
    pairs = []
    for y in range(SIDE):
        for x in range(SIDE):
            for k in range(4):
                for j in range(4):
                    pairs.append((
                        device(y, x, 2 * k + j // 2, j % 2),
                        device(y, j, 2 * k + x // 2, x % 2),
                    ))
    return pairs


def expand(pattern, rows, cols):
    br, bc = pattern.shape
    up = (lax.broadcasted_iota(jnp.int32, (rows, br), 0) // BLK
          == lax.broadcasted_iota(jnp.int32, (rows, br), 1)).astype(F32)
    across = (lax.broadcasted_iota(jnp.int32, (bc, cols), 1) // BLK
              == lax.broadcasted_iota(jnp.int32, (bc, cols), 0)).astype(F32)
    tall = jnp.dot(up, pattern.astype(F32), preferred_element_type=F32)
    return jnp.dot(tall, across, preferred_element_type=F32)


def mask_kernel(matrix_ref, pattern_ref, out_ref):
    keep = expand(pattern_ref[...], *matrix_ref.shape) == 1.0
    out_ref[...] = jnp.where(keep, matrix_ref[...], jnp.zeros_like(matrix_ref))


def mask(matrix, pattern):
    return pl.pallas_call(
        mask_kernel,
        out_shape=jax.ShapeDtypeStruct(matrix.shape, BF16),
        name="mask",
    )(matrix, pattern)


def partial_kernel(where_ref, a0, a1, a2, a3, b0, b1, b2, b3, out_ref):
    total = jnp.dot(a0[...], b0[...], preferred_element_type=F32)
    total += jnp.dot(a1[...], b1[...], preferred_element_type=F32)
    total += jnp.dot(a2[...], b2[...], preferred_element_type=F32)
    total += jnp.dot(a3[...], b3[...], preferred_element_type=F32)
    out_ref[...] = total.astype(out_ref.dtype)


def partial_product(where, held, right, step, dtype):
    size = held.shape[-1]
    cols = right[0].shape[1]
    tile = size // 2

    def held_spec(j):
        return pl.BlockSpec((None, None, tile, size), lambda i, w: (w[j], w[4 + step], i, 0))

    return pl.pallas_call(
        partial_kernel,
        grid_spec=pltpu.PrefetchScalarGridSpec(
            num_scalar_prefetch=1,
            grid=(2,),
            in_specs=[held_spec(j) for j in range(4)]
            + [pl.BlockSpec((size, cols), lambda i, w: (0, 0))] * 4,
            out_specs=pl.BlockSpec((tile, cols), lambda i, w: (i, 0)),
        ),
        out_shape=jax.ShapeDtypeStruct((size, cols), dtype),
        compiler_params=pltpu.CompilerParams(vmem_limit_bytes=24 << 20),
        cost_estimate=pl.CostEstimate(
            flops=2 * size * 4 * size * cols,
            bytes_accessed=2 * (4 * size * size + 4 * size * cols + size * cols),
            transcendentals=0),
        name="partial_product",
    )(where, held, held, held, held, *right)


def add_kernel(middle, chunk, chunks, where_ref, own, p1, p2, p3, pattern_ref, out_ref):
    rows, cols = out_ref.shape
    total = own[...] + p1[...].astype(F32) + p2[...].astype(F32) + p3[...].astype(F32)
    keep = expand(pattern_ref[...], rows, cols * chunks)[:, chunk * cols:(chunk + 1) * cols]
    total = keep * total
    if middle:
        diagonal = (lax.broadcasted_iota(jnp.int32, (rows, cols), 0) + where_ref[8]
                    == lax.broadcasted_iota(jnp.int32, (rows, cols), 1) + chunk * cols)
        total = jnp.where(diagonal, 1.5, 0.0) - 0.5 * total
    out_ref[...] = total.astype(out_ref.dtype)


def add_partials(where, parts, pattern, middle, chunk, chunks):
    rows, cols = parts[0].shape
    vmem = pl.BlockSpec(memory_space=pltpu.VMEM)
    return pl.pallas_call(
        functools.partial(add_kernel, middle, chunk, chunks),
        in_specs=[pl.BlockSpec(memory_space=pltpu.SMEM)] + [vmem] * 5,
        out_specs=vmem,
        out_shape=jax.ShapeDtypeStruct((rows, cols), BF16),
        cost_estimate=pl.CostEstimate(flops=8 * rows * cols, bytes_accessed=12 * rows * cols, transcendentals=0),
        name="add_partials",
    )(where, *parts, pattern)


def local(matrix, pattern):
    size = matrix.shape[0]
    cols = matrix.shape[1] // CHUNKS
    row, col = lax.axis_index("row"), lax.axis_index("col")
    y, x = row // SIDE, row % SIDE
    where = jnp.stack(
        [(y + SIDE - j) % SIDE for j in range(4)]
        + [(x + j) % SIDE for j in range(4)]
        + [(row - col) * size]
    ).astype(jnp.int32)

    def gather_y(block):
        return [block] + [lax.ppermute(block, AXES, shift_perm(j, 0)) for j in (1, 2, 3)]

    def reduce_x(held, right):
        sent = {}
        for step in (2, 1, 3):
            part = partial_product(where, held, right, step, BF16)
            sent[step] = lax.ppermute(part, AXES, shift_perm(0, step))
        own = partial_product(where, held, right, 0, F32)
        return [own, sent[1], sent[2], sent[3]]

    masked = mask(matrix, pattern)
    placed = lax.ppermute(masked, AXES, exchange_perm())
    held = lax.all_gather(placed, "col", axis=0, tiled=False).reshape(4, 4, size, size)
    chunks = [masked[:, k * cols:(k + 1) * cols] for k in range(CHUNKS)]
    rights = [gather_y(block) for block in chunks]
    squares = [reduce_x(held, right) for right in rights]
    middles = [add_partials(where, parts, pattern, True, k, CHUNKS) for k, parts in enumerate(squares)]
    rights = [gather_y(block) for block in middles]
    products = [reduce_x(held, right) for right in rights]
    outs = [add_partials(where, parts, pattern, False, k, CHUNKS) for k, parts in enumerate(products)]
    return jnp.concatenate(outs, axis=1)


def solution(mesh):
    spec = P("row", "col")
    return jax.shard_map(local, mesh=mesh, in_specs=(spec, spec), out_specs=spec, check_vma=False)
```

time: 265 us -> 177 us (0.67)
  waiting for transfers between devices: 225 us -> 74.2 us
  starting transfers between devices: 0.08 us -> 36.1 us
  Pallas kernels: 0 us -> 34.8 us
  matrix products: 22.2 us -> 0 us
  local copies, waits for them, and re-layouts: 2.18 us -> 15.6 us
    all_gather x3 -> x1, waiting for transfers between devices: 224 us -> 50.8 us  [local(): lax.all_gather(placed, 'col', axis=0, tiled=False).reshape(4, 4, size, size)]
    ppermute x0 -> x25, starting transfers between devices: none -> 36.1 us  [the longest x12 17 us: reduce_x(): sent[step] = lax.ppermute(part, AXES, shift_perm(0, step))]
    pallas_call x0 -> x21, Pallas kernels: none -> 34.8 us  [the longest x16 23.1 us: partial_product(): pl.pallas_call(partial_kernel, grid_spec=pltpu.PrefetchScalarGridSpec(num...]
    ppermute x0 -> x25, waiting for transfers between devices: none -> 23.4 us  [the longest x1 11.1 us: local(): placed = lax.ppermute(masked, AXES, exchange_perm())]
    dot_general x2 -> x0, matrix products: 22.2 us -> none  [multiply_passed(): jnp.dot(lax.all_gather(left, 'col', axis=1, tiled=True), gathered, prefer...]
    unnamed x1 -> x36, local copies, waits for them, and re-layouts: 1.26 us -> 14.5 us
  transfers between devices with their start and end apart: 3 -> 26, of which waited for: 3 -> 8; matrix products, arithmetic and copies ran while one was open for 0% -> 1% of each run, Pallas kernels for 0% -> 17%
where the time goes in v1:
time: 177 us; the launch traced here: 176 us
  waiting for transfers between devices  74.2 us (42%)
  starting transfers between devices  36.1 us (20%)
  Pallas kernels  34.8 us (20%)
  local copies, waits for them, and re-layouts  15.6 us (9%)
  between operations  13.8 us (8%)
  other arithmetic  1.86 us (1%)
    all_gather x1, waiting for transfers between devices, local(): lax.all_gather(placed, 'col', axis=0, tiled=False).reshape(4, 4, size, size)  50.8 us
    pallas_call x16, Pallas kernels, partial_product(): pl.pallas_call(partial_kernel, grid_spec=pltpu.PrefetchScalarGridSpec(num...  23.1 us
    ppermute x12, starting transfers between devices, reduce_x(): sent[step] = lax.ppermute(part, AXES, shift_perm(0, step))  17 us
    ppermute x12, starting transfers between devices, gather_y(): lax.ppermute(block, AXES, shift_perm(j, 0))  14.6 us
    unnamed x36, local copies, waits for them, and re-layouts  14.5 us
    ppermute x1, waiting for transfers between devices, local(): placed = lax.ppermute(masked, AXES, exchange_perm())  11.1 us
    pallas_call x4, Pallas kernels, add_partials(): pl.pallas_call(functools.partial(add_kernel, middle, chunk, chunks), in_s...  9.44 us
    ppermute x12, waiting for transfers between devices, reduce_x(): sent[step] = lax.ppermute(part, AXES, shift_perm(0, step))  8.1 us
  transfers between devices with their start and end apart: 26, of which 8 were waited for; matrix products, arithmetic and copies ran while one was open for 1% of the time, Pallas kernels for 17%

profile of v1, /device:TPU:1, one launch (start us, length us, event | category | flops | bytes accessed | tf_op | source)
XLA Modules:
  0.0 176.3 jit_solution(6223573578109901683)
XLA Ops:
  6.5 2.2 %mask.1 = bf16[512,512]{1,0:T(8,128)(2,1)} custom-call(bf16[512,512]{1,0:T(8,128)(2,1)} %matrix_ref.1, s32[8,8]{1,0:T(8,128)} %pattern_ref.9), custom_call_target="tpu_custom_call" | custom-call | tf_op jit(solution)/shard_map/mask/pallas_call | solution.py:58
  8.8 4.5 %collective-permute-start = (bf16[512,512]{1,0:T(8,128)(2,1)}, bf16[512,512]{1,0:T(8,128)(2,1)S(1)}, u32[]{:S(2)}, u32[]{:S(2)}) collective-permute-start(bf16[512,512]{1,0:T(8,128)(2,1)} %mask.1), channel_id=1, source_target_pairs={{0,0},{1,16},{2,32},{3,48},{4,4},{5,20},{6,36},{7,52},{8,8},{9,24}... | collective-permute-start | bytes 1572872 | tf_op jit(solution)/shard_map/ppermute | solution.py:148
  13.3 11.1 %collective-permute-done = bf16[512,512]{1,0:T(8,128)(2,1)S(1)} collective-permute-done((bf16[512,512]{1,0:T(8,128)(2,1)}, bf16[512,512]{1,0:T(8,128)(2,1)S(1)}, u32[]{:S(2)}, u32[]{:S(2)}) %collective-permute-start) | collective-permute-done | bytes 524320 | tf_op jit(solution)/shard_map/ppermute | solution.py:148
  24.4 0.8 copy-done.12
  25.2 1.1 fusion
  26.3 1.4 collective-permute-start.1
  27.7 2.6 %collective-permute-start.2 = (bf16[512,256]{1,0:T(8,128)(2,1)S(1)}, bf16[512,256]{1,0:T(8,128)(2,1)S(1)}, u32[]{:S(2)}, u32[]{:S(2)}) collective-permute-start(bf16[512,256]{1,0:T(8,128)(2,1)S(1)} %get-tuple-element.5.b0), channel_id=1, source_target_pairs={{0,128},{1,129},{2,130},{3,131},{4,132},{5,133},{6,134},{7,135},{8... | collective-permute-start | bytes 786440 | tf_op jit(solution)/shard_map/ppermute | solution.py:137
  30.3 1.1 collective-permute-start.3
  31.3 0.4 collective-permute-start.13
  31.7 0.8 collective-permute-start.14
  32.5 1.3 collective-permute-done.1.b1
  33.8 0.8 collective-permute-start.15
  34.6 0.1 stack.39.where_ref
  34.7 2.2 %collective-permute-done.2.b2 = bf16[512,256]{1,0:T(8,128)(2,1)S(1)} collective-permute-done((bf16[512,256]{1,0:T(8,128)(2,1)S(1)}, bf16[512,256]{1,0:T(8,128)(2,1)S(1)}, u32[]{:S(2)}, u32[]{:S(2)}) %collective-permute-start.2) | collective-permute-done | bytes 262176 | tf_op jit(solution)/shard_map/ppermute | solution.py:137
  36.9 0.7 collective-permute-done.3.b3
  37.6 50.8 %all-gather.3.cloned.1.call-done = bf16[8192,512]{1,0:T(8,128)(2,1)} async-done(((bf16[512,512]{1,0:T(8,128)(2,1)}), bf16[8192,512]{1,0:T(8,128)(2,1)}) %all-gather.3.cloned.1.call-update) | async-done | bytes 8388624 | tf_op jit(solution)/shard_map/all_gather | solution.py:149
  88.4 3.4 %copy-done = bf16[8192,512]{1,0:T(8,128)(2,1)S(1)} copy-done((bf16[8192,512]{1,0:T(8,128)(2,1)S(1)}, bf16[8192,512]{1,0:T(8,128)(2,1)}, u32[]{:S(2)}) %copy-start) | copy-done | bytes 8388632
  91.7 1.4 partial_product.17
  93.2 1.3 collective-permute-start.4
  94.5 1.4 partial_product.18
  95.9 2.5 %collective-permute-start.5 = (bf16[512,256]{1,0:T(8,128)(2,1)S(1)}, bf16[512,256]{1,0:T(8,128)(2,1)S(1)}, u32[]{:S(2)}, u32[]{:S(2)}) collective-permute-start(bf16[512,256]{1,0:T(8,128)(2,1)S(1)} %partial_product.18), channel_id=1, source_target_pairs={{0,32},{1,33},{2,34},{3,35},{4,36},{5,37},{6,38},{7,39},{8,40},{9,... | collective-permute-start | bytes 786440 | tf_op jit(solution)/shard_map/ppermute | solution.py:143
  98.4 1.4 partial_product.19
  99.9 1.3 collective-permute-start.6
  101.1 1.4 partial_product.27
  102.6 0.1 collective-permute-start.18
  102.7 1.4 partial_product.26
  104.1 2.1 %collective-permute-start.17 = (bf16[512,256]{1,0:T(8,128)(2,1)S(1)}, bf16[512,256]{1,0:T(8,128)(2,1)}, u32[]{:S(2)}, u32[]{:S(2)}) collective-permute-start(bf16[512,256]{1,0:T(8,128)(2,1)S(1)} %partial_product.26), channel_id=1, source_target_pairs={{0,32},{1,33},{2,34},{3,35},{4,36},{5,37},{6,38},{7,39},{8,40},{9,... | collective-permute-start | bytes 786440 | tf_op jit(solution)/shard_map/ppermute | solution.py:143
  106.3 1.4 partial_product.16.own
  107.7 1.4 partial_product.25
  109.3 0.6 copy-done.16
  109.9 0.7 copy-done.17
  110.7 2.4 %add_partials.4.b0 = bf16[512,256]{1,0:T(8,128)(2,1)} custom-call(s32[9]{0:T(128)} %copy-done.9, f32[512,256]{1,0:T(8,128)} %copy-done.6, bf16[512,256]{1,0:T(8,128)(2,1)} %copy-done.16, bf16[512,256]{1,0:T(8,128)(2,1)} %copy-done.17, bf16[512,256]{1,0:T(8,128)(2,1)} %collective-permute-done.6.p3, s32[8,8]{1,0:T(8,128)} %pattern_ref.9), custom_call_target="tpu_custom_call" | custom-call | flops 1048576 | bytes 1572864 | tf_op jit(solution)/shard_map/add_partials/pallas_call | solution.py:115
  113.0 1.2 collective-permute-start.7
  114.2 2.4 %collective-permute-start.8 = (bf16[512,256]{1,0:T(8,128)(2,1)}, bf16[512,256]{1,0:T(8,128)(2,1)S(1)}, u32[]{:S(2)}, u32[]{:S(2)}) collective-permute-start(bf16[512,256]{1,0:T(8,128)(2,1)} %add_partials.4.b0), channel_id=1, source_target_pairs={{0,128},{1,129},{2,130},{3,131},{4,132},{5,133},{6,134},{7,135},{8... | collective-permute-start | bytes 786440 | tf_op jit(solution)/shard_map/ppermute | solution.py:137
  116.7 1.2 collective-permute-start.9
  117.9 3.4 %copy-done.1 = bf16[8192,512]{1,0:T(8,128)(2,1)S(1)} copy-done((bf16[8192,512]{1,0:T(8,128)(2,1)S(1)}, bf16[8192,512]{1,0:T(8,128)(2,1)}, u32[]{:S(2)}) %copy-start.1) | copy-done | bytes 8388632
  121.3 0.6 copy-done.10
  121.9 1.4 partial_product.24.own
  123.4 0.8 copy-done.8
  124.2 2.4 %add_partials.6.b0 = bf16[512,256]{1,0:T(8,128)(2,1)} custom-call(s32[9]{0:T(128)} %copy-done.9, f32[512,256]{1,0:T(8,128)} %copy-done.8, bf16[512,256]{1,0:T(8,128)(2,1)} %collective-permute-done.16.p1, bf16[512,256]{1,0:T(8,128)(2,1)} %collective-permute-done.17.p2, bf16[512,256]{1,0:T(8,128)(2,1)} %copy-done.13, s32[8,8]{1,0:T(8,128)} %pattern_ref.9), custom_call_target="tpu_custom_call" | custom-call | flops 1048576 | bytes 1572864 | tf_op jit(solution)/shard_map/add_partials/pallas_call | solution.py:115
  126.5 0.2 collective-permute-start.19
  126.8 1.5 collective-permute-start.20
  128.3 0.9 collective-permute-start.21
  129.2 3.4 %copy-done.2 = bf16[8192,512]{1,0:T(8,128)(2,1)S(1)} copy-done((bf16[8192,512]{1,0:T(8,128)(2,1)S(1)}, bf16[8192,512]{1,0:T(8,128)(2,1)}, u32[]{:S(2)}) %copy-start.2) | copy-done | bytes 8388632
  132.6 1.4 partial_product.23
  134.1 4.0 %collective-permute-start.12 = (bf16[512,256]{1,0:T(8,128)(2,1)S(1)}, bf16[512,256]{1,0:T(8,128)(2,1)S(1)}, u32[]{:S(2)}, u32[]{:S(2)}) collective-permute-start(bf16[512,256]{1,0:T(8,128)(2,1)S(1)} %partial_product.23), channel_id=1, source_target_pairs={{0,48},{1,49},{2,50},{3,51},{4,52},{5,53},{6,54},{7,55},{8,56},{9,... | collective-permute-start | bytes 786440 | tf_op jit(solution)/shard_map/ppermute | solution.py:143
  138.1 1.4 partial_product.22
  139.5 1.6 collective-permute-start.11
  141.1 1.4 partial_product.21
  142.6 0.1 collective-permute-start.10
  142.7 1.4 partial_product.31
  144.2 2.7 %collective-permute-start.24 = (bf16[512,256]{1,0:T(8,128)(2,1)S(1)}, bf16[512,256]{1,0:T(8,128)(2,1)}, u32[]{:S(2)}, u32[]{:S(2)}) collective-permute-start(bf16[512,256]{1,0:T(8,128)(2,1)S(1)} %partial_product.31), channel_id=1, source_target_pairs={{0,48},{1,49},{2,50},{3,51},{4,52},{5,53},{6,54},{7,55},{8,56},{9,... | collective-permute-start | bytes 786440 | tf_op jit(solution)/shard_map/ppermute | solution.py:143
  146.9 1.4 partial_product.30
  148.4 1.2 collective-permute-start.23
  149.5 1.4 partial_product.29
  151.1 1.4 partial_product.20.own
  152.6 1.4 partial_product.28.own
  154.1 0.7 copy-done.15
  154.8 0.4 collective-permute-done.10.p1
  155.2 2.4 %add_partials.5 = bf16[512,256]{1,0:T(8,128)(2,1)} custom-call(s32[9]{0:T(128)} %copy-done.9, f32[512,256]{1,0:T(8,128)} %copy-done.7, bf16[512,256]{1,0:T(8,128)(2,1)} %collective-permute-done.10.p1, bf16[512,256]{1,0:T(8,128)(2,1)} %copy-done.15, bf16[512,256]{1,0:T(8,128)(2,1)} %copy-done.14, s32[8,8]{1,0:T(8,128)} %pattern_ref.9), custom_call_target="tpu_custom_call" | custom-call | flops 1048576 | bytes 1572864 | tf_op jit(solution)/shard_map/add_partials/pallas_call | solution.py:115
  157.5 0.9 collective-permute-done.23.p2
  158.4 6.8 %collective-permute-done.22.p1 = bf16[512,256]{1,0:T(8,128)(2,1)} collective-permute-done((bf16[512,256]{1,0:T(8,128)(2,1)S(1)}, bf16[512,256]{1,0:T(8,128)(2,1)}, u32[]{:S(2)}, u32[]{:S(2)}) %collective-permute-start.22) | collective-permute-done | bytes 262176 | tf_op jit(solution)/shard_map/ppermute | solution.py:143
  165.2 2.4 %add_partials.7 = bf16[512,256]{1,0:T(8,128)(2,1)} custom-call(s32[9]{0:T(128)} %copy-done.9, f32[512,256]{1,0:T(8,128)} %copy-done.5, bf16[512,256]{1,0:T(8,128)(2,1)} %collective-permute-done.22.p1, bf16[512,256]{1,0:T(8,128)(2,1)} %collective-permute-done.23.p2, bf16[512,256]{1,0:T(8,128)(2,1)} %collective-permute-done.24.p3, s32[8,8]{1,0:T(8,128)} %pattern_ref.9), custom_call_target="tpu_custom_call" | custom-call | flops 1048576 | bytes 1572864 | tf_op jit(solution)/shard_map/add_partials/pallas_call | solution.py:115
  167.6 1.9 %pad_maximum_fusion = bf16[512,512]{1,0:T(8,128)(2,1)} fusion(bf16[512,256]{1,0:T(8,128)(2,1)} %add_partials.7, bf16[512,256]{1,0:T(8,128)(2,1)} %add_partials.5), kind=kLoop, calls=%fused_computation | loop fusion | flops 1048576 | bytes 1048576 | tf_op jit(solution)/shard_map/concatenate | solution.py:157
  (49 shorter events, 0.3 us)
Async XLA Ops:
  6.5 81.8 %all-gather.3.cloned.1.call-start = ((), (), s32[]{:S(2)}) async-start(), calls=%async_computation | async-start | bytes 8912896 | tf_op jit(solution)/shard_map/all_gather | solution.py:149
  8.8 15.6 %collective-permute-start = (bf16[512,512]{1,0:T(8,128)(2,1)}, bf16[512,512]{1,0:T(8,128)(2,1)S(1)}, u32[]{:S(2)}, u32[]{:S(2)}) collective-permute-start(bf16[512,512]{1,0:T(8,128)(2,1)} %mask.1), channel_id=1, source_target_pairs={{0,0},{1,16},{2,32},{3,48},{4,4},{5,20},{6,36},{7,52},{8,8},{9,24}... | collective-permute-start | bytes 1572872 | tf_op jit(solution)/shard_map/ppermute | solution.py:148
  24.4 0.8 copy-start.12
  26.3 7.5 %collective-permute-start.1 = (bf16[512,256]{1,0:T(8,128)(2,1)S(1)}, bf16[512,256]{1,0:T(8,128)(2,1)S(1)}, u32[]{:S(2)}, u32[]{:S(2)}) collective-permute-start(bf16[512,256]{1,0:T(8,128)(2,1)S(1)} %get-tuple-element.5.b0), channel_id=1, source_target_pairs={{0,64},{1,65},{2,66},{3,67},{4,68},{5,69},{6,70},{7,71},{8,72},{9,... | collective-permute-start | bytes 786440 | tf_op jit(solution)/shard_map/ppermute | solution.py:137
  27.7 9.3 %collective-permute-start.2 = (bf16[512,256]{1,0:T(8,128)(2,1)S(1)}, bf16[512,256]{1,0:T(8,128)(2,1)S(1)}, u32[]{:S(2)}, u32[]{:S(2)}) collective-permute-start(bf16[512,256]{1,0:T(8,128)(2,1)S(1)} %get-tuple-element.5.b0), channel_id=1, source_target_pairs={{0,128},{1,129},{2,130},{3,131},{4,132},{5,133},{6,134},{7,135},{8... | collective-permute-start | bytes 786440 | tf_op jit(solution)/shard_map/ppermute | solution.py:137
  30.3 7.3 %collective-permute-start.3 = (bf16[512,256]{1,0:T(8,128)(2,1)S(1)}, bf16[512,256]{1,0:T(8,128)(2,1)S(1)}, u32[]{:S(2)}, u32[]{:S(2)}) collective-permute-start(bf16[512,256]{1,0:T(8,128)(2,1)S(1)} %get-tuple-element.5.b0), channel_id=1, source_target_pairs={{0,192},{1,193},{2,194},{3,195},{4,196},{5,197},{6,198},{7,199},{8... | collective-permute-start | bytes 786440 | tf_op jit(solution)/shard_map/ppermute | solution.py:137
  31.3 68.5 %collective-permute-start.13 = (bf16[512,256]{1,0:T(8,128)(2,1)S(1)}, bf16[512,256]{1,0:T(8,128)(2,1)S(1)}, u32[]{:S(2)}, u32[]{:S(2)}) collective-permute-start(bf16[512,256]{1,0:T(8,128)(2,1)S(1)} %get-tuple-element.6.b0), channel_id=1, source_target_pairs={{0,64},{1,65},{2,66},{3,67},{4,68},{5,69},{6,70},{7,71},{8,72},{9,... | collective-permute-start | bytes 786440 | tf_op jit(solution)/shard_map/ppermute | solution.py:137
  31.7 69.4 %collective-permute-start.14 = (bf16[512,256]{1,0:T(8,128)(2,1)S(1)}, bf16[512,256]{1,0:T(8,128)(2,1)S(1)}, u32[]{:S(2)}, u32[]{:S(2)}) collective-permute-start(bf16[512,256]{1,0:T(8,128)(2,1)S(1)} %get-tuple-element.6.b0), channel_id=1, source_target_pairs={{0,128},{1,129},{2,130},{3,131},{4,132},{5,133},{6,134},{7,135},{8... | collective-permute-start | bytes 786440 | tf_op jit(solution)/shard_map/ppermute | solution.py:137
  33.8 67.3 %collective-permute-start.15 = (bf16[512,256]{1,0:T(8,128)(2,1)S(1)}, bf16[512,256]{1,0:T(8,128)(2,1)S(1)}, u32[]{:S(2)}, u32[]{:S(2)}) collective-permute-start(bf16[512,256]{1,0:T(8,128)(2,1)S(1)} %get-tuple-element.6.b0), channel_id=1, source_target_pairs={{0,192},{1,193},{2,194},{3,195},{4,196},{5,197},{6,198},{7,199},{8... | collective-permute-start | bytes 786440 | tf_op jit(solution)/shard_map/ppermute | solution.py:137
  34.7 73.0 %copy-start.9 = (s32[9]{0:T(128)}, s32[9]{0:T(128)S(1)}, u32[]{:S(2)}) copy-start(s32[9]{0:T(128)S(1)} %stack.39.where_ref) | copy-start | bytes 112
  88.4 3.4 %copy-start = (bf16[8192,512]{1,0:T(8,128)(2,1)S(1)}, bf16[8192,512]{1,0:T(8,128)(2,1)}, u32[]{:S(2)}) copy-start(bf16[8192,512]{1,0:T(8,128)(2,1)} %all-gather.3.cloned.1.call-done) | copy-start | bytes 25165828
  93.2 16.0 %collective-permute-start.4 = (bf16[512,256]{1,0:T(8,128)(2,1)S(1)}, bf16[512,256]{1,0:T(8,128)(2,1)S(1)}, u32[]{:S(2)}, u32[]{:S(2)}) collective-permute-start(bf16[512,256]{1,0:T(8,128)(2,1)S(1)} %partial_product.17), channel_id=1, source_target_pairs={{0,16},{1,17},{2,18},{3,19},{4,20},{5,21},{6,22},{7,23},{8,24},{9,... | collective-permute-start | bytes 786440 | tf_op jit(solution)/shard_map/ppermute | solution.py:143
  95.9 13.4 %collective-permute-start.5 = (bf16[512,256]{1,0:T(8,128)(2,1)S(1)}, bf16[512,256]{1,0:T(8,128)(2,1)S(1)}, u32[]{:S(2)}, u32[]{:S(2)}) collective-permute-start(bf16[512,256]{1,0:T(8,128)(2,1)S(1)} %partial_product.18), channel_id=1, source_target_pairs={{0,32},{1,33},{2,34},{3,35},{4,36},{5,37},{6,38},{7,39},{8,40},{9,... | collective-permute-start | bytes 786440 | tf_op jit(solution)/shard_map/ppermute | solution.py:143
  99.9 10.8 %collective-permute-start.6 = (bf16[512,256]{1,0:T(8,128)(2,1)S(1)}, bf16[512,256]{1,0:T(8,128)(2,1)}, u32[]{:S(2)}, u32[]{:S(2)}) collective-permute-start(bf16[512,256]{1,0:T(8,128)(2,1)S(1)} %partial_product.19), channel_id=1, source_target_pairs={{0,48},{1,49},{2,50},{3,51},{4,52},{5,53},{6,54},{7,55},{8,56},{9,... | collective-permute-start | bytes 786440 | tf_op jit(solution)/shard_map/ppermute | solution.py:143
  102.6 14.1 %collective-permute-start.18 = (bf16[512,256]{1,0:T(8,128)(2,1)S(1)}, bf16[512,256]{1,0:T(8,128)(2,1)S(1)}, u32[]{:S(2)}, u32[]{:S(2)}) collective-permute-start(bf16[512,256]{1,0:T(8,128)(2,1)S(1)} %partial_product.27), channel_id=1, source_target_pairs={{0,48},{1,49},{2,50},{3,51},{4,52},{5,53},{6,54},{7,55},{8,56},{9,... | collective-permute-start | bytes 786440 | tf_op jit(solution)/shard_map/ppermute | solution.py:143
  104.1 20.0 %collective-permute-start.17 = (bf16[512,256]{1,0:T(8,128)(2,1)S(1)}, bf16[512,256]{1,0:T(8,128)(2,1)}, u32[]{:S(2)}, u32[]{:S(2)}) collective-permute-start(bf16[512,256]{1,0:T(8,128)(2,1)S(1)} %partial_product.26), channel_id=1, source_target_pairs={{0,32},{1,33},{2,34},{3,35},{4,36},{5,37},{6,38},{7,39},{8,40},{9,... | collective-permute-start | bytes 786440 | tf_op jit(solution)/shard_map/ppermute | solution.py:143
  107.7 1.5 copy-start.6
  109.2 0.7 copy-start.16
  109.2 14.9 %collective-permute-start.16 = (bf16[512,256]{1,0:T(8,128)(2,1)S(1)}, bf16[512,256]{1,0:T(8,128)(2,1)}, u32[]{:S(2)}, u32[]{:S(2)}) collective-permute-start(bf16[512,256]{1,0:T(8,128)(2,1)S(1)} %partial_product.25), channel_id=1, source_target_pairs={{0,16},{1,17},{2,18},{3,19},{4,20},{5,21},{6,22},{7,23},{8,24},{9,... | collective-permute-start | bytes 786440 | tf_op jit(solution)/shard_map/ppermute | solution.py:143
  109.9 0.7 copy-start.17
  110.6 18.6 %copy-start.11 = (s32[9]{0:T(128)S(1)}, s32[9]{0:T(128)}, u32[]{:S(2)}) copy-start(s32[9]{0:T(128)} %copy-done.9) | copy-start | bytes 112
  113.0 15.3 %collective-permute-start.7 = (bf16[512,256]{1,0:T(8,128)(2,1)}, bf16[512,256]{1,0:T(8,128)(2,1)S(1)}, u32[]{:S(2)}, u32[]{:S(2)}) collective-permute-start(bf16[512,256]{1,0:T(8,128)(2,1)} %add_partials.4.b0), channel_id=1, source_target_pairs={{0,64},{1,65},{2,66},{3,67},{4,68},{5,69},{6,70},{7,71},{8,72},{9,... | collective-permute-start | bytes 786440 | tf_op jit(solution)/shard_map/ppermute | solution.py:137
  114.2 15.0 %collective-permute-start.8 = (bf16[512,256]{1,0:T(8,128)(2,1)}, bf16[512,256]{1,0:T(8,128)(2,1)S(1)}, u32[]{:S(2)}, u32[]{:S(2)}) collective-permute-start(bf16[512,256]{1,0:T(8,128)(2,1)} %add_partials.4.b0), channel_id=1, source_target_pairs={{0,128},{1,129},{2,130},{3,131},{4,132},{5,133},{6,134},{7,135},{8... | collective-permute-start | bytes 786440 | tf_op jit(solution)/shard_map/ppermute | solution.py:137
  116.7 6.7 %copy-start.13 = (bf16[512,256]{1,0:T(8,128)(2,1)}, bf16[512,256]{1,0:T(8,128)(2,1)S(1)}, u32[]{:S(2)}) copy-start(bf16[512,256]{1,0:T(8,128)(2,1)S(1)} %collective-permute-done.18.p3) | copy-start | bytes 786436
  116.7 12.6 %collective-permute-start.9 = (bf16[512,256]{1,0:T(8,128)(2,1)}, bf16[512,256]{1,0:T(8,128)(2,1)S(1)}, u32[]{:S(2)}, u32[]{:S(2)}) collective-permute-start(bf16[512,256]{1,0:T(8,128)(2,1)} %add_partials.4.b0), channel_id=1, source_target_pairs={{0,192},{1,193},{2,194},{3,195},{4,196},{5,197},{6,198},{7,199},{8... | collective-permute-start | bytes 786440 | tf_op jit(solution)/shard_map/ppermute | solution.py:137
  117.9 3.4 %copy-start.1 = (bf16[8192,512]{1,0:T(8,128)(2,1)S(1)}, bf16[8192,512]{1,0:T(8,128)(2,1)}, u32[]{:S(2)}) copy-start(bf16[8192,512]{1,0:T(8,128)(2,1)} %all-gather.3.cloned.1.call-done) | copy-start | bytes 25165828
  121.3 0.6 copy-start.10
  121.9 7.3 %copy-start.3 = (bf16[512,256]{1,0:T(8,128)(2,1)S(1)}, bf16[512,256]{1,0:T(8,128)(2,1)}, u32[]{:S(2)}) copy-start(bf16[512,256]{1,0:T(8,128)(2,1)} %add_partials.4.b0) | copy-start | bytes 786436
  123.4 0.8 copy-start.8
  126.5 16.1 %collective-permute-start.19 = (bf16[512,256]{1,0:T(8,128)(2,1)}, bf16[512,256]{1,0:T(8,128)(2,1)S(1)}, u32[]{:S(2)}, u32[]{:S(2)}) collective-permute-start(bf16[512,256]{1,0:T(8,128)(2,1)} %add_partials.6.b0), channel_id=1, source_target_pairs={{0,64},{1,65},{2,66},{3,67},{4,68},{5,69},{6,70},{7,71},{8,72},{9,... | collective-permute-start | bytes 786440 | tf_op jit(solution)/shard_map/ppermute | solution.py:137
  126.8 15.9 %collective-permute-start.20 = (bf16[512,256]{1,0:T(8,128)(2,1)}, bf16[512,256]{1,0:T(8,128)(2,1)S(1)}, u32[]{:S(2)}, u32[]{:S(2)}) collective-permute-start(bf16[512,256]{1,0:T(8,128)(2,1)} %add_partials.6.b0), channel_id=1, source_target_pairs={{0,128},{1,129},{2,130},{3,131},{4,132},{5,133},{6,134},{7,135},{8... | collective-permute-start | bytes 786440 | tf_op jit(solution)/shard_map/ppermute | solution.py:137
  128.3 14.4 %collective-permute-start.21 = (bf16[512,256]{1,0:T(8,128)(2,1)}, bf16[512,256]{1,0:T(8,128)(2,1)S(1)}, u32[]{:S(2)}, u32[]{:S(2)}) collective-permute-start(bf16[512,256]{1,0:T(8,128)(2,1)} %add_partials.6.b0), channel_id=1, source_target_pairs={{0,192},{1,193},{2,194},{3,195},{4,196},{5,197},{6,198},{7,199},{8... | collective-permute-start | bytes 786440 | tf_op jit(solution)/shard_map/ppermute | solution.py:137
  129.2 3.4 %copy-start.2 = (bf16[8192,512]{1,0:T(8,128)(2,1)S(1)}, bf16[8192,512]{1,0:T(8,128)(2,1)}, u32[]{:S(2)}) copy-start(bf16[8192,512]{1,0:T(8,128)(2,1)} %all-gather.3.cloned.1.call-done) | copy-start | bytes 25165828
  134.1 16.9 %collective-permute-start.12 = (bf16[512,256]{1,0:T(8,128)(2,1)S(1)}, bf16[512,256]{1,0:T(8,128)(2,1)S(1)}, u32[]{:S(2)}, u32[]{:S(2)}) collective-permute-start(bf16[512,256]{1,0:T(8,128)(2,1)S(1)} %partial_product.23), channel_id=1, source_target_pairs={{0,48},{1,49},{2,50},{3,51},{4,52},{5,53},{6,54},{7,55},{8,56},{9,... | collective-permute-start | bytes 786440 | tf_op jit(solution)/shard_map/ppermute | solution.py:143
  139.5 3.2 %copy-start.4 = (bf16[512,256]{1,0:T(8,128)(2,1)S(1)}, bf16[512,256]{1,0:T(8,128)(2,1)}, u32[]{:S(2)}) copy-start(bf16[512,256]{1,0:T(8,128)(2,1)} %add_partials.6.b0) | copy-start | bytes 786436
  139.5 14.5 %collective-permute-start.11 = (bf16[512,256]{1,0:T(8,128)(2,1)S(1)}, bf16[512,256]{1,0:T(8,128)(2,1)S(1)}, u32[]{:S(2)}, u32[]{:S(2)}) collective-permute-start(bf16[512,256]{1,0:T(8,128)(2,1)S(1)} %partial_product.22), channel_id=1, source_target_pairs={{0,32},{1,33},{2,34},{3,35},{4,36},{5,37},{6,38},{7,39},{8,40},{9,... | collective-permute-start | bytes 786440 | tf_op jit(solution)/shard_map/ppermute | solution.py:143
  142.6 12.6 %collective-permute-start.10 = (bf16[512,256]{1,0:T(8,128)(2,1)S(1)}, bf16[512,256]{1,0:T(8,128)(2,1)}, u32[]{:S(2)}, u32[]{:S(2)}) collective-permute-start(bf16[512,256]{1,0:T(8,128)(2,1)S(1)} %partial_product.21), channel_id=1, source_target_pairs={{0,16},{1,17},{2,18},{3,19},{4,20},{5,21},{6,22},{7,23},{8,24},{9,... | collective-permute-start | bytes 786440 | tf_op jit(solution)/shard_map/ppermute | solution.py:143
  144.2 13.4 %collective-permute-start.24 = (bf16[512,256]{1,0:T(8,128)(2,1)S(1)}, bf16[512,256]{1,0:T(8,128)(2,1)}, u32[]{:S(2)}, u32[]{:S(2)}) collective-permute-start(bf16[512,256]{1,0:T(8,128)(2,1)S(1)} %partial_product.31), channel_id=1, source_target_pairs={{0,48},{1,49},{2,50},{3,51},{4,52},{5,53},{6,54},{7,55},{8,56},{9,... | collective-permute-start | bytes 786440 | tf_op jit(solution)/shard_map/ppermute | solution.py:143
  148.4 10.1 %collective-permute-start.23 = (bf16[512,256]{1,0:T(8,128)(2,1)S(1)}, bf16[512,256]{1,0:T(8,128)(2,1)}, u32[]{:S(2)}, u32[]{:S(2)}) collective-permute-start(bf16[512,256]{1,0:T(8,128)(2,1)S(1)} %partial_product.30), channel_id=1, source_target_pairs={{0,32},{1,33},{2,34},{3,35},{4,36},{5,37},{6,38},{7,39},{8,40},{9,... | collective-permute-start | bytes 786440 | tf_op jit(solution)/shard_map/ppermute | solution.py:143
  151.0 1.6 copy-start.14
  151.0 14.3 %collective-permute-start.22 = (bf16[512,256]{1,0:T(8,128)(2,1)S(1)}, bf16[512,256]{1,0:T(8,128)(2,1)}, u32[]{:S(2)}, u32[]{:S(2)}) collective-permute-start(bf16[512,256]{1,0:T(8,128)(2,1)S(1)} %partial_product.29), channel_id=1, source_target_pairs={{0,16},{1,17},{2,18},{3,19},{4,20},{5,21},{6,22},{7,23},{8,24},{9,... | collective-permute-start | bytes 786440 | tf_op jit(solution)/shard_map/ppermute | solution.py:143
  152.5 1.5 copy-start.7
  154.0 11.2 %copy-start.5 = (f32[512,256]{1,0:T(8,128)}, f32[512,256]{1,0:T(8,128)S(1)}, u32[]{:S(2)}) copy-start(f32[512,256]{1,0:T(8,128)S(1)} %partial_product.28.own) | copy-start | bytes 1572868
  154.0 0.8 copy-start.15
Sparse Core Ops, SparseCore 0:
  25.3 62.9 all-gather.2

commit v2 on v0

v2 whole, which is shorter than its diff:
```python
import functools

import jax
import jax.numpy as jnp
from jax import lax
from jax.experimental import pallas as pl
from jax.experimental.pallas import tpu as pltpu
from jax.sharding import PartitionSpec as P

BLK = 64
SIDE = 4
DEEP = 8
TILES = 16
AXES = ("row", "col")
F32 = jnp.float32
BF16 = jnp.bfloat16
VMEM = pl.BlockSpec(memory_space=pltpu.VMEM)
SMEM = pl.BlockSpec(memory_space=pltpu.SMEM)
SMALL = pltpu.CompilerParams(vmem_limit_bytes=4 << 20)
LARGE = pltpu.CompilerParams(vmem_limit_bytes=16 << 20)


def device(y, x, z, c):
    return ((y % SIDE) * SIDE + x % SIDE) * 2 * DEEP + (z % DEEP) * 2 + c


PLACES = [(y, x, z, c) for y in range(SIDE) for x in range(SIDE) for z in range(DEEP) for c in range(2)]
SWAP = [(device(y, x, z, c), device(y, x, z, 1 - c)) for y, x, z, c in PLACES]
RING = [(device(y, x, z, c), device(y, x, z + 1 - 2 * c, c)) for y, x, z, c in PLACES]


def first_axis(step):
    return [(device(y, x, z, c), device(y + step * c, x + step * (1 - c), z, c)) for y, x, z, c in PLACES]


def second_axis(step):
    return [(device(y, x, z, c), device(y + step * (1 - c), x + step * c, z, c)) for y, x, z, c in PLACES]


def send(block, pairs):
    return lax.ppermute(block, AXES, pairs)


def mask_kernel(matrix_ref, pattern_ref, out_ref, keep_ref):
    rows, cols = matrix_ref.shape
    br, bc = pattern_ref.shape
    up = (lax.broadcasted_iota(jnp.int32, (rows, br), 0) // BLK
          == lax.broadcasted_iota(jnp.int32, (rows, br), 1)).astype(F32).astype(BF16)
    across = (lax.broadcasted_iota(jnp.int32, (bc, cols), 1) // BLK
              == lax.broadcasted_iota(jnp.int32, (bc, cols), 0)).astype(F32).astype(BF16)
    pattern = pattern_ref[...].astype(F32).astype(BF16)
    tall = jnp.dot(up, pattern, preferred_element_type=F32).astype(BF16)
    keep = jnp.dot(tall, across, preferred_element_type=F32)
    keep_ref[...] = keep.astype(BF16)
    out_ref[...] = jnp.where(keep == 1.0, matrix_ref[...].astype(F32), 0.0).astype(BF16)


def mask(matrix, pattern):
    shape = jax.ShapeDtypeStruct(matrix.shape, BF16)
    return pl.pallas_call(
        mask_kernel, in_specs=[VMEM, VMEM], out_specs=[VMEM, VMEM], out_shape=[shape, shape],
        compiler_params=SMALL, name="mask",
    )(matrix, pattern)


def join_kernel(*refs):
    out_ref, first = refs[-1], 0
    for ref in refs[:-1]:
        out_ref[first:first + ref.shape[0], :] = ref[...]
        first += ref.shape[0]


def join(*parts):
    rows, cols = sum(part.shape[0] for part in parts), parts[0].shape[1]
    return pl.pallas_call(
        join_kernel, in_specs=[VMEM] * len(parts), out_specs=VMEM,
        out_shape=jax.ShapeDtypeStruct((rows, cols), BF16),
        compiler_params=SMALL, name="join",
    )(*parts)


def arrange_kernel(where_ref, *refs):
    tiles, out_ref = refs[:-1], refs[-1]
    cols = tiles[0].shape[1]
    for t, tile in enumerate(tiles):
        at = pl.multiple_of(where_ref[TILES + t] * cols, cols)
        out_ref[where_ref[t], :, pl.ds(at, cols)] = tile[...]


def arrange(where, tiles):
    rows, cols = tiles[0].shape
    return pl.pallas_call(
        arrange_kernel, in_specs=[SMEM] + [VMEM] * TILES, out_specs=VMEM,
        out_shape=jax.ShapeDtypeStruct((TILES // 2, rows, 2 * cols), BF16),
        compiler_params=SMALL, name="arrange",
    )(where, *tiles)


def cost(pairs, panel, right):
    rows, deep, cols = panel.shape[1], right.shape[0], right.shape[1]
    return pl.CostEstimate(
        flops=2 * pairs * rows * deep * cols, bytes_accessed=2 * pairs * deep * (rows + cols), transcendentals=0)


def total_of(panel_ref, rights, places):
    total = None
    for ref, (pair, first) in zip(rights, places):
        width = panel_ref.shape[2]
        for top in range(0, ref.shape[0], width):
            rows = min(width, ref.shape[0] - top)
            left = panel_ref[pair + top // width, :, first:first + rows]
            term = jnp.dot(left, ref[top:top + rows, :], preferred_element_type=F32)
            total = term if total is None else total + term
    return total


def begin_kernel(places, panel_ref, *refs):
    refs[-1][...] = total_of(panel_ref, refs[:-1], places)


def begin(panel, rights, places):
    return pl.pallas_call(
        functools.partial(begin_kernel, places), in_specs=[VMEM] * (1 + len(rights)), out_specs=VMEM,
        out_shape=jax.ShapeDtypeStruct((panel.shape[1], rights[0].shape[1]), F32),
        compiler_params=LARGE, cost_estimate=cost(6, panel, rights[0]), name="begin",
    )(panel, *rights)


def finish_kernel(middle, places, where_ref, panel_ref, sum_ref, *refs):
    keep_ref, out_ref = refs[-2:]
    total = sum_ref[...] + total_of(panel_ref, refs[:-2], places)
    total = keep_ref[...].astype(F32) * total
    if middle:
        diagonal = (lax.broadcasted_iota(jnp.int32, total.shape, 0) + where_ref[2 * TILES]
                    == lax.broadcasted_iota(jnp.int32, total.shape, 1))
        total = jnp.where(diagonal, 1.5, 0.0) - 0.5 * total
    out_ref[...] = total.astype(BF16)


def finish(where, panel, begun, rights, places, keep, middle):
    return pl.pallas_call(
        functools.partial(finish_kernel, middle, places),
        in_specs=[SMEM] + [VMEM] * (3 + len(rights)), out_specs=VMEM,
        out_shape=jax.ShapeDtypeStruct(keep.shape, BF16),
        compiler_params=LARGE, cost_estimate=cost(2, panel, rights[0]), name="finish",
    )(where, panel, begun, *rights, keep)


def around(block, axis):
    return send(block, axis(1)), send(block, axis(3))


def opposite(up, down, axis):
    half = up.shape[0] // 2
    return send(up[:half], axis(1)), send(down[half:], axis(3))


def together(*arrays):
    return lax.optimization_barrier(arrays)


def gather(block):
    f1, f3 = around(block, first_axis)
    near = join(block, f1)
    near1, near3 = together(*around(near, second_axis))
    far = join(f3, *opposite(f1, f3, first_axis))
    near2 = opposite(near1, near3, second_axis)
    far1, far3 = together(*around(far, second_axis))
    half = block.shape[0]
    early = [near, far, near1, far1, near3, far3, *near2]
    places = [(0, 0), (1, 0), (2, 0), (3, 0), (6, 0), (7, 0), (4, 0), (4, half)]
    return early, places, opposite(far1, far3, second_axis), [(5, 0), (5, half)]


def local(matrix, pattern):
    size = matrix.shape[0]
    row, col = lax.axis_index("row"), lax.axis_index("col")
    y, x, z, c = row >> 2, row & 3, col >> 1, col & 1
    up = 1 - 2 * c
    along, against = [(z - s * up) & 7 for s in range(5)], [(z + s * up) & 7 for s in range(5)]
    tiles = [2 * a + c for a in along] + [2 * a + 1 - c for a in along[:4]]
    tiles += [2 * a + 1 - c for a in against[1:]] + [2 * a + c for a in against[1:4]]
    pairs, sides = [], []
    for tile in tiles:
        dy, dx = (y - (tile >> 2)) & 3, (x - (tile & 3)) & 3
        first, second = jnp.where(c == 0, dx, dy), jnp.where(c == 0, dy, dx)
        pairs.append(2 * second + (first >> 1))
        sides.append((first ^ (first >> 1)) & 1)
    where = jnp.stack(pairs + sides + [(row - col) * size]).astype(jnp.int32)

    matrix, where = lax.optimization_barrier((matrix, where))
    masked, keep = mask(matrix, pattern)
    own, other = [masked], [send(masked, SWAP)]
    f1, f3 = around(masked, first_axis)
    f2 = send(masked, first_axis(2))
    own.append(send(own[0], RING))
    other.append(send(other[0], RING))
    own[1], f1, f3, f2 = together(own[1], f1, f3, f2)
    full = join(masked, f1, f3, f2)
    full1, full3 = around(full, second_axis)
    for _ in range(2):
        own.append(send(own[-1], RING))
        other.append(send(other[-1], RING))
    own.append(send(own[-1], RING))
    late = opposite(full1, full3, second_axis)
    swapped = [send(a, SWAP) for a in own[1:] + other[1:]]
    swapped[-1], *late = together(swapped[-1], *late)
    panel = arrange(where, own + other + swapped)
    begun = begin(panel, [full, full1, full3], [(0, 0), (2, 0), (6, 0)])
    middle = finish(where, panel, begun, late, [(4, 0), (5, 0)], keep, True)
    early, places, late, late_places = gather(middle)
    return finish(where, panel, begin(panel, early, places), late, late_places, keep, False)


def solution(mesh):
    spec = P("row", "col")
    return jax.shard_map(local, mesh=mesh, in_specs=(spec, spec), out_specs=spec, check_vma=False)
```

time: 265 us -> 133 us (0.50)
  waiting for transfers between devices: 225 us -> 62 us
  starting transfers between devices: 0.08 us -> 54.4 us
  matrix products: 22.2 us -> 0 us
  Pallas kernels: 0 us -> 13.1 us
  between operations: 13.1 us -> 0.19 us
    all_gather x3 -> x0, waiting for transfers between devices: 224 us -> none  [the longest x2 166 us: gather_right(): return lax.all_gather(operand, 'row', axis=0, tiled=True)]
    ppermute x0 -> x34, waiting for transfers between devices: none -> 62 us  [send(): return lax.ppermute(block, AXES, pairs)]
    ppermute x0 -> x34, starting transfers between devices: none -> 54.4 us  [send(): return lax.ppermute(block, AXES, pairs)]
    dot_general x2 -> x0, matrix products: 22.2 us -> none  [multiply_passed(): jnp.dot(lax.all_gather(left, 'col', axis=1, tiled=True), gathered, prefer...]
    pallas_call x0 -> x9, Pallas kernels: none -> 13.1 us  [the longest x2 7.34 us: begin(): pl.pallas_call(functools.partial(begin_kernel, places), in_specs=[VMEM] *...]
  transfers between devices with their start and end apart: 3 -> 34, of which waited for: 3 -> 21; matrix products, arithmetic and copies ran while one was open for 0% -> 0% of each run, Pallas kernels for 0% -> 3%
where the time goes in v2:
time: 133 us; the launch traced here: 132 us
  waiting for transfers between devices  62 us (47%)
  starting transfers between devices  54.4 us (41%)
  Pallas kernels  13.1 us (10%)
  local copies, waits for them, and re-layouts  2.15 us (2%)
    ppermute x34, waiting for transfers between devices, send(): return lax.ppermute(block, AXES, pairs)  62 us
    ppermute x34, starting transfers between devices, send(): return lax.ppermute(block, AXES, pairs)  54.4 us
    pallas_call x2, Pallas kernels, begin(): pl.pallas_call(functools.partial(begin_kernel, places), in_specs=[VMEM] *...  7.34 us
    pallas_call x2, Pallas kernels, finish(): pl.pallas_call(functools.partial(finish_kernel, middle, places), in_specs...  3.94 us
  transfers between devices with their start and end apart: 34, of which 21 were waited for; matrix products, arithmetic and copies ran while one was open for 0% of the time, Pallas kernels for 3%

profile of v2, /device:TPU:1, one launch (start us, length us, event | category | flops | bytes accessed | tf_op | source)
XLA Modules:
  0.0 131.9 jit_solution(13951989832765970865)
XLA Ops:
  0.0 0.1 stack.135.where_ref
  0.1 1.0 copy-done
  1.2 0.7 copy-done.1
  1.8 0.4 mask.1
  2.2 3.8 %collective-permute-start.3 = (bf16[512,512]{1,0:T(8,128)(2,1)S(1)}, bf16[512,512]{1,0:T(8,128)(2,1)S(1)}, u32[]{:S(2)}, u32[]{:S(2)}) collective-permute-start(bf16[512,512]{1,0:T(8,128)(2,1)S(1)} %get-tuple-element.22.refs_0_), channel_id=1, source_target_pairs={{0,32},{1,129},{2,34},{3,131},{4,36},{5,133},{6,38},{7,135},{8,40}... | collective-permute-start | bytes 1572872 | tf_op jit(solution)/shard_map/ppermute | solution.py:41
  6.1 0.8 collective-permute-start.2
  6.9 0.7 collective-permute-start.1
  7.5 5.6 %collective-permute-start = (bf16[512,512]{1,0:T(8,128)(2,1)S(1)}, bf16[512,512]{1,0:T(8,128)(2,1)S(1)}, u32[]{:S(2)}, u32[]{:S(2)}) collective-permute-start(bf16[512,512]{1,0:T(8,128)(2,1)S(1)} %get-tuple-element.22.refs_0_), channel_id=1, source_target_pairs={{0,2},{1,15},{2,4},{3,1},{4,6},{5,3},{6,8},{7,5},{8,10},{9,7},{10,... | collective-permute-start | bytes 1572872 | tf_op jit(solution)/shard_map/ppermute | solution.py:41
  13.1 5.9 %collective-permute-done.2.refs_2_ = bf16[512,512]{1,0:T(8,128)(2,1)S(1)} collective-permute-done((bf16[512,512]{1,0:T(8,128)(2,1)S(1)}, bf16[512,512]{1,0:T(8,128)(2,1)S(1)}, u32[]{:S(2)}, u32[]{:S(2)}) %collective-permute-start.2) | collective-permute-done | bytes 524320 | tf_op jit(solution)/shard_map/ppermute | solution.py:41
  19.0 0.2 collective-permute-done.refs_1_
  19.2 0.1 join.3.refs_0_
  19.4 2.6 %collective-permute-start.20 = (bf16[2048,512]{1,0:T(8,128)(2,1)S(1)}, bf16[2048,512]{1,0:T(8,128)(2,1)S(1)}, u32[]{:S(2)}, u32[]{:S(2)}) collective-permute-start(bf16[2048,512]{1,0:T(8,128)(2,1)S(1)} %join.3.refs_0_), channel_id=1, source_target_pairs={{0,192},{1,49},{2,194},{3,51},{4,196},{5,53},{6,198},{7,55},{8,200... | collective-permute-start | bytes 6291464 | tf_op jit(solution)/shard_map/ppermute | solution.py:41
  21.9 3.2 %collective-permute-start.7 = (bf16[512,512]{1,0:T(8,128)(2,1)S(1)}, bf16[512,512]{1,0:T(8,128)(2,1)S(1)}, u32[]{:S(2)}, u32[]{:S(2)}) collective-permute-start(bf16[512,512]{1,0:T(8,128)(2,1)S(1)} %get-tuple-element.22.refs_0_), channel_id=1, source_target_pairs={{0,1},{1,0},{2,3},{3,2},{4,5},{5,4},{6,7},{7,6},{8,9},{9,8},{10,11... | collective-permute-start | bytes 1572872 | tf_op jit(solution)/shard_map/ppermute | solution.py:41
  25.1 1.5 %collective-permute-done.7.refs_5_ = bf16[512,512]{1,0:T(8,128)(2,1)S(1)} collective-permute-done((bf16[512,512]{1,0:T(8,128)(2,1)S(1)}, bf16[512,512]{1,0:T(8,128)(2,1)S(1)}, u32[]{:S(2)}, u32[]{:S(2)}) %collective-permute-start.7) | collective-permute-done | bytes 524320 | tf_op jit(solution)/shard_map/ppermute | solution.py:41
  26.7 3.9 %collective-permute-start.8 = (bf16[512,512]{1,0:T(8,128)(2,1)S(1)}, bf16[512,512]{1,0:T(8,128)(2,1)S(1)}, u32[]{:S(2)}, u32[]{:S(2)}) collective-permute-start(bf16[512,512]{1,0:T(8,128)(2,1)S(1)} %collective-permute-done.7.refs_5_), channel_id=1, source_target_pairs={{0,2},{1,15},{2,4},{3,1},{4,6},{5,3},{6,8},{7,5},{8,10},{9,7},{10,... | collective-permute-start | bytes 1572872 | tf_op jit(solution)/shard_map/ppermute | solution.py:41
  30.6 0.7 collective-permute-start.4
  31.3 5.4 %collective-permute-done.8.refs_6_ = bf16[512,512]{1,0:T(8,128)(2,1)S(1)} collective-permute-done((bf16[512,512]{1,0:T(8,128)(2,1)S(1)}, bf16[512,512]{1,0:T(8,128)(2,1)S(1)}, u32[]{:S(2)}, u32[]{:S(2)}) %collective-permute-start.8) | collective-permute-done | bytes 524320 | tf_op jit(solution)/shard_map/ppermute | solution.py:41
  36.7 3.4 %collective-permute-start.9 = (bf16[512,512]{1,0:T(8,128)(2,1)S(1)}, bf16[512,512]{1,0:T(8,128)(2,1)S(1)}, u32[]{:S(2)}, u32[]{:S(2)}) collective-permute-start(bf16[512,512]{1,0:T(8,128)(2,1)S(1)} %collective-permute-done.8.refs_6_), channel_id=1, source_target_pairs={{0,2},{1,15},{2,4},{3,1},{4,6},{5,3},{6,8},{7,5},{8,10},{9,7},{10,... | collective-permute-start | bytes 1572872 | tf_op jit(solution)/shard_map/ppermute | solution.py:41
  40.2 2.2 %collective-permute-done.4.refs_2_ = bf16[512,512]{1,0:T(8,128)(2,1)S(1)} collective-permute-done((bf16[512,512]{1,0:T(8,128)(2,1)S(1)}, bf16[512,512]{1,0:T(8,128)(2,1)S(1)}, u32[]{:S(2)}, u32[]{:S(2)}) %collective-permute-start.4) | collective-permute-done | bytes 524320 | tf_op jit(solution)/shard_map/ppermute | solution.py:41
  42.4 3.4 %collective-permute-start.5 = (bf16[512,512]{1,0:T(8,128)(2,1)S(1)}, bf16[512,512]{1,0:T(8,128)(2,1)S(1)}, u32[]{:S(2)}, u32[]{:S(2)}) collective-permute-start(bf16[512,512]{1,0:T(8,128)(2,1)S(1)} %collective-permute-done.4.refs_2_), channel_id=1, source_target_pairs={{0,2},{1,15},{2,4},{3,1},{4,6},{5,3},{6,8},{7,5},{8,10},{9,7},{10,... | collective-permute-start | bytes 1572872 | tf_op jit(solution)/shard_map/ppermute | solution.py:41
  45.8 2.2 %collective-permute-done.9.refs_7_ = bf16[512,512]{1,0:T(8,128)(2,1)S(1)} collective-permute-done((bf16[512,512]{1,0:T(8,128)(2,1)S(1)}, bf16[512,512]{1,0:T(8,128)(2,1)S(1)}, u32[]{:S(2)}, u32[]{:S(2)}) %collective-permute-start.9) | collective-permute-done | bytes 524320 | tf_op jit(solution)/shard_map/ppermute | solution.py:41
  48.0 3.4 %collective-permute-start.10 = (bf16[512,512]{1,0:T(8,128)(2,1)S(1)}, bf16[512,512]{1,0:T(8,128)(2,1)S(1)}, u32[]{:S(2)}, u32[]{:S(2)}) collective-permute-start(bf16[512,512]{1,0:T(8,128)(2,1)S(1)} %collective-permute-done.9.refs_7_), channel_id=1, source_target_pairs={{0,2},{1,15},{2,4},{3,1},{4,6},{5,3},{6,8},{7,5},{8,10},{9,7},{10,... | collective-permute-start | bytes 1572872 | tf_op jit(solution)/shard_map/ppermute | solution.py:41
  51.4 0.1 slice.33
  51.5 2.4 %collective-permute-start.21 = (bf16[1024,512]{1,0:T(8,128)(2,1)S(1)}, bf16[1024,512]{1,0:T(8,128)(2,1)S(1)}, u32[]{:S(2)}, u32[]{:S(2)}) collective-permute-start(bf16[1024,512]{1,0:T(8,128)(2,1)S(1)} %slice.33), channel_id=1, source_target_pairs={{0,192},{1,49},{2,194},{3,51},{4,196},{5,53},{6,198},{7,55},{8,200... | collective-permute-start | bytes 3145736 | tf_op jit(solution)/shard_map/ppermute | solution.py:41
  53.9 0.1 slice.32
  54.0 0.1 collective-permute-start.19
  54.1 0.1 collective-permute-start.11
  54.2 2.6 %collective-permute-start.6 = (bf16[512,512]{1,0:T(8,128)(2,1)S(1)}, bf16[512,512]{1,0:T(8,128)(2,1)S(1)}, u32[]{:S(2)}, u32[]{:S(2)}) collective-permute-start(bf16[512,512]{1,0:T(8,128)(2,1)S(1)} %collective-permute-done.5.refs_3_), channel_id=1, source_target_pairs={{0,2},{1,15},{2,4},{3,1},{4,6},{5,3},{6,8},{7,5},{8,10},{9,7},{10,... | collective-permute-start | bytes 1572872 | tf_op jit(solution)/shard_map/ppermute | solution.py:41
  56.7 2.5 %collective-permute-done.10.refs_8_ = bf16[512,512]{1,0:T(8,128)(2,1)S(1)} collective-permute-done((bf16[512,512]{1,0:T(8,128)(2,1)S(1)}, bf16[512,512]{1,0:T(8,128)(2,1)S(1)}, u32[]{:S(2)}, u32[]{:S(2)}) %collective-permute-start.10) | collective-permute-done | bytes 524320 | tf_op jit(solution)/shard_map/ppermute | solution.py:41
  59.2 1.7 %collective-permute-start.17 = (bf16[512,512]{1,0:T(8,128)(2,1)S(1)}, bf16[512,512]{1,0:T(8,128)(2,1)S(1)}, u32[]{:S(2)}, u32[]{:S(2)}) collective-permute-start(bf16[512,512]{1,0:T(8,128)(2,1)S(1)} %collective-permute-done.10.refs_8_), channel_id=1, source_target_pairs={{0,1},{1,0},{2,3},{3,2},{4,5},{5,4},{6,7},{7,6},{8,9},{9,8},{10,11... | collective-permute-start | bytes 1572872 | tf_op jit(solution)/shard_map/ppermute | solution.py:41
  60.9 3.9 %collective-permute-done.6.refs_4_ = bf16[512,512]{1,0:T(8,128)(2,1)S(1)} collective-permute-done((bf16[512,512]{1,0:T(8,128)(2,1)S(1)}, bf16[512,512]{1,0:T(8,128)(2,1)S(1)}, u32[]{:S(2)}, u32[]{:S(2)}) %collective-permute-start.6) | collective-permute-done | bytes 524320 | tf_op jit(solution)/shard_map/ppermute | solution.py:41
  64.8 1.7 %collective-permute-start.12 = (bf16[512,512]{1,0:T(8,128)(2,1)S(1)}, bf16[512,512]{1,0:T(8,128)(2,1)S(1)}, u32[]{:S(2)}, u32[]{:S(2)}) collective-permute-start(bf16[512,512]{1,0:T(8,128)(2,1)S(1)} %collective-permute-done.4.refs_2_), channel_id=1, source_target_pairs={{0,1},{1,0},{2,3},{3,2},{4,5},{5,4},{6,7},{7,6},{8,9},{9,8},{10,11... | collective-permute-start | bytes 1572872 | tf_op jit(solution)/shard_map/ppermute | solution.py:41
  66.5 0.5 collective-permute-start.13
  67.0 1.9 %collective-permute-done.19.refs_0_ = bf16[1024,512]{1,0:T(8,128)(2,1)S(1)} collective-permute-done((bf16[1024,512]{1,0:T(8,128)(2,1)S(1)}, bf16[1024,512]{1,0:T(8,128)(2,1)S(1)}, u32[]{:S(2)}, u32[]{:S(2)}) %collective-permute-start.19) | collective-permute-done | bytes 1048608 | tf_op jit(solution)/shard_map/ppermute | solution.py:41
  68.9 0.3 collective-permute-start.14
  69.2 0.3 collective-permute-done.13.refs_11_
  69.6 1.3 collective-permute-done.14.refs_12_
  70.8 1.2 arrange.1.panel_ref
  72.0 3.4 %begin.2.sum_ref = f32[512,512]{1,0:T(8,128)S(1)} custom-call(bf16[8,512,1024]{2,1,0:T(8,128)(2,1)S(1)} %arrange.1.panel_ref, bf16[2048,512]{1,0:T(8,128)(2,1)S(1)} %join.3.refs_0_, bf16[2048,512]{1,0:T(8,128)(2,1)S(1)} %collective-permute-done.18.refs_1_, bf16[2048,512]{1,0:T(8,128)(2,1)S(1)} %collective-permute-done.20.refs_2_), custom_call_target="tpu_custom_call" | custom-call | flops 6442450944 | bytes 25165824 | tf_op jit(solution)/shard_map/begin/pallas_call | solution.py:122
  75.4 1.9 %finish.2.refs_0_ = bf16[512,512]{1,0:T(8,128)(2,1)S(1)} custom-call(s32[33]{0:T(128)S(1)} %stack.135.where_ref, bf16[8,512,1024]{2,1,0:T(8,128)(2,1)S(1)} %arrange.1.panel_ref, f32[512,512]{1,0:T(8,128)S(1)} %begin.2.sum_ref, bf16[1024,512]{1,0:T(8,128)(2,1)S(1)} %collective-permute-done.19.refs_0_, bf16[1024,512]{1,0:T(8,128)(2,1)S(1)} %collective-permute-done.21.refs_1_, ...), custom_call_target="tpu_custom_call" | custom-call | flops 1073741824 | bytes 4194304 | tf_op jit(solution)/shard_map/finish/pallas_call | solution.py:141
  77.3 0.1 collective-permute-start.22
  77.4 3.0 %collective-permute-start.23 = (bf16[512,512]{1,0:T(8,128)(2,1)S(1)}, bf16[512,512]{1,0:T(8,128)(2,1)S(1)}, u32[]{:S(2)}, u32[]{:S(2)}) collective-permute-start(bf16[512,512]{1,0:T(8,128)(2,1)S(1)} %finish.2.refs_0_), channel_id=1, source_target_pairs={{0,48},{1,193},{2,50},{3,195},{4,52},{5,197},{6,54},{7,199},{8,56}... | collective-permute-start | bytes 1572872 | tf_op jit(solution)/shard_map/ppermute | solution.py:41
  80.5 6.8 %collective-permute-done.22.refs_1_ = bf16[512,512]{1,0:T(8,128)(2,1)S(1)} collective-permute-done((bf16[512,512]{1,0:T(8,128)(2,1)S(1)}, bf16[512,512]{1,0:T(8,128)(2,1)S(1)}, u32[]{:S(2)}, u32[]{:S(2)}) %collective-permute-start.22) | collective-permute-done | bytes 524320 | tf_op jit(solution)/shard_map/ppermute | solution.py:41
  87.2 0.1 join.4.refs_0_
  87.3 2.1 %collective-permute-start.27 = (bf16[1024,512]{1,0:T(8,128)(2,1)S(1)}, bf16[1024,512]{1,0:T(8,128)(2,1)S(1)}, u32[]{:S(2)}, u32[]{:S(2)}) collective-permute-start(bf16[1024,512]{1,0:T(8,128)(2,1)S(1)} %join.4.refs_0_), channel_id=1, source_target_pairs={{0,192},{1,49},{2,194},{3,51},{4,196},{5,53},{6,198},{7,55},{8,200... | collective-permute-start | bytes 3145736 | tf_op jit(solution)/shard_map/ppermute | solution.py:41
  89.4 1.4 %collective-permute-start.25 = (bf16[256,512]{1,0:T(8,128)(2,1)S(1)}, bf16[256,512]{1,0:T(8,128)(2,1)S(1)}, u32[]{:S(2)}, u32[]{:S(2)}) collective-permute-start(bf16[256,512]{1,0:T(8,128)(2,1)S(1)} %slice.35), channel_id=1, source_target_pairs={{0,48},{1,193},{2,50},{3,195},{4,52},{5,197},{6,54},{7,199},{8,56}... | collective-permute-start | bytes 786440 | tf_op jit(solution)/shard_map/ppermute | solution.py:41
  90.8 0.3 collective-permute-start.24
  91.1 6.7 %collective-permute-done.25.refs_2_ = bf16[256,512]{1,0:T(8,128)(2,1)S(1)} collective-permute-done((bf16[256,512]{1,0:T(8,128)(2,1)S(1)}, bf16[256,512]{1,0:T(8,128)(2,1)S(1)}, u32[]{:S(2)}, u32[]{:S(2)}) %collective-permute-start.25) | collective-permute-done | bytes 262176 | tf_op jit(solution)/shard_map/ppermute | solution.py:41
  97.8 1.8 %collective-permute-done.24.refs_1_ = bf16[256,512]{1,0:T(8,128)(2,1)S(1)} collective-permute-done((bf16[256,512]{1,0:T(8,128)(2,1)S(1)}, bf16[256,512]{1,0:T(8,128)(2,1)S(1)}, u32[]{:S(2)}, u32[]{:S(2)}) %collective-permute-start.24) | collective-permute-done | bytes 262176 | tf_op jit(solution)/shard_map/ppermute | solution.py:41
  99.5 0.1 join.5.refs_1_
  99.6 3.6 %collective-permute-start.29 = (bf16[1024,512]{1,0:T(8,128)(2,1)S(1)}, bf16[1024,512]{1,0:T(8,128)(2,1)S(1)}, u32[]{:S(2)}, u32[]{:S(2)}) collective-permute-start(bf16[1024,512]{1,0:T(8,128)(2,1)S(1)} %join.5.refs_1_), channel_id=1, source_target_pairs={{0,192},{1,49},{2,194},{3,51},{4,196},{5,53},{6,198},{7,55},{8,200... | collective-permute-start | bytes 3145736 | tf_op jit(solution)/shard_map/ppermute | solution.py:41
  103.2 0.9 collective-permute-done.27.refs_4_
  104.1 3.2 %collective-permute-done.26.refs_2_ = bf16[1024,512]{1,0:T(8,128)(2,1)S(1)} collective-permute-done((bf16[1024,512]{1,0:T(8,128)(2,1)S(1)}, bf16[1024,512]{1,0:T(8,128)(2,1)S(1)}, u32[]{:S(2)}, u32[]{:S(2)}) %collective-permute-start.26) | collective-permute-done | bytes 1048608 | tf_op jit(solution)/shard_map/ppermute | solution.py:41
  107.4 0.1 collective-permute-start.31
  107.5 1.5 %collective-permute-start.30 = (bf16[512,512]{1,0:T(8,128)(2,1)S(1)}, bf16[512,512]{1,0:T(8,128)(2,1)S(1)}, u32[]{:S(2)}, u32[]{:S(2)}) collective-permute-start(bf16[512,512]{1,0:T(8,128)(2,1)S(1)} %slice.28), channel_id=1, source_target_pairs={{0,64},{1,17},{2,66},{3,19},{4,68},{5,21},{6,70},{7,23},{8,72},{9,... | collective-permute-start | bytes 1572872 | tf_op jit(solution)/shard_map/ppermute | solution.py:41
  109.0 6.4 %collective-permute-done.29.refs_5_ = bf16[1024,512]{1,0:T(8,128)(2,1)S(1)} collective-permute-done((bf16[1024,512]{1,0:T(8,128)(2,1)S(1)}, bf16[1024,512]{1,0:T(8,128)(2,1)S(1)}, u32[]{:S(2)}, u32[]{:S(2)}) %collective-permute-start.29) | collective-permute-done | bytes 1048608 | tf_op jit(solution)/shard_map/ppermute | solution.py:41
  115.4 3.2 %collective-permute-done.28.refs_3_ = bf16[1024,512]{1,0:T(8,128)(2,1)S(1)} collective-permute-done((bf16[1024,512]{1,0:T(8,128)(2,1)S(1)}, bf16[1024,512]{1,0:T(8,128)(2,1)S(1)}, u32[]{:S(2)}, u32[]{:S(2)}) %collective-permute-start.28) | collective-permute-done | bytes 1048608 | tf_op jit(solution)/shard_map/ppermute | solution.py:41
  118.7 0.1 collective-permute-start.33
  118.8 1.5 %collective-permute-start.32 = (bf16[512,512]{1,0:T(8,128)(2,1)S(1)}, bf16[512,512]{1,0:T(8,128)(2,1)S(1)}, u32[]{:S(2)}, u32[]{:S(2)}) collective-permute-start(bf16[512,512]{1,0:T(8,128)(2,1)S(1)} %slice.30), channel_id=1, source_target_pairs={{0,64},{1,17},{2,66},{3,19},{4,68},{5,21},{6,70},{7,23},{8,72},{9,... | collective-permute-start | bytes 1572872 | tf_op jit(solution)/shard_map/ppermute | solution.py:41
  120.2 0.8 collective-permute-done.31.refs_7_
  121.0 3.2 %collective-permute-done.30.refs_6_ = bf16[512,512]{1,0:T(8,128)(2,1)S(1)} collective-permute-done((bf16[512,512]{1,0:T(8,128)(2,1)S(1)}, bf16[512,512]{1,0:T(8,128)(2,1)S(1)}, u32[]{:S(2)}, u32[]{:S(2)}) %collective-permute-start.30) | collective-permute-done | bytes 524320 | tf_op jit(solution)/shard_map/ppermute | solution.py:41
  124.2 3.9 %begin.3.sum_ref = f32[512,512]{1,0:T(8,128)S(1)} custom-call(bf16[8,512,1024]{2,1,0:T(8,128)(2,1)S(1)} %arrange.1.panel_ref, bf16[1024,512]{1,0:T(8,128)(2,1)S(1)} %join.4.refs_0_, bf16[1024,512]{1,0:T(8,128)(2,1)S(1)} %join.5.refs_1_, bf16[1024,512]{1,0:T(8,128)(2,1)S(1)} %collective-permute-done.26.refs_2_, ...), custom_call_target="tpu_custom_call" | custom-call | flops 3221225472 | bytes 12582912 | tf_op jit(solution)/shard_map/begin/pallas_call | solution.py:122
  128.2 1.7 %collective-permute-done.32.refs_0_ = bf16[512,512]{1,0:T(8,128)(2,1)S(1)} collective-permute-done((bf16[512,512]{1,0:T(8,128)(2,1)S(1)}, bf16[512,512]{1,0:T(8,128)(2,1)S(1)}, u32[]{:S(2)}, u32[]{:S(2)}) %collective-permute-start.32) | collective-permute-done | bytes 524320 | tf_op jit(solution)/shard_map/ppermute | solution.py:41
  129.8 2.0 %finish.3 = bf16[512,512]{1,0:T(8,128)(2,1)} custom-call(s32[33]{0:T(128)S(1)} %stack.135.where_ref, bf16[8,512,1024]{2,1,0:T(8,128)(2,1)S(1)} %arrange.1.panel_ref, f32[512,512]{1,0:T(8,128)S(1)} %begin.3.sum_ref, bf16[512,512]{1,0:T(8,128)(2,1)S(1)} %collective-permute-done.32.refs_0_, bf16[512,512]{1,0:T(8,128)(2,1)S(1)} %collective-permute-done.33.refs_1_, ...), custom_call_target="tpu_custom_call" | custom-call | flops 536870912 | bytes 2097152 | tf_op jit(solution)/shard_map/finish/pallas_call | solution.py:141
  (26 shorter events, 0.2 us)
Async XLA Ops:
  0.1 1.0 copy-start
  1.2 0.7 copy-start.1
  2.2 10.9 %collective-permute-start.3 = (bf16[512,512]{1,0:T(8,128)(2,1)S(1)}, bf16[512,512]{1,0:T(8,128)(2,1)S(1)}, u32[]{:S(2)}, u32[]{:S(2)}) collective-permute-start(bf16[512,512]{1,0:T(8,128)(2,1)S(1)} %get-tuple-element.22.refs_0_), channel_id=1, source_target_pairs={{0,32},{1,129},{2,34},{3,131},{4,36},{5,133},{6,38},{7,135},{8,40}... | collective-permute-start | bytes 1572872 | tf_op jit(solution)/shard_map/ppermute | solution.py:41
  6.1 12.9 %collective-permute-start.2 = (bf16[512,512]{1,0:T(8,128)(2,1)S(1)}, bf16[512,512]{1,0:T(8,128)(2,1)S(1)}, u32[]{:S(2)}, u32[]{:S(2)}) collective-permute-start(bf16[512,512]{1,0:T(8,128)(2,1)S(1)} %get-tuple-element.22.refs_0_), channel_id=1, source_target_pairs={{0,48},{1,193},{2,50},{3,195},{4,52},{5,197},{6,54},{7,199},{8,56}... | collective-permute-start | bytes 1572872 | tf_op jit(solution)/shard_map/ppermute | solution.py:41
  6.9 12.1 %collective-permute-start.1 = (bf16[512,512]{1,0:T(8,128)(2,1)S(1)}, bf16[512,512]{1,0:T(8,128)(2,1)S(1)}, u32[]{:S(2)}, u32[]{:S(2)}) collective-permute-start(bf16[512,512]{1,0:T(8,128)(2,1)S(1)} %get-tuple-element.22.refs_0_), channel_id=1, source_target_pairs={{0,16},{1,65},{2,18},{3,67},{4,20},{5,69},{6,22},{7,71},{8,24},{9,... | collective-permute-start | bytes 1572872 | tf_op jit(solution)/shard_map/ppermute | solution.py:41
  7.5 11.7 %collective-permute-start = (bf16[512,512]{1,0:T(8,128)(2,1)S(1)}, bf16[512,512]{1,0:T(8,128)(2,1)S(1)}, u32[]{:S(2)}, u32[]{:S(2)}) collective-permute-start(bf16[512,512]{1,0:T(8,128)(2,1)S(1)} %get-tuple-element.22.refs_0_), channel_id=1, source_target_pairs={{0,2},{1,15},{2,4},{3,1},{4,6},{5,3},{6,8},{7,5},{8,10},{9,7},{10,... | collective-permute-start | bytes 1572872 | tf_op jit(solution)/shard_map/ppermute | solution.py:41
  19.4 32.0 %collective-permute-start.20 = (bf16[2048,512]{1,0:T(8,128)(2,1)S(1)}, bf16[2048,512]{1,0:T(8,128)(2,1)S(1)}, u32[]{:S(2)}, u32[]{:S(2)}) collective-permute-start(bf16[2048,512]{1,0:T(8,128)(2,1)S(1)} %join.3.refs_0_), channel_id=1, source_target_pairs={{0,192},{1,49},{2,194},{3,51},{4,196},{5,53},{6,198},{7,55},{8,200... | collective-permute-start | bytes 6291464 | tf_op jit(solution)/shard_map/ppermute | solution.py:41
  21.9 32.0 %collective-permute-start.18 = (bf16[2048,512]{1,0:T(8,128)(2,1)S(1)}, bf16[2048,512]{1,0:T(8,128)(2,1)S(1)}, u32[]{:S(2)}, u32[]{:S(2)}) collective-permute-start(bf16[2048,512]{1,0:T(8,128)(2,1)S(1)} %join.3.refs_0_), channel_id=1, source_target_pairs={{0,64},{1,17},{2,66},{3,19},{4,68},{5,21},{6,70},{7,23},{8,72},{9,... | collective-permute-start | bytes 6291464 | tf_op jit(solution)/shard_map/ppermute | solution.py:41
  21.9 4.7 %collective-permute-start.7 = (bf16[512,512]{1,0:T(8,128)(2,1)S(1)}, bf16[512,512]{1,0:T(8,128)(2,1)S(1)}, u32[]{:S(2)}, u32[]{:S(2)}) collective-permute-start(bf16[512,512]{1,0:T(8,128)(2,1)S(1)} %get-tuple-element.22.refs_0_), channel_id=1, source_target_pairs={{0,1},{1,0},{2,3},{3,2},{4,5},{5,4},{6,7},{7,6},{8,9},{9,8},{10,11... | collective-permute-start | bytes 1572872 | tf_op jit(solution)/shard_map/ppermute | solution.py:41
  26.7 10.1 %collective-permute-start.8 = (bf16[512,512]{1,0:T(8,128)(2,1)S(1)}, bf16[512,512]{1,0:T(8,128)(2,1)S(1)}, u32[]{:S(2)}, u32[]{:S(2)}) collective-permute-start(bf16[512,512]{1,0:T(8,128)(2,1)S(1)} %collective-permute-done.7.refs_5_), channel_id=1, source_target_pairs={{0,2},{1,15},{2,4},{3,1},{4,6},{5,3},{6,8},{7,5},{8,10},{9,7},{10,... | collective-permute-start | bytes 1572872 | tf_op jit(solution)/shard_map/ppermute | solution.py:41
  30.6 11.7 %collective-permute-start.4 = (bf16[512,512]{1,0:T(8,128)(2,1)S(1)}, bf16[512,512]{1,0:T(8,128)(2,1)S(1)}, u32[]{:S(2)}, u32[]{:S(2)}) collective-permute-start(bf16[512,512]{1,0:T(8,128)(2,1)S(1)} %collective-permute-done.refs_1_), channel_id=1, source_target_pairs={{0,2},{1,15},{2,4},{3,1},{4,6},{5,3},{6,8},{7,5},{8,10},{9,7},{10,... | collective-permute-start | bytes 1572872 | tf_op jit(solution)/shard_map/ppermute | solution.py:41
  36.7 11.2 %collective-permute-start.9 = (bf16[512,512]{1,0:T(8,128)(2,1)S(1)}, bf16[512,512]{1,0:T(8,128)(2,1)S(1)}, u32[]{:S(2)}, u32[]{:S(2)}) collective-permute-start(bf16[512,512]{1,0:T(8,128)(2,1)S(1)} %collective-permute-done.8.refs_6_), channel_id=1, source_target_pairs={{0,2},{1,15},{2,4},{3,1},{4,6},{5,3},{6,8},{7,5},{8,10},{9,7},{10,... | collective-permute-start | bytes 1572872 | tf_op jit(solution)/shard_map/ppermute | solution.py:41
  42.4 11.8 %collective-permute-start.5 = (bf16[512,512]{1,0:T(8,128)(2,1)S(1)}, bf16[512,512]{1,0:T(8,128)(2,1)S(1)}, u32[]{:S(2)}, u32[]{:S(2)}) collective-permute-start(bf16[512,512]{1,0:T(8,128)(2,1)S(1)} %collective-permute-done.4.refs_2_), channel_id=1, source_target_pairs={{0,2},{1,15},{2,4},{3,1},{4,6},{5,3},{6,8},{7,5},{8,10},{9,7},{10,... | collective-permute-start | bytes 1572872 | tf_op jit(solution)/shard_map/ppermute | solution.py:41
  48.0 11.2 %collective-permute-start.10 = (bf16[512,512]{1,0:T(8,128)(2,1)S(1)}, bf16[512,512]{1,0:T(8,128)(2,1)S(1)}, u32[]{:S(2)}, u32[]{:S(2)}) collective-permute-start(bf16[512,512]{1,0:T(8,128)(2,1)S(1)} %collective-permute-done.9.refs_7_), channel_id=1, source_target_pairs={{0,2},{1,15},{2,4},{3,1},{4,6},{5,3},{6,8},{7,5},{8,10},{9,7},{10,... | collective-permute-start | bytes 1572872 | tf_op jit(solution)/shard_map/ppermute | solution.py:41
  51.5 15.1 %collective-permute-start.21 = (bf16[1024,512]{1,0:T(8,128)(2,1)S(1)}, bf16[1024,512]{1,0:T(8,128)(2,1)S(1)}, u32[]{:S(2)}, u32[]{:S(2)}) collective-permute-start(bf16[1024,512]{1,0:T(8,128)(2,1)S(1)} %slice.33), channel_id=1, source_target_pairs={{0,192},{1,49},{2,194},{3,51},{4,196},{5,53},{6,198},{7,55},{8,200... | collective-permute-start | bytes 3145736 | tf_op jit(solution)/shard_map/ppermute | solution.py:41
  54.0 14.9 %collective-permute-start.19 = (bf16[1024,512]{1,0:T(8,128)(2,1)S(1)}, bf16[1024,512]{1,0:T(8,128)(2,1)S(1)}, u32[]{:S(2)}, u32[]{:S(2)}) collective-permute-start(bf16[1024,512]{1,0:T(8,128)(2,1)S(1)} %slice.32), channel_id=1, source_target_pairs={{0,64},{1,17},{2,66},{3,19},{4,68},{5,21},{6,70},{7,23},{8,72},{9,... | collective-permute-start | bytes 3145736 | tf_op jit(solution)/shard_map/ppermute | solution.py:41
  54.1 6.8 %collective-permute-start.11 = (bf16[512,512]{1,0:T(8,128)(2,1)S(1)}, bf16[512,512]{1,0:T(8,128)(2,1)S(1)}, u32[]{:S(2)}, u32[]{:S(2)}) collective-permute-start(bf16[512,512]{1,0:T(8,128)(2,1)S(1)} %collective-permute-done.refs_1_), channel_id=1, source_target_pairs={{0,1},{1,0},{2,3},{3,2},{4,5},{5,4},{6,7},{7,6},{8,9},{9,8},{10,11... | collective-permute-start | bytes 1572872 | tf_op jit(solution)/shard_map/ppermute | solution.py:41
  54.2 10.7 %collective-permute-start.6 = (bf16[512,512]{1,0:T(8,128)(2,1)S(1)}, bf16[512,512]{1,0:T(8,128)(2,1)S(1)}, u32[]{:S(2)}, u32[]{:S(2)}) collective-permute-start(bf16[512,512]{1,0:T(8,128)(2,1)S(1)} %collective-permute-done.5.refs_3_), channel_id=1, source_target_pairs={{0,2},{1,15},{2,4},{3,1},{4,6},{5,3},{6,8},{7,5},{8,10},{9,7},{10,... | collective-permute-start | bytes 1572872 | tf_op jit(solution)/shard_map/ppermute | solution.py:41
  59.2 7.3 %collective-permute-start.17 = (bf16[512,512]{1,0:T(8,128)(2,1)S(1)}, bf16[512,512]{1,0:T(8,128)(2,1)S(1)}, u32[]{:S(2)}, u32[]{:S(2)}) collective-permute-start(bf16[512,512]{1,0:T(8,128)(2,1)S(1)} %collective-permute-done.10.refs_8_), channel_id=1, source_target_pairs={{0,1},{1,0},{2,3},{3,2},{4,5},{5,4},{6,7},{7,6},{8,9},{9,8},{10,11... | collective-permute-start | bytes 1572872 | tf_op jit(solution)/shard_map/ppermute | solution.py:41
  60.9 8.3 %collective-permute-start.15 = (bf16[512,512]{1,0:T(8,128)(2,1)S(1)}, bf16[512,512]{1,0:T(8,128)(2,1)S(1)}, u32[]{:S(2)}, u32[]{:S(2)}) collective-permute-start(bf16[512,512]{1,0:T(8,128)(2,1)S(1)} %collective-permute-done.8.refs_6_), channel_id=1, source_target_pairs={{0,1},{1,0},{2,3},{3,2},{4,5},{5,4},{6,7},{7,6},{8,9},{9,8},{10,11... | collective-permute-start | bytes 1572872 | tf_op jit(solution)/shard_map/ppermute | solution.py:41
  64.8 4.4 %collective-permute-start.12 = (bf16[512,512]{1,0:T(8,128)(2,1)S(1)}, bf16[512,512]{1,0:T(8,128)(2,1)S(1)}, u32[]{:S(2)}, u32[]{:S(2)}) collective-permute-start(bf16[512,512]{1,0:T(8,128)(2,1)S(1)} %collective-permute-done.4.refs_2_), channel_id=1, source_target_pairs={{0,1},{1,0},{2,3},{3,2},{4,5},{5,4},{6,7},{7,6},{8,9},{9,8},{10,11... | collective-permute-start | bytes 1572872 | tf_op jit(solution)/shard_map/ppermute | solution.py:41
  66.5 2.7 %collective-permute-start.16 = (bf16[512,512]{1,0:T(8,128)(2,1)S(1)}, bf16[512,512]{1,0:T(8,128)(2,1)S(1)}, u32[]{:S(2)}, u32[]{:S(2)}) collective-permute-start(bf16[512,512]{1,0:T(8,128)(2,1)S(1)} %collective-permute-done.9.refs_7_), channel_id=1, source_target_pairs={{0,1},{1,0},{2,3},{3,2},{4,5},{5,4},{6,7},{7,6},{8,9},{9,8},{10,11... | collective-permute-start | bytes 1572872 | tf_op jit(solution)/shard_map/ppermute | solution.py:41
  66.5 3.0 %collective-permute-start.13 = (bf16[512,512]{1,0:T(8,128)(2,1)S(1)}, bf16[512,512]{1,0:T(8,128)(2,1)S(1)}, u32[]{:S(2)}, u32[]{:S(2)}) collective-permute-start(bf16[512,512]{1,0:T(8,128)(2,1)S(1)} %collective-permute-done.5.refs_3_), channel_id=1, source_target_pairs={{0,1},{1,0},{2,3},{3,2},{4,5},{5,4},{6,7},{7,6},{8,9},{9,8},{10,11... | collective-permute-start | bytes 1572872 | tf_op jit(solution)/shard_map/ppermute | solution.py:41
  68.9 1.9 %collective-permute-start.14 = (bf16[512,512]{1,0:T(8,128)(2,1)S(1)}, bf16[512,512]{1,0:T(8,128)(2,1)S(1)}, u32[]{:S(2)}, u32[]{:S(2)}) collective-permute-start(bf16[512,512]{1,0:T(8,128)(2,1)S(1)} %collective-permute-done.6.refs_4_), channel_id=1, source_target_pairs={{0,1},{1,0},{2,3},{3,2},{4,5},{5,4},{6,7},{7,6},{8,9},{9,8},{10,11... | collective-permute-start | bytes 1572872 | tf_op jit(solution)/shard_map/ppermute | solution.py:41
  77.3 9.9 %collective-permute-start.22 = (bf16[512,512]{1,0:T(8,128)(2,1)S(1)}, bf16[512,512]{1,0:T(8,128)(2,1)S(1)}, u32[]{:S(2)}, u32[]{:S(2)}) collective-permute-start(bf16[512,512]{1,0:T(8,128)(2,1)S(1)} %finish.2.refs_0_), channel_id=1, source_target_pairs={{0,16},{1,65},{2,18},{3,67},{4,20},{5,69},{6,22},{7,71},{8,24},{9,... | collective-permute-start | bytes 1572872 | tf_op jit(solution)/shard_map/ppermute | solution.py:41
  77.4 12.0 %collective-permute-start.23 = (bf16[512,512]{1,0:T(8,128)(2,1)S(1)}, bf16[512,512]{1,0:T(8,128)(2,1)S(1)}, u32[]{:S(2)}, u32[]{:S(2)}) collective-permute-start(bf16[512,512]{1,0:T(8,128)(2,1)S(1)} %finish.2.refs_0_), channel_id=1, source_target_pairs={{0,48},{1,193},{2,50},{3,195},{4,52},{5,197},{6,54},{7,199},{8,56}... | collective-permute-start | bytes 1572872 | tf_op jit(solution)/shard_map/ppermute | solution.py:41
  87.3 16.8 %collective-permute-start.27 = (bf16[1024,512]{1,0:T(8,128)(2,1)S(1)}, bf16[1024,512]{1,0:T(8,128)(2,1)S(1)}, u32[]{:S(2)}, u32[]{:S(2)}) collective-permute-start(bf16[1024,512]{1,0:T(8,128)(2,1)S(1)} %join.4.refs_0_), channel_id=1, source_target_pairs={{0,192},{1,49},{2,194},{3,51},{4,196},{5,53},{6,198},{7,55},{8,200... | collective-permute-start | bytes 3145736 | tf_op jit(solution)/shard_map/ppermute | solution.py:41
  89.4 18.0 %collective-permute-start.26 = (bf16[1024,512]{1,0:T(8,128)(2,1)S(1)}, bf16[1024,512]{1,0:T(8,128)(2,1)S(1)}, u32[]{:S(2)}, u32[]{:S(2)}) collective-permute-start(bf16[1024,512]{1,0:T(8,128)(2,1)S(1)} %join.4.refs_0_), channel_id=1, source_target_pairs={{0,64},{1,17},{2,66},{3,19},{4,68},{5,21},{6,70},{7,23},{8,72},{9,... | collective-permute-start | bytes 3145736 | tf_op jit(solution)/shard_map/ppermute | solution.py:41
  89.4 8.4 %collective-permute-start.25 = (bf16[256,512]{1,0:T(8,128)(2,1)S(1)}, bf16[256,512]{1,0:T(8,128)(2,1)S(1)}, u32[]{:S(2)}, u32[]{:S(2)}) collective-permute-start(bf16[256,512]{1,0:T(8,128)(2,1)S(1)} %slice.35), channel_id=1, source_target_pairs={{0,48},{1,193},{2,50},{3,195},{4,52},{5,197},{6,54},{7,199},{8,56}... | collective-permute-start | bytes 786440 | tf_op jit(solution)/shard_map/ppermute | solution.py:41
  90.8 8.7 %collective-permute-start.24 = (bf16[256,512]{1,0:T(8,128)(2,1)S(1)}, bf16[256,512]{1,0:T(8,128)(2,1)S(1)}, u32[]{:S(2)}, u32[]{:S(2)}) collective-permute-start(bf16[256,512]{1,0:T(8,128)(2,1)S(1)} %slice.34), channel_id=1, source_target_pairs={{0,16},{1,65},{2,18},{3,67},{4,20},{5,69},{6,22},{7,71},{8,24},{9,... | collective-permute-start | bytes 786440 | tf_op jit(solution)/shard_map/ppermute | solution.py:41
  99.6 15.8 %collective-permute-start.29 = (bf16[1024,512]{1,0:T(8,128)(2,1)S(1)}, bf16[1024,512]{1,0:T(8,128)(2,1)S(1)}, u32[]{:S(2)}, u32[]{:S(2)}) collective-permute-start(bf16[1024,512]{1,0:T(8,128)(2,1)S(1)} %join.5.refs_1_), channel_id=1, source_target_pairs={{0,192},{1,49},{2,194},{3,51},{4,196},{5,53},{6,198},{7,55},{8,200... | collective-permute-start | bytes 3145736 | tf_op jit(solution)/shard_map/ppermute | solution.py:41
  103.2 15.4 %collective-permute-start.28 = (bf16[1024,512]{1,0:T(8,128)(2,1)S(1)}, bf16[1024,512]{1,0:T(8,128)(2,1)S(1)}, u32[]{:S(2)}, u32[]{:S(2)}) collective-permute-start(bf16[1024,512]{1,0:T(8,128)(2,1)S(1)} %join.5.refs_1_), channel_id=1, source_target_pairs={{0,64},{1,17},{2,66},{3,19},{4,68},{5,21},{6,70},{7,23},{8,72},{9,... | collective-permute-start | bytes 3145736 | tf_op jit(solution)/shard_map/ppermute | solution.py:41
  107.4 13.5 %collective-permute-start.31 = (bf16[512,512]{1,0:T(8,128)(2,1)S(1)}, bf16[512,512]{1,0:T(8,128)(2,1)S(1)}, u32[]{:S(2)}, u32[]{:S(2)}) collective-permute-start(bf16[512,512]{1,0:T(8,128)(2,1)S(1)} %slice.29), channel_id=1, source_target_pairs={{0,192},{1,49},{2,194},{3,51},{4,196},{5,53},{6,198},{7,55},{8,200... | collective-permute-start | bytes 1572872 | tf_op jit(solution)/shard_map/ppermute | solution.py:41
  107.5 16.7 %collective-permute-start.30 = (bf16[512,512]{1,0:T(8,128)(2,1)S(1)}, bf16[512,512]{1,0:T(8,128)(2,1)S(1)}, u32[]{:S(2)}, u32[]{:S(2)}) collective-permute-start(bf16[512,512]{1,0:T(8,128)(2,1)S(1)} %slice.28), channel_id=1, source_target_pairs={{0,64},{1,17},{2,66},{3,19},{4,68},{5,21},{6,70},{7,23},{8,72},{9,... | collective-permute-start | bytes 1572872 | tf_op jit(solution)/shard_map/ppermute | solution.py:41
  118.7 9.5 %collective-permute-start.33 = (bf16[512,512]{1,0:T(8,128)(2,1)S(1)}, bf16[512,512]{1,0:T(8,128)(2,1)S(1)}, u32[]{:S(2)}, u32[]{:S(2)}) collective-permute-start(bf16[512,512]{1,0:T(8,128)(2,1)S(1)} %slice.31), channel_id=1, source_target_pairs={{0,192},{1,49},{2,194},{3,51},{4,196},{5,53},{6,198},{7,55},{8,200... | collective-permute-start | bytes 1572872 | tf_op jit(solution)/shard_map/ppermute | solution.py:41
  118.8 11.1 %collective-permute-start.32 = (bf16[512,512]{1,0:T(8,128)(2,1)S(1)}, bf16[512,512]{1,0:T(8,128)(2,1)S(1)}, u32[]{:S(2)}, u32[]{:S(2)}) collective-permute-start(bf16[512,512]{1,0:T(8,128)(2,1)S(1)} %slice.30), channel_id=1, source_target_pairs={{0,64},{1,17},{2,66},{3,19},{4,68},{5,21},{6,70},{7,23},{8,72},{9,... | collective-permute-start | bytes 1572872 | tf_op jit(solution)/shard_map/ppermute | solution.py:41

commit v3 on v2

--- a/solution.py
+++ b/solution.py
@@ -122,7 +122,7 @@
     return pl.pallas_call(
         functools.partial(begin_kernel, places), in_specs=[VMEM] * (1 + len(rights)), out_specs=VMEM,
         out_shape=jax.ShapeDtypeStruct((panel.shape[1], rights[0].shape[1]), F32),
-        compiler_params=LARGE, cost_estimate=cost(6, panel, rights[0]), name="begin",
+        compiler_params=LARGE, cost_estimate=cost(0, panel, rights[0]), name="begin",
     )(panel, *rights)
 
 
@@ -195,7 +195,7 @@
     f2 = send(masked, first_axis(2))
     own.append(send(own[0], RING))
     other.append(send(other[0], RING))
-    own[1], f1, f3, f2 = together(own[1], f1, f3, f2)
+    own[1], other[1], f1, f3, f2 = together(own[1], other[1], f1, f3, f2)
     full = join(masked, f1, f3, f2)
     full1, full3 = around(full, second_axis)
     for _ in range(2):
@@ -204,9 +204,9 @@
     own.append(send(own[-1], RING))
     late = opposite(full1, full3, second_axis)
     swapped = [send(a, SWAP) for a in own[1:] + other[1:]]
-    swapped[-1], *late = together(swapped[-1], *late)
     panel = arrange(where, own + other + swapped)
     begun = begin(panel, [full, full1, full3], [(0, 0), (2, 0), (6, 0)])
+    begun, *late = together(begun, *late)
     middle = finish(where, panel, begun, late, [(4, 0), (5, 0)], keep, True)
     early, places, late, late_places = gather(middle)
     return finish(where, panel, begin(panel, early, places), late, late_places, keep, False)

time: 133 us -> 126 us (0.947)
  starting transfers between devices: 54.4 us -> 48 us
    ppermute x34, starting transfers between devices: 54.4 us -> 48 us  [send(): return lax.ppermute(block, AXES, pairs)]
  transfers between devices with their start and end apart: 34 -> 34, of which waited for: 21 -> 15; matrix products, arithmetic and copies ran while one was open for 0% -> 0% of each run, Pallas kernels for 3% -> 7%
where the time goes in v3:
time: 126 us; the launch traced here: 125 us
  waiting for transfers between devices  61.5 us (49%)
  starting transfers between devices  48 us (38%)
  Pallas kernels  13.1 us (10%)
  local copies, waits for them, and re-layouts  2.15 us (2%)
    ppermute x34, waiting for transfers between devices, send(): return lax.ppermute(block, AXES, pairs)  61.5 us
    ppermute x34, starting transfers between devices, send(): return lax.ppermute(block, AXES, pairs)  48 us
    pallas_call x2, Pallas kernels, begin(): pl.pallas_call(functools.partial(begin_kernel, places), in_specs=[VMEM] *...  7.34 us
    pallas_call x2, Pallas kernels, finish(): pl.pallas_call(functools.partial(finish_kernel, middle, places), in_specs...  3.94 us
  transfers between devices with their start and end apart: 34, of which 15 were waited for; matrix products, arithmetic and copies ran while one was open for 0% of the time, Pallas kernels for 7%

profile of v3, /device:TPU:1, one launch (start us, length us, event | category | flops | bytes accessed | tf_op | source)
XLA Modules:
  0.0 125.0 jit_solution(7846989867225745191)
XLA Ops:
  0.0 0.1 stack.135.where_ref
  0.1 0.0 copy-start
  0.1 1.0 copy-done
  1.2 0.7 copy-done.1
  1.8 0.4 mask.1
  2.2 3.3 %collective-permute-start.1 = (bf16[512,512]{1,0:T(8,128)(2,1)S(1)}, bf16[512,512]{1,0:T(8,128)(2,1)S(1)}, u32[]{:S(2)}, u32[]{:S(2)}) collective-permute-start(bf16[512,512]{1,0:T(8,128)(2,1)S(1)} %get-tuple-element.23.refs_0_), channel_id=1, source_target_pairs={{0,1},{1,0},{2,3},{3,2},{4,5},{5,4},{6,7},{7,6},{8,9},{9,8},{10,11... | collective-permute-start | bytes 1572872 | tf_op jit(solution)/shard_map/ppermute | solution.py:41
  5.6 3.8 %collective-permute-start = (bf16[512,512]{1,0:T(8,128)(2,1)S(1)}, bf16[512,512]{1,0:T(8,128)(2,1)S(1)}, u32[]{:S(2)}, u32[]{:S(2)}) collective-permute-start(bf16[512,512]{1,0:T(8,128)(2,1)S(1)} %get-tuple-element.23.refs_0_), channel_id=1, source_target_pairs={{0,2},{1,15},{2,4},{3,1},{4,6},{5,3},{6,8},{7,5},{8,10},{9,7},{10,... | collective-permute-start | bytes 1572872 | tf_op jit(solution)/shard_map/ppermute | solution.py:41
  9.4 1.3 %collective-permute-start.3 = (bf16[512,512]{1,0:T(8,128)(2,1)S(1)}, bf16[512,512]{1,0:T(8,128)(2,1)S(1)}, u32[]{:S(2)}, u32[]{:S(2)}) collective-permute-start(bf16[512,512]{1,0:T(8,128)(2,1)S(1)} %get-tuple-element.23.refs_0_), channel_id=1, source_target_pairs={{0,16},{1,65},{2,18},{3,67},{4,20},{5,69},{6,22},{7,71},{8,24},{9,... | collective-permute-start | bytes 1572872 | tf_op jit(solution)/shard_map/ppermute | solution.py:41
  10.7 1.4 %collective-permute-start.4 = (bf16[512,512]{1,0:T(8,128)(2,1)S(1)}, bf16[512,512]{1,0:T(8,128)(2,1)S(1)}, u32[]{:S(2)}, u32[]{:S(2)}) collective-permute-start(bf16[512,512]{1,0:T(8,128)(2,1)S(1)} %get-tuple-element.23.refs_0_), channel_id=1, source_target_pairs={{0,48},{1,193},{2,50},{3,195},{4,52},{5,197},{6,54},{7,199},{8,56}... | collective-permute-start | bytes 1572872 | tf_op jit(solution)/shard_map/ppermute | solution.py:41
  12.1 1.6 %collective-permute-start.5 = (bf16[512,512]{1,0:T(8,128)(2,1)S(1)}, bf16[512,512]{1,0:T(8,128)(2,1)S(1)}, u32[]{:S(2)}, u32[]{:S(2)}) collective-permute-start(bf16[512,512]{1,0:T(8,128)(2,1)S(1)} %get-tuple-element.23.refs_0_), channel_id=1, source_target_pairs={{0,32},{1,129},{2,34},{3,131},{4,36},{5,133},{6,38},{7,135},{8,40}... | collective-permute-start | bytes 1572872 | tf_op jit(solution)/shard_map/ppermute | solution.py:41
  13.8 0.7 collective-permute-start.2
  14.5 1.0 collective-permute-done.refs_1_
  15.5 3.5 %collective-permute-done.3.refs_1_ = bf16[512,512]{1,0:T(8,128)(2,1)S(1)} collective-permute-done((bf16[512,512]{1,0:T(8,128)(2,1)S(1)}, bf16[512,512]{1,0:T(8,128)(2,1)S(1)}, u32[]{:S(2)}, u32[]{:S(2)}) %collective-permute-start.3) | collective-permute-done | bytes 524320 | tf_op jit(solution)/shard_map/ppermute | solution.py:41
  19.0 0.0 collective-permute-done.4.refs_2_
  19.0 6.5 %collective-permute-done.5.refs_3_ = bf16[512,512]{1,0:T(8,128)(2,1)S(1)} collective-permute-done((bf16[512,512]{1,0:T(8,128)(2,1)S(1)}, bf16[512,512]{1,0:T(8,128)(2,1)S(1)}, u32[]{:S(2)}, u32[]{:S(2)}) %collective-permute-start.5) | collective-permute-done | bytes 524320 | tf_op jit(solution)/shard_map/ppermute | solution.py:41
  25.5 0.0 collective-permute-done.2.refs_6_
  25.5 0.1 join.3.refs_0_
  25.7 1.3 %collective-permute-start.18 = (bf16[2048,512]{1,0:T(8,128)(2,1)S(1)}, bf16[2048,512]{1,0:T(8,128)(2,1)S(1)}, u32[]{:S(2)}, u32[]{:S(2)}) collective-permute-start(bf16[2048,512]{1,0:T(8,128)(2,1)S(1)} %join.3.refs_0_), channel_id=1, source_target_pairs={{0,64},{1,17},{2,66},{3,19},{4,68},{5,21},{6,70},{7,23},{8,72},{9,... | collective-permute-start | bytes 6291464 | tf_op jit(solution)/shard_map/ppermute | solution.py:41
  26.9 1.5 %collective-permute-start.19 = (bf16[2048,512]{1,0:T(8,128)(2,1)S(1)}, bf16[2048,512]{1,0:T(8,128)(2,1)S(1)}, u32[]{:S(2)}, u32[]{:S(2)}) collective-permute-start(bf16[2048,512]{1,0:T(8,128)(2,1)S(1)} %join.3.refs_0_), channel_id=1, source_target_pairs={{0,192},{1,49},{2,194},{3,51},{4,196},{5,53},{6,198},{7,55},{8,200... | collective-permute-start | bytes 6291464 | tf_op jit(solution)/shard_map/ppermute | solution.py:41
  28.4 0.7 collective-permute-start.6
  29.1 1.0 collective-permute-start.9
  30.2 6.6 %collective-permute-done.6.refs_2_ = bf16[512,512]{1,0:T(8,128)(2,1)S(1)} collective-permute-done((bf16[512,512]{1,0:T(8,128)(2,1)S(1)}, bf16[512,512]{1,0:T(8,128)(2,1)S(1)}, u32[]{:S(2)}, u32[]{:S(2)}) %collective-permute-start.6) | collective-permute-done | bytes 524320 | tf_op jit(solution)/shard_map/ppermute | solution.py:41
  36.7 1.9 %collective-permute-start.7 = (bf16[512,512]{1,0:T(8,128)(2,1)S(1)}, bf16[512,512]{1,0:T(8,128)(2,1)S(1)}, u32[]{:S(2)}, u32[]{:S(2)}) collective-permute-start(bf16[512,512]{1,0:T(8,128)(2,1)S(1)} %collective-permute-done.6.refs_2_), channel_id=1, source_target_pairs={{0,2},{1,15},{2,4},{3,1},{4,6},{5,3},{6,8},{7,5},{8,10},{9,7},{10,... | collective-permute-start | bytes 1572872 | tf_op jit(solution)/shard_map/ppermute | solution.py:41
  38.7 3.7 %collective-permute-done.9.refs_7_ = bf16[512,512]{1,0:T(8,128)(2,1)S(1)} collective-permute-done((bf16[512,512]{1,0:T(8,128)(2,1)S(1)}, bf16[512,512]{1,0:T(8,128)(2,1)S(1)}, u32[]{:S(2)}, u32[]{:S(2)}) %collective-permute-start.9) | collective-permute-done | bytes 524320 | tf_op jit(solution)/shard_map/ppermute | solution.py:41
  42.4 0.7 collective-permute-start.15
  43.1 0.0 collective-permute-done.11.refs_9_
  43.1 1.7 %collective-permute-start.10 = (bf16[512,512]{1,0:T(8,128)(2,1)S(1)}, bf16[512,512]{1,0:T(8,128)(2,1)S(1)}, u32[]{:S(2)}, u32[]{:S(2)}) collective-permute-start(bf16[512,512]{1,0:T(8,128)(2,1)S(1)} %collective-permute-done.9.refs_7_), channel_id=1, source_target_pairs={{0,2},{1,15},{2,4},{3,1},{4,6},{5,3},{6,8},{7,5},{8,10},{9,7},{10,... | collective-permute-start | bytes 1572872 | tf_op jit(solution)/shard_map/ppermute | solution.py:41
  44.8 3.1 %collective-permute-done.7.refs_3_ = bf16[512,512]{1,0:T(8,128)(2,1)S(1)} collective-permute-done((bf16[512,512]{1,0:T(8,128)(2,1)S(1)}, bf16[512,512]{1,0:T(8,128)(2,1)S(1)}, u32[]{:S(2)}, u32[]{:S(2)}) %collective-permute-start.7) | collective-permute-done | bytes 524320 | tf_op jit(solution)/shard_map/ppermute | solution.py:41
  48.0 0.7 collective-permute-start.12
  48.7 3.4 %collective-permute-done.18.refs_1_ = bf16[2048,512]{1,0:T(8,128)(2,1)S(1)} collective-permute-done((bf16[2048,512]{1,0:T(8,128)(2,1)S(1)}, bf16[2048,512]{1,0:T(8,128)(2,1)S(1)}, u32[]{:S(2)}, u32[]{:S(2)}) %collective-permute-start.18) | collective-permute-done | bytes 2097184 | tf_op jit(solution)/shard_map/ppermute | solution.py:41
  52.1 1.9 %collective-permute-start.8 = (bf16[512,512]{1,0:T(8,128)(2,1)S(1)}, bf16[512,512]{1,0:T(8,128)(2,1)S(1)}, u32[]{:S(2)}, u32[]{:S(2)}) collective-permute-start(bf16[512,512]{1,0:T(8,128)(2,1)S(1)} %collective-permute-done.7.refs_3_), channel_id=1, source_target_pairs={{0,2},{1,15},{2,4},{3,1},{4,6},{5,3},{6,8},{7,5},{8,10},{9,7},{10,... | collective-permute-start | bytes 1572872 | tf_op jit(solution)/shard_map/ppermute | solution.py:41
  54.1 0.1 slice.32
  54.1 0.1 slice.33
  54.2 1.2 collective-permute-start.20
  55.4 1.5 %collective-permute-start.21 = (bf16[1024,512]{1,0:T(8,128)(2,1)S(1)}, bf16[1024,512]{1,0:T(8,128)(2,1)S(1)}, u32[]{:S(2)}, u32[]{:S(2)}) collective-permute-start(bf16[1024,512]{1,0:T(8,128)(2,1)S(1)} %slice.33), channel_id=1, source_target_pairs={{0,192},{1,49},{2,194},{3,51},{4,196},{5,53},{6,198},{7,55},{8,200... | collective-permute-start | bytes 3145736 | tf_op jit(solution)/shard_map/ppermute | solution.py:41
  57.0 0.5 collective-permute-start.17
  57.5 3.0 %collective-permute-done.8.refs_4_ = bf16[512,512]{1,0:T(8,128)(2,1)S(1)} collective-permute-done((bf16[512,512]{1,0:T(8,128)(2,1)S(1)}, bf16[512,512]{1,0:T(8,128)(2,1)S(1)}, u32[]{:S(2)}, u32[]{:S(2)}) %collective-permute-start.8) | collective-permute-done | bytes 524320 | tf_op jit(solution)/shard_map/ppermute | solution.py:41
  60.5 2.6 %collective-permute-start.14 = (bf16[512,512]{1,0:T(8,128)(2,1)S(1)}, bf16[512,512]{1,0:T(8,128)(2,1)S(1)}, u32[]{:S(2)}, u32[]{:S(2)}) collective-permute-start(bf16[512,512]{1,0:T(8,128)(2,1)S(1)} %collective-permute-done.8.refs_4_), channel_id=1, source_target_pairs={{0,1},{1,0},{2,3},{3,2},{4,5},{5,4},{6,7},{7,6},{8,9},{9,8},{10,11... | collective-permute-start | bytes 1572872 | tf_op jit(solution)/shard_map/ppermute | solution.py:41
  63.0 1.5 %collective-permute-done.14.refs_12_ = bf16[512,512]{1,0:T(8,128)(2,1)S(1)} collective-permute-done((bf16[512,512]{1,0:T(8,128)(2,1)S(1)}, bf16[512,512]{1,0:T(8,128)(2,1)S(1)}, u32[]{:S(2)}, u32[]{:S(2)}) %collective-permute-start.14) | collective-permute-done | bytes 524320 | tf_op jit(solution)/shard_map/ppermute | solution.py:41
  64.6 1.2 arrange.1.panel_ref
  65.8 3.4 %begin.2.sum_ref = f32[512,512]{1,0:T(8,128)S(1)} custom-call(bf16[8,512,1024]{2,1,0:T(8,128)(2,1)S(1)} %arrange.1.panel_ref, bf16[2048,512]{1,0:T(8,128)(2,1)S(1)} %join.3.refs_0_, bf16[2048,512]{1,0:T(8,128)(2,1)S(1)} %collective-permute-done.18.refs_1_, bf16[2048,512]{1,0:T(8,128)(2,1)S(1)} %collective-permute-done.19.refs_2_), custom_call_target="tpu_custom_call" | custom-call | tf_op jit(solution)/shard_map/begin/pallas_call | solution.py:122
  69.2 1.9 %finish.2.refs_0_ = bf16[512,512]{1,0:T(8,128)(2,1)S(1)} custom-call(s32[33]{0:T(128)S(1)} %stack.135.where_ref, bf16[8,512,1024]{2,1,0:T(8,128)(2,1)S(1)} %arrange.1.panel_ref, f32[512,512]{1,0:T(8,128)S(1)} %begin.2.sum_ref, bf16[1024,512]{1,0:T(8,128)(2,1)S(1)} %collective-permute-done.20.refs_0_, bf16[1024,512]{1,0:T(8,128)(2,1)S(1)} %collective-permute-done.21.refs_1_, ...), custom_call_target="tpu_custom_call" | custom-call | flops 1073741824 | bytes 4194304 | tf_op jit(solution)/shard_map/finish/pallas_call | solution.py:141
  71.1 0.9 collective-permute-start.22
  72.0 1.8 %collective-permute-start.23 = (bf16[512,512]{1,0:T(8,128)(2,1)S(1)}, bf16[512,512]{1,0:T(8,128)(2,1)S(1)}, u32[]{:S(2)}, u32[]{:S(2)}) collective-permute-start(bf16[512,512]{1,0:T(8,128)(2,1)S(1)} %finish.2.refs_0_), channel_id=1, source_target_pairs={{0,48},{1,193},{2,50},{3,195},{4,52},{5,197},{6,54},{7,199},{8,56}... | collective-permute-start | bytes 1572872 | tf_op jit(solution)/shard_map/ppermute | solution.py:41
  73.9 6.9 %collective-permute-done.22.refs_1_ = bf16[512,512]{1,0:T(8,128)(2,1)S(1)} collective-permute-done((bf16[512,512]{1,0:T(8,128)(2,1)S(1)}, bf16[512,512]{1,0:T(8,128)(2,1)S(1)}, u32[]{:S(2)}, u32[]{:S(2)}) %collective-permute-start.22) | collective-permute-done | bytes 524320 | tf_op jit(solution)/shard_map/ppermute | solution.py:41
  80.7 0.1 collective-permute-start.24
  80.9 2.7 %collective-permute-start.25 = (bf16[256,512]{1,0:T(8,128)(2,1)S(1)}, bf16[256,512]{1,0:T(8,128)(2,1)S(1)}, u32[]{:S(2)}, u32[]{:S(2)}) collective-permute-start(bf16[256,512]{1,0:T(8,128)(2,1)S(1)} %slice.35), channel_id=1, source_target_pairs={{0,48},{1,193},{2,50},{3,195},{4,52},{5,197},{6,54},{7,199},{8,56}... | collective-permute-start | bytes 786440 | tf_op jit(solution)/shard_map/ppermute | solution.py:41
  83.6 0.1 join.4.refs_0_
  83.7 0.2 collective-permute-start.26
  83.9 2.6 %collective-permute-start.27 = (bf16[1024,512]{1,0:T(8,128)(2,1)S(1)}, bf16[1024,512]{1,0:T(8,128)(2,1)S(1)}, u32[]{:S(2)}, u32[]{:S(2)}) collective-permute-start(bf16[1024,512]{1,0:T(8,128)(2,1)S(1)} %join.4.refs_0_), channel_id=1, source_target_pairs={{0,192},{1,49},{2,194},{3,51},{4,196},{5,53},{6,198},{7,55},{8,200... | collective-permute-start | bytes 3145736 | tf_op jit(solution)/shard_map/ppermute | solution.py:41
  86.5 1.1 collective-permute-done.24.refs_1_
  87.6 0.1 join.5.refs_1_
  87.6 0.1 collective-permute-start.28
  87.7 3.4 %collective-permute-start.29 = (bf16[1024,512]{1,0:T(8,128)(2,1)S(1)}, bf16[1024,512]{1,0:T(8,128)(2,1)S(1)}, u32[]{:S(2)}, u32[]{:S(2)}) collective-permute-start(bf16[1024,512]{1,0:T(8,128)(2,1)S(1)} %join.5.refs_1_), channel_id=1, source_target_pairs={{0,192},{1,49},{2,194},{3,51},{4,196},{5,53},{6,198},{7,55},{8,200... | collective-permute-start | bytes 3145736 | tf_op jit(solution)/shard_map/ppermute | solution.py:41
  91.1 9.3 %collective-permute-done.26.refs_2_ = bf16[1024,512]{1,0:T(8,128)(2,1)S(1)} collective-permute-done((bf16[1024,512]{1,0:T(8,128)(2,1)S(1)}, bf16[1024,512]{1,0:T(8,128)(2,1)S(1)}, u32[]{:S(2)}, u32[]{:S(2)}) %collective-permute-start.26) | collective-permute-done | bytes 1048608 | tf_op jit(solution)/shard_map/ppermute | solution.py:41
  100.5 0.1 collective-permute-start.30
  100.6 3.1 %collective-permute-start.31 = (bf16[512,512]{1,0:T(8,128)(2,1)S(1)}, bf16[512,512]{1,0:T(8,128)(2,1)S(1)}, u32[]{:S(2)}, u32[]{:S(2)}) collective-permute-start(bf16[512,512]{1,0:T(8,128)(2,1)S(1)} %slice.29), channel_id=1, source_target_pairs={{0,192},{1,49},{2,194},{3,51},{4,196},{5,53},{6,198},{7,55},{8,200... | collective-permute-start | bytes 1572872 | tf_op jit(solution)/shard_map/ppermute | solution.py:41
  103.8 7.9 %collective-permute-done.28.refs_3_ = bf16[1024,512]{1,0:T(8,128)(2,1)S(1)} collective-permute-done((bf16[1024,512]{1,0:T(8,128)(2,1)S(1)}, bf16[1024,512]{1,0:T(8,128)(2,1)S(1)}, u32[]{:S(2)}, u32[]{:S(2)}) %collective-permute-start.28) | collective-permute-done | bytes 1048608 | tf_op jit(solution)/shard_map/ppermute | solution.py:41
  111.7 0.1 collective-permute-start.32
  111.9 3.1 %collective-permute-start.33 = (bf16[512,512]{1,0:T(8,128)(2,1)S(1)}, bf16[512,512]{1,0:T(8,128)(2,1)S(1)}, u32[]{:S(2)}, u32[]{:S(2)}) collective-permute-start(bf16[512,512]{1,0:T(8,128)(2,1)S(1)} %slice.31), channel_id=1, source_target_pairs={{0,192},{1,49},{2,194},{3,51},{4,196},{5,53},{6,198},{7,55},{8,200... | collective-permute-start | bytes 1572872 | tf_op jit(solution)/shard_map/ppermute | solution.py:41
  115.0 2.3 %collective-permute-done.30.refs_6_ = bf16[512,512]{1,0:T(8,128)(2,1)S(1)} collective-permute-done((bf16[512,512]{1,0:T(8,128)(2,1)S(1)}, bf16[512,512]{1,0:T(8,128)(2,1)S(1)}, u32[]{:S(2)}, u32[]{:S(2)}) %collective-permute-start.30) | collective-permute-done | bytes 524320 | tf_op jit(solution)/shard_map/ppermute | solution.py:41
  117.3 3.9 %begin.3.sum_ref = f32[512,512]{1,0:T(8,128)S(1)} custom-call(bf16[8,512,1024]{2,1,0:T(8,128)(2,1)S(1)} %arrange.1.panel_ref, bf16[1024,512]{1,0:T(8,128)(2,1)S(1)} %join.4.refs_0_, bf16[1024,512]{1,0:T(8,128)(2,1)S(1)} %join.5.refs_1_, bf16[1024,512]{1,0:T(8,128)(2,1)S(1)} %collective-permute-done.26.refs_2_, ...), custom_call_target="tpu_custom_call" | custom-call | tf_op jit(solution)/shard_map/begin/pallas_call | solution.py:122
  121.3 1.7 %collective-permute-done.32.refs_0_ = bf16[512,512]{1,0:T(8,128)(2,1)S(1)} collective-permute-done((bf16[512,512]{1,0:T(8,128)(2,1)S(1)}, bf16[512,512]{1,0:T(8,128)(2,1)S(1)}, u32[]{:S(2)}, u32[]{:S(2)}) %collective-permute-start.32) | collective-permute-done | bytes 524320 | tf_op jit(solution)/shard_map/ppermute | solution.py:41
  122.9 2.0 %finish.3 = bf16[512,512]{1,0:T(8,128)(2,1)} custom-call(s32[33]{0:T(128)S(1)} %stack.135.where_ref, bf16[8,512,1024]{2,1,0:T(8,128)(2,1)S(1)} %arrange.1.panel_ref, f32[512,512]{1,0:T(8,128)S(1)} %begin.3.sum_ref, bf16[512,512]{1,0:T(8,128)(2,1)S(1)} %collective-permute-done.32.refs_0_, bf16[512,512]{1,0:T(8,128)(2,1)S(1)} %collective-permute-done.33.refs_1_, ...), custom_call_target="tpu_custom_call" | custom-call | flops 536870912 | bytes 2097152 | tf_op jit(solution)/shard_map/finish/pallas_call | solution.py:141
  (26 shorter events, 0.2 us)
Async XLA Ops:
  0.1 1.0 copy-start
  1.2 0.7 copy-start.1
  2.2 11.6 %collective-permute-start.1 = (bf16[512,512]{1,0:T(8,128)(2,1)S(1)}, bf16[512,512]{1,0:T(8,128)(2,1)S(1)}, u32[]{:S(2)}, u32[]{:S(2)}) collective-permute-start(bf16[512,512]{1,0:T(8,128)(2,1)S(1)} %get-tuple-element.23.refs_0_), channel_id=1, source_target_pairs={{0,1},{1,0},{2,3},{3,2},{4,5},{5,4},{6,7},{7,6},{8,9},{9,8},{10,11... | collective-permute-start | bytes 1572872 | tf_op jit(solution)/shard_map/ppermute | solution.py:41
  5.6 10.0 %collective-permute-start = (bf16[512,512]{1,0:T(8,128)(2,1)S(1)}, bf16[512,512]{1,0:T(8,128)(2,1)S(1)}, u32[]{:S(2)}, u32[]{:S(2)}) collective-permute-start(bf16[512,512]{1,0:T(8,128)(2,1)S(1)} %get-tuple-element.23.refs_0_), channel_id=1, source_target_pairs={{0,2},{1,15},{2,4},{3,1},{4,6},{5,3},{6,8},{7,5},{8,10},{9,7},{10,... | collective-permute-start | bytes 1572872 | tf_op jit(solution)/shard_map/ppermute | solution.py:41
  9.4 9.6 %collective-permute-start.3 = (bf16[512,512]{1,0:T(8,128)(2,1)S(1)}, bf16[512,512]{1,0:T(8,128)(2,1)S(1)}, u32[]{:S(2)}, u32[]{:S(2)}) collective-permute-start(bf16[512,512]{1,0:T(8,128)(2,1)S(1)} %get-tuple-element.23.refs_0_), channel_id=1, source_target_pairs={{0,16},{1,65},{2,18},{3,67},{4,20},{5,69},{6,22},{7,71},{8,24},{9,... | collective-permute-start | bytes 1572872 | tf_op jit(solution)/shard_map/ppermute | solution.py:41
  10.7 8.3 %collective-permute-start.4 = (bf16[512,512]{1,0:T(8,128)(2,1)S(1)}, bf16[512,512]{1,0:T(8,128)(2,1)S(1)}, u32[]{:S(2)}, u32[]{:S(2)}) collective-permute-start(bf16[512,512]{1,0:T(8,128)(2,1)S(1)} %get-tuple-element.23.refs_0_), channel_id=1, source_target_pairs={{0,48},{1,193},{2,50},{3,195},{4,52},{5,197},{6,54},{7,199},{8,56}... | collective-permute-start | bytes 1572872 | tf_op jit(solution)/shard_map/ppermute | solution.py:41
  12.1 13.4 %collective-permute-start.5 = (bf16[512,512]{1,0:T(8,128)(2,1)S(1)}, bf16[512,512]{1,0:T(8,128)(2,1)S(1)}, u32[]{:S(2)}, u32[]{:S(2)}) collective-permute-start(bf16[512,512]{1,0:T(8,128)(2,1)S(1)} %get-tuple-element.23.refs_0_), channel_id=1, source_target_pairs={{0,32},{1,129},{2,34},{3,131},{4,36},{5,133},{6,38},{7,135},{8,40}... | collective-permute-start | bytes 1572872 | tf_op jit(solution)/shard_map/ppermute | solution.py:41
  13.8 11.7 %collective-permute-start.2 = (bf16[512,512]{1,0:T(8,128)(2,1)S(1)}, bf16[512,512]{1,0:T(8,128)(2,1)S(1)}, u32[]{:S(2)}, u32[]{:S(2)}) collective-permute-start(bf16[512,512]{1,0:T(8,128)(2,1)S(1)} %collective-permute-done.1.refs_5_), channel_id=1, source_target_pairs={{0,2},{1,15},{2,4},{3,1},{4,6},{5,3},{6,8},{7,5},{8,10},{9,7},{10,... | collective-permute-start | bytes 1572872 | tf_op jit(solution)/shard_map/ppermute | solution.py:41
  25.7 26.5 %collective-permute-start.18 = (bf16[2048,512]{1,0:T(8,128)(2,1)S(1)}, bf16[2048,512]{1,0:T(8,128)(2,1)S(1)}, u32[]{:S(2)}, u32[]{:S(2)}) collective-permute-start(bf16[2048,512]{1,0:T(8,128)(2,1)S(1)} %join.3.refs_0_), channel_id=1, source_target_pairs={{0,64},{1,17},{2,66},{3,19},{4,68},{5,21},{6,70},{7,23},{8,72},{9,... | collective-permute-start | bytes 6291464 | tf_op jit(solution)/shard_map/ppermute | solution.py:41
  26.9 25.2 %collective-permute-start.19 = (bf16[2048,512]{1,0:T(8,128)(2,1)S(1)}, bf16[2048,512]{1,0:T(8,128)(2,1)S(1)}, u32[]{:S(2)}, u32[]{:S(2)}) collective-permute-start(bf16[2048,512]{1,0:T(8,128)(2,1)S(1)} %join.3.refs_0_), channel_id=1, source_target_pairs={{0,192},{1,49},{2,194},{3,51},{4,196},{5,53},{6,198},{7,55},{8,200... | collective-permute-start | bytes 6291464 | tf_op jit(solution)/shard_map/ppermute | solution.py:41
  28.4 8.3 %collective-permute-start.6 = (bf16[512,512]{1,0:T(8,128)(2,1)S(1)}, bf16[512,512]{1,0:T(8,128)(2,1)S(1)}, u32[]{:S(2)}, u32[]{:S(2)}) collective-permute-start(bf16[512,512]{1,0:T(8,128)(2,1)S(1)} %collective-permute-done.refs_1_), channel_id=1, source_target_pairs={{0,2},{1,15},{2,4},{3,1},{4,6},{5,3},{6,8},{7,5},{8,10},{9,7},{10,... | collective-permute-start | bytes 1572872 | tf_op jit(solution)/shard_map/ppermute | solution.py:41
  29.1 13.2 %collective-permute-start.9 = (bf16[512,512]{1,0:T(8,128)(2,1)S(1)}, bf16[512,512]{1,0:T(8,128)(2,1)S(1)}, u32[]{:S(2)}, u32[]{:S(2)}) collective-permute-start(bf16[512,512]{1,0:T(8,128)(2,1)S(1)} %collective-permute-done.2.refs_6_), channel_id=1, source_target_pairs={{0,2},{1,15},{2,4},{3,1},{4,6},{5,3},{6,8},{7,5},{8,10},{9,7},{10,... | collective-permute-start | bytes 1572872 | tf_op jit(solution)/shard_map/ppermute | solution.py:41
  30.2 12.9 %collective-permute-start.11 = (bf16[512,512]{1,0:T(8,128)(2,1)S(1)}, bf16[512,512]{1,0:T(8,128)(2,1)S(1)}, u32[]{:S(2)}, u32[]{:S(2)}) collective-permute-start(bf16[512,512]{1,0:T(8,128)(2,1)S(1)} %collective-permute-done.refs_1_), channel_id=1, source_target_pairs={{0,1},{1,0},{2,3},{3,2},{4,5},{5,4},{6,7},{7,6},{8,9},{9,8},{10,11... | collective-permute-start | bytes 1572872 | tf_op jit(solution)/shard_map/ppermute | solution.py:41
  36.7 11.2 %collective-permute-start.7 = (bf16[512,512]{1,0:T(8,128)(2,1)S(1)}, bf16[512,512]{1,0:T(8,128)(2,1)S(1)}, u32[]{:S(2)}, u32[]{:S(2)}) collective-permute-start(bf16[512,512]{1,0:T(8,128)(2,1)S(1)} %collective-permute-done.6.refs_2_), channel_id=1, source_target_pairs={{0,2},{1,15},{2,4},{3,1},{4,6},{5,3},{6,8},{7,5},{8,10},{9,7},{10,... | collective-permute-start | bytes 1572872 | tf_op jit(solution)/shard_map/ppermute | solution.py:41
  42.4 11.9 %collective-permute-start.15 = (bf16[512,512]{1,0:T(8,128)(2,1)S(1)}, bf16[512,512]{1,0:T(8,128)(2,1)S(1)}, u32[]{:S(2)}, u32[]{:S(2)}) collective-permute-start(bf16[512,512]{1,0:T(8,128)(2,1)S(1)} %collective-permute-done.2.refs_6_), channel_id=1, source_target_pairs={{0,1},{1,0},{2,3},{3,2},{4,5},{5,4},{6,7},{7,6},{8,9},{9,8},{10,11... | collective-permute-start | bytes 1572872 | tf_op jit(solution)/shard_map/ppermute | solution.py:41
  43.1 12.3 %collective-permute-start.10 = (bf16[512,512]{1,0:T(8,128)(2,1)S(1)}, bf16[512,512]{1,0:T(8,128)(2,1)S(1)}, u32[]{:S(2)}, u32[]{:S(2)}) collective-permute-start(bf16[512,512]{1,0:T(8,128)(2,1)S(1)} %collective-permute-done.9.refs_7_), channel_id=1, source_target_pairs={{0,2},{1,15},{2,4},{3,1},{4,6},{5,3},{6,8},{7,5},{8,10},{9,7},{10,... | collective-permute-start | bytes 1572872 | tf_op jit(solution)/shard_map/ppermute | solution.py:41
  48.0 9.0 %collective-permute-start.12 = (bf16[512,512]{1,0:T(8,128)(2,1)S(1)}, bf16[512,512]{1,0:T(8,128)(2,1)S(1)}, u32[]{:S(2)}, u32[]{:S(2)}) collective-permute-start(bf16[512,512]{1,0:T(8,128)(2,1)S(1)} %collective-permute-done.6.refs_2_), channel_id=1, source_target_pairs={{0,1},{1,0},{2,3},{3,2},{4,5},{5,4},{6,7},{7,6},{8,9},{9,8},{10,11... | collective-permute-start | bytes 1572872 | tf_op jit(solution)/shard_map/ppermute | solution.py:41
  52.1 4.9 %collective-permute-start.16 = (bf16[512,512]{1,0:T(8,128)(2,1)S(1)}, bf16[512,512]{1,0:T(8,128)(2,1)S(1)}, u32[]{:S(2)}, u32[]{:S(2)}) collective-permute-start(bf16[512,512]{1,0:T(8,128)(2,1)S(1)} %collective-permute-done.9.refs_7_), channel_id=1, source_target_pairs={{0,1},{1,0},{2,3},{3,2},{4,5},{5,4},{6,7},{7,6},{8,9},{9,8},{10,11... | collective-permute-start | bytes 1572872 | tf_op jit(solution)/shard_map/ppermute | solution.py:41
  52.1 8.3 %collective-permute-start.8 = (bf16[512,512]{1,0:T(8,128)(2,1)S(1)}, bf16[512,512]{1,0:T(8,128)(2,1)S(1)}, u32[]{:S(2)}, u32[]{:S(2)}) collective-permute-start(bf16[512,512]{1,0:T(8,128)(2,1)S(1)} %collective-permute-done.7.refs_3_), channel_id=1, source_target_pairs={{0,2},{1,15},{2,4},{3,1},{4,6},{5,3},{6,8},{7,5},{8,10},{9,7},{10,... | collective-permute-start | bytes 1572872 | tf_op jit(solution)/shard_map/ppermute | solution.py:41
  54.2 15.0 %collective-permute-start.20 = (bf16[1024,512]{1,0:T(8,128)(2,1)S(1)}, bf16[1024,512]{1,0:T(8,128)(2,1)S(1)}, u32[]{:S(2)}, u32[]{:S(2)}) collective-permute-start(bf16[1024,512]{1,0:T(8,128)(2,1)S(1)} %slice.32), channel_id=1, source_target_pairs={{0,64},{1,17},{2,66},{3,19},{4,68},{5,21},{6,70},{7,23},{8,72},{9,... | collective-permute-start | bytes 3145736 | tf_op jit(solution)/shard_map/ppermute | solution.py:41
  55.4 13.8 %collective-permute-start.21 = (bf16[1024,512]{1,0:T(8,128)(2,1)S(1)}, bf16[1024,512]{1,0:T(8,128)(2,1)S(1)}, u32[]{:S(2)}, u32[]{:S(2)}) collective-permute-start(bf16[1024,512]{1,0:T(8,128)(2,1)S(1)} %slice.33), channel_id=1, source_target_pairs={{0,192},{1,49},{2,194},{3,51},{4,196},{5,53},{6,198},{7,55},{8,200... | collective-permute-start | bytes 3145736 | tf_op jit(solution)/shard_map/ppermute | solution.py:41
  57.0 6.1 %collective-permute-start.13 = (bf16[512,512]{1,0:T(8,128)(2,1)S(1)}, bf16[512,512]{1,0:T(8,128)(2,1)S(1)}, u32[]{:S(2)}, u32[]{:S(2)}) collective-permute-start(bf16[512,512]{1,0:T(8,128)(2,1)S(1)} %collective-permute-done.7.refs_3_), channel_id=1, source_target_pairs={{0,1},{1,0},{2,3},{3,2},{4,5},{5,4},{6,7},{7,6},{8,9},{9,8},{10,11... | collective-permute-start | bytes 1572872 | tf_op jit(solution)/shard_map/ppermute | solution.py:41
  57.0 6.1 %collective-permute-start.17 = (bf16[512,512]{1,0:T(8,128)(2,1)S(1)}, bf16[512,512]{1,0:T(8,128)(2,1)S(1)}, u32[]{:S(2)}, u32[]{:S(2)}) collective-permute-start(bf16[512,512]{1,0:T(8,128)(2,1)S(1)} %collective-permute-done.10.refs_8_), channel_id=1, source_target_pairs={{0,1},{1,0},{2,3},{3,2},{4,5},{5,4},{6,7},{7,6},{8,9},{9,8},{10,11... | collective-permute-start | bytes 1572872 | tf_op jit(solution)/shard_map/ppermute | solution.py:41
  60.5 4.1 %collective-permute-start.14 = (bf16[512,512]{1,0:T(8,128)(2,1)S(1)}, bf16[512,512]{1,0:T(8,128)(2,1)S(1)}, u32[]{:S(2)}, u32[]{:S(2)}) collective-permute-start(bf16[512,512]{1,0:T(8,128)(2,1)S(1)} %collective-permute-done.8.refs_4_), channel_id=1, source_target_pairs={{0,1},{1,0},{2,3},{3,2},{4,5},{5,4},{6,7},{7,6},{8,9},{9,8},{10,11... | collective-permute-start | bytes 1572872 | tf_op jit(solution)/shard_map/ppermute | solution.py:41
  71.1 9.6 %collective-permute-start.22 = (bf16[512,512]{1,0:T(8,128)(2,1)S(1)}, bf16[512,512]{1,0:T(8,128)(2,1)S(1)}, u32[]{:S(2)}, u32[]{:S(2)}) collective-permute-start(bf16[512,512]{1,0:T(8,128)(2,1)S(1)} %finish.2.refs_0_), channel_id=1, source_target_pairs={{0,16},{1,65},{2,18},{3,67},{4,20},{5,69},{6,22},{7,71},{8,24},{9,... | collective-permute-start | bytes 1572872 | tf_op jit(solution)/shard_map/ppermute | solution.py:41
  72.0 8.8 %collective-permute-start.23 = (bf16[512,512]{1,0:T(8,128)(2,1)S(1)}, bf16[512,512]{1,0:T(8,128)(2,1)S(1)}, u32[]{:S(2)}, u32[]{:S(2)}) collective-permute-start(bf16[512,512]{1,0:T(8,128)(2,1)S(1)} %finish.2.refs_0_), channel_id=1, source_target_pairs={{0,48},{1,193},{2,50},{3,195},{4,52},{5,197},{6,54},{7,199},{8,56}... | collective-permute-start | bytes 1572872 | tf_op jit(solution)/shard_map/ppermute | solution.py:41
  80.7 6.8 %collective-permute-start.24 = (bf16[256,512]{1,0:T(8,128)(2,1)S(1)}, bf16[256,512]{1,0:T(8,128)(2,1)S(1)}, u32[]{:S(2)}, u32[]{:S(2)}) collective-permute-start(bf16[256,512]{1,0:T(8,128)(2,1)S(1)} %slice.34), channel_id=1, source_target_pairs={{0,16},{1,65},{2,18},{3,67},{4,20},{5,69},{6,22},{7,71},{8,24},{9,... | collective-permute-start | bytes 786440 | tf_op jit(solution)/shard_map/ppermute | solution.py:41
  80.9 6.7 %collective-permute-start.25 = (bf16[256,512]{1,0:T(8,128)(2,1)S(1)}, bf16[256,512]{1,0:T(8,128)(2,1)S(1)}, u32[]{:S(2)}, u32[]{:S(2)}) collective-permute-start(bf16[256,512]{1,0:T(8,128)(2,1)S(1)} %slice.35), channel_id=1, source_target_pairs={{0,48},{1,193},{2,50},{3,195},{4,52},{5,197},{6,54},{7,199},{8,56}... | collective-permute-start | bytes 786440 | tf_op jit(solution)/shard_map/ppermute | solution.py:41
  83.7 16.8 %collective-permute-start.26 = (bf16[1024,512]{1,0:T(8,128)(2,1)S(1)}, bf16[1024,512]{1,0:T(8,128)(2,1)S(1)}, u32[]{:S(2)}, u32[]{:S(2)}) collective-permute-start(bf16[1024,512]{1,0:T(8,128)(2,1)S(1)} %join.4.refs_0_), channel_id=1, source_target_pairs={{0,64},{1,17},{2,66},{3,19},{4,68},{5,21},{6,70},{7,23},{8,72},{9,... | collective-permute-start | bytes 3145736 | tf_op jit(solution)/shard_map/ppermute | solution.py:41
  83.9 16.6 %collective-permute-start.27 = (bf16[1024,512]{1,0:T(8,128)(2,1)S(1)}, bf16[1024,512]{1,0:T(8,128)(2,1)S(1)}, u32[]{:S(2)}, u32[]{:S(2)}) collective-permute-start(bf16[1024,512]{1,0:T(8,128)(2,1)S(1)} %join.4.refs_0_), channel_id=1, source_target_pairs={{0,192},{1,49},{2,194},{3,51},{4,196},{5,53},{6,198},{7,55},{8,200... | collective-permute-start | bytes 3145736 | tf_op jit(solution)/shard_map/ppermute | solution.py:41
  87.6 24.1 %collective-permute-start.28 = (bf16[1024,512]{1,0:T(8,128)(2,1)S(1)}, bf16[1024,512]{1,0:T(8,128)(2,1)S(1)}, u32[]{:S(2)}, u32[]{:S(2)}) collective-permute-start(bf16[1024,512]{1,0:T(8,128)(2,1)S(1)} %join.5.refs_1_), channel_id=1, source_target_pairs={{0,64},{1,17},{2,66},{3,19},{4,68},{5,21},{6,70},{7,23},{8,72},{9,... | collective-permute-start | bytes 3145736 | tf_op jit(solution)/shard_map/ppermute | solution.py:41
  87.7 24.0 %collective-permute-start.29 = (bf16[1024,512]{1,0:T(8,128)(2,1)S(1)}, bf16[1024,512]{1,0:T(8,128)(2,1)S(1)}, u32[]{:S(2)}, u32[]{:S(2)}) collective-permute-start(bf16[1024,512]{1,0:T(8,128)(2,1)S(1)} %join.5.refs_1_), channel_id=1, source_target_pairs={{0,192},{1,49},{2,194},{3,51},{4,196},{5,53},{6,198},{7,55},{8,200... | collective-permute-start | bytes 3145736 | tf_op jit(solution)/shard_map/ppermute | solution.py:41
  100.5 16.8 %collective-permute-start.30 = (bf16[512,512]{1,0:T(8,128)(2,1)S(1)}, bf16[512,512]{1,0:T(8,128)(2,1)S(1)}, u32[]{:S(2)}, u32[]{:S(2)}) collective-permute-start(bf16[512,512]{1,0:T(8,128)(2,1)S(1)} %slice.28), channel_id=1, source_target_pairs={{0,64},{1,17},{2,66},{3,19},{4,68},{5,21},{6,70},{7,23},{8,72},{9,... | collective-permute-start | bytes 1572872 | tf_op jit(solution)/shard_map/ppermute | solution.py:41
  100.6 16.7 %collective-permute-start.31 = (bf16[512,512]{1,0:T(8,128)(2,1)S(1)}, bf16[512,512]{1,0:T(8,128)(2,1)S(1)}, u32[]{:S(2)}, u32[]{:S(2)}) collective-permute-start(bf16[512,512]{1,0:T(8,128)(2,1)S(1)} %slice.29), channel_id=1, source_target_pairs={{0,192},{1,49},{2,194},{3,51},{4,196},{5,53},{6,198},{7,55},{8,200... | collective-permute-start | bytes 1572872 | tf_op jit(solution)/shard_map/ppermute | solution.py:41
  111.7 11.2 %collective-permute-start.32 = (bf16[512,512]{1,0:T(8,128)(2,1)S(1)}, bf16[512,512]{1,0:T(8,128)(2,1)S(1)}, u32[]{:S(2)}, u32[]{:S(2)}) collective-permute-start(bf16[512,512]{1,0:T(8,128)(2,1)S(1)} %slice.30), channel_id=1, source_target_pairs={{0,64},{1,17},{2,66},{3,19},{4,68},{5,21},{6,70},{7,23},{8,72},{9,... | collective-permute-start | bytes 1572872 | tf_op jit(solution)/shard_map/ppermute | solution.py:41
  111.9 11.1 %collective-permute-start.33 = (bf16[512,512]{1,0:T(8,128)(2,1)S(1)}, bf16[512,512]{1,0:T(8,128)(2,1)S(1)}, u32[]{:S(2)}, u32[]{:S(2)}) collective-permute-start(bf16[512,512]{1,0:T(8,128)(2,1)S(1)} %slice.31), channel_id=1, source_target_pairs={{0,192},{1,49},{2,194},{3,51},{4,196},{5,53},{6,198},{7,55},{8,200... | collective-permute-start | bytes 1572872 | tf_op jit(solution)/shard_map/ppermute | solution.py:41

commit v4 on v3

--- a/solution.py
+++ b/solution.py
@@ -16,6 +16,7 @@
 BF16 = jnp.bfloat16
 VMEM = pl.BlockSpec(memory_space=pltpu.VMEM)
 SMEM = pl.BlockSpec(memory_space=pltpu.SMEM)
+ANY = pl.BlockSpec(memory_space=pl.ANY)
 SMALL = pltpu.CompilerParams(vmem_limit_bytes=4 << 20)
 LARGE = pltpu.CompilerParams(vmem_limit_bytes=16 << 20)
 
@@ -126,24 +127,46 @@
     )(panel, *rights)
 
 
-def finish_kernel(middle, places, where_ref, panel_ref, sum_ref, *refs):
+def middle_kernel(places, where_ref, panel_ref, sum_ref, *refs):
     keep_ref, out_ref = refs[-2:]
     total = sum_ref[...] + total_of(panel_ref, refs[:-2], places)
     total = keep_ref[...].astype(F32) * total
-    if middle:
-        diagonal = (lax.broadcasted_iota(jnp.int32, total.shape, 0) + where_ref[2 * TILES]
-                    == lax.broadcasted_iota(jnp.int32, total.shape, 1))
-        total = jnp.where(diagonal, 1.5, 0.0) - 0.5 * total
-    out_ref[...] = total.astype(BF16)
-
-
-def finish(where, panel, begun, rights, places, keep, middle):
-    return pl.pallas_call(
-        functools.partial(finish_kernel, middle, places),
+    diagonal = (lax.broadcasted_iota(jnp.int32, total.shape, 0) + where_ref[2 * TILES]
+                == lax.broadcasted_iota(jnp.int32, total.shape, 1))
+    out_ref[...] = (jnp.where(diagonal, 1.5, 0.0) - 0.5 * total).astype(BF16)
+
+
+def finish_middle(where, panel, begun, rights, places, keep):
+    return pl.pallas_call(
+        functools.partial(middle_kernel, places),
         in_specs=[SMEM] + [VMEM] * (3 + len(rights)), out_specs=VMEM,
         out_shape=jax.ShapeDtypeStruct(keep.shape, BF16),
-        compiler_params=LARGE, cost_estimate=cost(2, panel, rights[0]), name="finish",
+        compiler_params=LARGE, cost_estimate=cost(2, panel, rights[0]), name="middle",
     )(where, panel, begun, *rights, keep)
+
+
+def last_kernel(places, panel_ref, sum_ref, *refs):
+    rights, keep_ref, out_hbm, out_ref, sems = refs[:-4], refs[-4], refs[-3], refs[-2], refs[-1]
+    half = out_ref.shape[0] // 2
+    stores = []
+    for k in range(2):
+        rows = pl.ds(k * half, half)
+        total = sum_ref[rows, :] + total_of(panel_ref.at[:, rows, :], rights, places)
+        out_ref[rows, :] = (keep_ref[rows, :].astype(F32) * total).astype(BF16)
+        stores.append(pltpu.make_async_copy(out_ref.at[rows], out_hbm.at[rows], sems.at[k]))
+        stores[-1].start()
+    for store in stores:
+        store.wait()
+
+
+def finish_last(panel, begun, rights, places, keep):
+    return pl.pallas_call(
+        functools.partial(last_kernel, places),
+        in_specs=[VMEM] * (3 + len(rights)), out_specs=ANY,
+        out_shape=jax.ShapeDtypeStruct(keep.shape, BF16),
+        scratch_shapes=[pltpu.VMEM(keep.shape, BF16), pltpu.SemaphoreType.DMA((2,))],
+        compiler_params=LARGE, cost_estimate=cost(2, panel, rights[0]), name="last",
+    )(panel, begun, *rights, keep)
 
 
 def around(block, axis):
@@ -198,18 +221,22 @@
     own[1], other[1], f1, f3, f2 = together(own[1], other[1], f1, f3, f2)
     full = join(masked, f1, f3, f2)
     full1, full3 = around(full, second_axis)
-    for _ in range(2):
-        own.append(send(own[-1], RING))
-        other.append(send(other[-1], RING))
-    own.append(send(own[-1], RING))
+    own.append(send(own[1], RING))
+    other.append(send(other[1], RING))
+    own[2], own1 = together(own[2], send(own[1], SWAP))
+    own.append(send(own[2], RING))
+    other[2], other1 = together(other[2], send(other[1], SWAP))
+    other.append(send(other[2], RING))
+    own[3], own2 = together(own[3], send(own[2], SWAP))
+    own.append(send(own[3], RING))
     late = opposite(full1, full3, second_axis)
-    swapped = [send(a, SWAP) for a in own[1:] + other[1:]]
+    swapped = [own1, own2, send(own[3], SWAP), send(own[4], SWAP), other1, send(other[2], SWAP), send(other[3], SWAP)]
     panel = arrange(where, own + other + swapped)
     begun = begin(panel, [full, full1, full3], [(0, 0), (2, 0), (6, 0)])
     begun, *late = together(begun, *late)
-    middle = finish(where, panel, begun, late, [(4, 0), (5, 0)], keep, True)
+    middle = finish_middle(where, panel, begun, late, [(4, 0), (5, 0)], keep)
     early, places, late, late_places = gather(middle)
-    return finish(where, panel, begin(panel, early, places), late, late_places, keep, False)
+    return finish_last(panel, begin(panel, early, places), late, late_places, keep)
 
 
 def solution(mesh):

time: 126 us -> 123 us (0.976)
  waiting for transfers between devices: 61.5 us -> 58.2 us
    ppermute x34, waiting for transfers between devices: 61.5 us -> 58.2 us  [send(): return lax.ppermute(block, AXES, pairs)]
  transfers between devices with their start and end apart: 34 -> 34, of which waited for: 15 -> 16; matrix products, arithmetic and copies ran while one was open for 0% -> 0% of each run, Pallas kernels for 7% -> 7%
where the time goes in v4:
time: 123 us; the launch traced here: 121 us
  waiting for transfers between devices  58.2 us (47%)
  starting transfers between devices  48.3 us (39%)
  Pallas kernels  12.5 us (10%)
  local copies, waits for them, and re-layouts  2.15 us (2%)
    ppermute x34, waiting for transfers between devices, send(): return lax.ppermute(block, AXES, pairs)  58.2 us
    ppermute x34, starting transfers between devices, send(): return lax.ppermute(block, AXES, pairs)  48.3 us
    pallas_call x2, Pallas kernels, begin(): pl.pallas_call(functools.partial(begin_kernel, places), in_specs=[VMEM] *...  7.34 us
  transfers between devices with their start and end apart: 34, of which 16 were waited for; matrix products, arithmetic and copies ran while one was open for 0% of the time, Pallas kernels for 7%

profile of v4, /device:TPU:1, one launch (start us, length us, event | category | flops | bytes accessed | tf_op | source)
XLA Modules:
  0.0 121.5 jit_solution(5165058421325389093)
XLA Ops:
  0.0 0.1 stack.135.where_ref
  0.1 0.0 copy-start
  0.1 1.0 copy-done
  1.2 0.7 copy-done.1
  1.8 0.4 mask.1
  2.2 3.3 %collective-permute-start.1 = (bf16[512,512]{1,0:T(8,128)(2,1)S(1)}, bf16[512,512]{1,0:T(8,128)(2,1)S(1)}, u32[]{:S(2)}, u32[]{:S(2)}) collective-permute-start(bf16[512,512]{1,0:T(8,128)(2,1)S(1)} %get-tuple-element.29.refs_0_), channel_id=1, source_target_pairs={{0,1},{1,0},{2,3},{3,2},{4,5},{5,4},{6,7},{7,6},{8,9},{9,8},{10,11... | collective-permute-start | bytes 1572872 | tf_op jit(solution)/shard_map/ppermute | solution.py:42
  5.6 3.8 %collective-permute-start = (bf16[512,512]{1,0:T(8,128)(2,1)S(1)}, bf16[512,512]{1,0:T(8,128)(2,1)S(1)}, u32[]{:S(2)}, u32[]{:S(2)}) collective-permute-start(bf16[512,512]{1,0:T(8,128)(2,1)S(1)} %get-tuple-element.29.refs_0_), channel_id=1, source_target_pairs={{0,2},{1,15},{2,4},{3,1},{4,6},{5,3},{6,8},{7,5},{8,10},{9,7},{10,... | collective-permute-start | bytes 1572872 | tf_op jit(solution)/shard_map/ppermute | solution.py:42
  9.4 1.3 %collective-permute-start.3 = (bf16[512,512]{1,0:T(8,128)(2,1)S(1)}, bf16[512,512]{1,0:T(8,128)(2,1)S(1)}, u32[]{:S(2)}, u32[]{:S(2)}) collective-permute-start(bf16[512,512]{1,0:T(8,128)(2,1)S(1)} %get-tuple-element.29.refs_0_), channel_id=1, source_target_pairs={{0,16},{1,65},{2,18},{3,67},{4,20},{5,69},{6,22},{7,71},{8,24},{9,... | collective-permute-start | bytes 1572872 | tf_op jit(solution)/shard_map/ppermute | solution.py:42
  10.7 1.4 %collective-permute-start.4 = (bf16[512,512]{1,0:T(8,128)(2,1)S(1)}, bf16[512,512]{1,0:T(8,128)(2,1)S(1)}, u32[]{:S(2)}, u32[]{:S(2)}) collective-permute-start(bf16[512,512]{1,0:T(8,128)(2,1)S(1)} %get-tuple-element.29.refs_0_), channel_id=1, source_target_pairs={{0,48},{1,193},{2,50},{3,195},{4,52},{5,197},{6,54},{7,199},{8,56}... | collective-permute-start | bytes 1572872 | tf_op jit(solution)/shard_map/ppermute | solution.py:42
  12.1 1.6 %collective-permute-start.5 = (bf16[512,512]{1,0:T(8,128)(2,1)S(1)}, bf16[512,512]{1,0:T(8,128)(2,1)S(1)}, u32[]{:S(2)}, u32[]{:S(2)}) collective-permute-start(bf16[512,512]{1,0:T(8,128)(2,1)S(1)} %get-tuple-element.29.refs_0_), channel_id=1, source_target_pairs={{0,32},{1,129},{2,34},{3,131},{4,36},{5,133},{6,38},{7,135},{8,40}... | collective-permute-start | bytes 1572872 | tf_op jit(solution)/shard_map/ppermute | solution.py:42
  13.8 0.7 collective-permute-start.2
  14.5 1.0 collective-permute-done.refs_1_
  15.5 3.5 %collective-permute-done.3.refs_1_ = bf16[512,512]{1,0:T(8,128)(2,1)S(1)} collective-permute-done((bf16[512,512]{1,0:T(8,128)(2,1)S(1)}, bf16[512,512]{1,0:T(8,128)(2,1)S(1)}, u32[]{:S(2)}, u32[]{:S(2)}) %collective-permute-start.3) | collective-permute-done | bytes 524320 | tf_op jit(solution)/shard_map/ppermute | solution.py:42
  19.0 0.0 collective-permute-done.4.refs_2_
  19.0 6.5 %collective-permute-done.5.refs_3_ = bf16[512,512]{1,0:T(8,128)(2,1)S(1)} collective-permute-done((bf16[512,512]{1,0:T(8,128)(2,1)S(1)}, bf16[512,512]{1,0:T(8,128)(2,1)S(1)}, u32[]{:S(2)}, u32[]{:S(2)}) %collective-permute-start.5) | collective-permute-done | bytes 524320 | tf_op jit(solution)/shard_map/ppermute | solution.py:42
  25.5 0.1 join.3.refs_0_
  25.7 1.3 %collective-permute-start.18 = (bf16[2048,512]{1,0:T(8,128)(2,1)S(1)}, bf16[2048,512]{1,0:T(8,128)(2,1)S(1)}, u32[]{:S(2)}, u32[]{:S(2)}) collective-permute-start(bf16[2048,512]{1,0:T(8,128)(2,1)S(1)} %join.3.refs_0_), channel_id=1, source_target_pairs={{0,64},{1,17},{2,66},{3,19},{4,68},{5,21},{6,70},{7,23},{8,72},{9,... | collective-permute-start | bytes 6291464 | tf_op jit(solution)/shard_map/ppermute | solution.py:42
  26.9 1.5 %collective-permute-start.19 = (bf16[2048,512]{1,0:T(8,128)(2,1)S(1)}, bf16[2048,512]{1,0:T(8,128)(2,1)S(1)}, u32[]{:S(2)}, u32[]{:S(2)}) collective-permute-start(bf16[2048,512]{1,0:T(8,128)(2,1)S(1)} %join.3.refs_0_), channel_id=1, source_target_pairs={{0,192},{1,49},{2,194},{3,51},{4,196},{5,53},{6,198},{7,55},{8,200... | collective-permute-start | bytes 6291464 | tf_op jit(solution)/shard_map/ppermute | solution.py:42
  28.4 0.7 collective-permute-start.6
  29.1 1.0 collective-permute-start.11
  30.2 6.6 %collective-permute-done.6.refs_2_ = bf16[512,512]{1,0:T(8,128)(2,1)S(1)} collective-permute-done((bf16[512,512]{1,0:T(8,128)(2,1)S(1)}, bf16[512,512]{1,0:T(8,128)(2,1)S(1)}, u32[]{:S(2)}, u32[]{:S(2)}) %collective-permute-start.6) | collective-permute-done | bytes 524320 | tf_op jit(solution)/shard_map/ppermute | solution.py:42
  36.7 0.7 collective-permute-start.12
  37.5 1.7 %collective-permute-start.8 = (bf16[512,512]{1,0:T(8,128)(2,1)S(1)}, bf16[512,512]{1,0:T(8,128)(2,1)S(1)}, u32[]{:S(2)}, u32[]{:S(2)}) collective-permute-start(bf16[512,512]{1,0:T(8,128)(2,1)S(1)} %collective-permute-done.6.refs_2_), channel_id=1, source_target_pairs={{0,2},{1,15},{2,4},{3,1},{4,6},{5,3},{6,8},{7,5},{8,10},{9,7},{10,... | collective-permute-start | bytes 1572872 | tf_op jit(solution)/shard_map/ppermute | solution.py:42
  39.2 3.1 %collective-permute-done.11.refs_7_ = bf16[512,512]{1,0:T(8,128)(2,1)S(1)} collective-permute-done((bf16[512,512]{1,0:T(8,128)(2,1)S(1)}, bf16[512,512]{1,0:T(8,128)(2,1)S(1)}, u32[]{:S(2)}, u32[]{:S(2)}) %collective-permute-start.11) | collective-permute-done | bytes 524320 | tf_op jit(solution)/shard_map/ppermute | solution.py:42
  42.4 0.7 collective-permute-start.9
  43.1 1.7 %collective-permute-start.13 = (bf16[512,512]{1,0:T(8,128)(2,1)S(1)}, bf16[512,512]{1,0:T(8,128)(2,1)S(1)}, u32[]{:S(2)}, u32[]{:S(2)}) collective-permute-start(bf16[512,512]{1,0:T(8,128)(2,1)S(1)} %collective-permute-done.11.refs_7_), channel_id=1, source_target_pairs={{0,2},{1,15},{2,4},{3,1},{4,6},{5,3},{6,8},{7,5},{8,10},{9,7},{10,... | collective-permute-start | bytes 1572872 | tf_op jit(solution)/shard_map/ppermute | solution.py:42
  44.8 3.1 %collective-permute-done.8.refs_3_ = bf16[512,512]{1,0:T(8,128)(2,1)S(1)} collective-permute-done((bf16[512,512]{1,0:T(8,128)(2,1)S(1)}, bf16[512,512]{1,0:T(8,128)(2,1)S(1)}, u32[]{:S(2)}, u32[]{:S(2)}) %collective-permute-start.8) | collective-permute-done | bytes 524320 | tf_op jit(solution)/shard_map/ppermute | solution.py:42
  48.0 0.7 collective-permute-start.16
  48.7 1.7 %collective-permute-start.10 = (bf16[512,512]{1,0:T(8,128)(2,1)S(1)}, bf16[512,512]{1,0:T(8,128)(2,1)S(1)}, u32[]{:S(2)}, u32[]{:S(2)}) collective-permute-start(bf16[512,512]{1,0:T(8,128)(2,1)S(1)} %collective-permute-done.8.refs_3_), channel_id=1, source_target_pairs={{0,2},{1,15},{2,4},{3,1},{4,6},{5,3},{6,8},{7,5},{8,10},{9,7},{10,... | collective-permute-start | bytes 1572872 | tf_op jit(solution)/shard_map/ppermute | solution.py:42
  50.5 1.7 %collective-permute-done.18.refs_1_ = bf16[2048,512]{1,0:T(8,128)(2,1)S(1)} collective-permute-done((bf16[2048,512]{1,0:T(8,128)(2,1)S(1)}, bf16[2048,512]{1,0:T(8,128)(2,1)S(1)}, u32[]{:S(2)}, u32[]{:S(2)}) %collective-permute-start.18) | collective-permute-done | bytes 2097184 | tf_op jit(solution)/shard_map/ppermute | solution.py:42
  52.1 0.1 slice.32
  52.2 0.1 collective-permute-start.20
  52.3 0.1 slice.33
  52.4 2.7 %collective-permute-start.21 = (bf16[1024,512]{1,0:T(8,128)(2,1)S(1)}, bf16[1024,512]{1,0:T(8,128)(2,1)S(1)}, u32[]{:S(2)}, u32[]{:S(2)}) collective-permute-start(bf16[1024,512]{1,0:T(8,128)(2,1)S(1)} %slice.33), channel_id=1, source_target_pairs={{0,192},{1,49},{2,194},{3,51},{4,196},{5,53},{6,198},{7,55},{8,200... | collective-permute-start | bytes 3145736 | tf_op jit(solution)/shard_map/ppermute | solution.py:42
  55.1 0.5 collective-permute-start.17
  55.6 3.6 %collective-permute-done.10.refs_4_ = bf16[512,512]{1,0:T(8,128)(2,1)S(1)} collective-permute-done((bf16[512,512]{1,0:T(8,128)(2,1)S(1)}, bf16[512,512]{1,0:T(8,128)(2,1)S(1)}, u32[]{:S(2)}, u32[]{:S(2)}) %collective-permute-start.10) | collective-permute-done | bytes 524320 | tf_op jit(solution)/shard_map/ppermute | solution.py:42
  59.2 0.7 collective-permute-start.15
  60.0 1.5 %collective-permute-done.15.refs_12_ = bf16[512,512]{1,0:T(8,128)(2,1)S(1)} collective-permute-done((bf16[512,512]{1,0:T(8,128)(2,1)S(1)}, bf16[512,512]{1,0:T(8,128)(2,1)S(1)}, u32[]{:S(2)}, u32[]{:S(2)}) %collective-permute-start.15) | collective-permute-done | bytes 524320 | tf_op jit(solution)/shard_map/ppermute | solution.py:42
  61.5 1.2 arrange.1.panel_ref
  62.7 3.4 %begin.2.sum_ref = f32[512,512]{1,0:T(8,128)S(1)} custom-call(bf16[8,512,1024]{2,1,0:T(8,128)(2,1)S(1)} %arrange.1.panel_ref, bf16[2048,512]{1,0:T(8,128)(2,1)S(1)} %join.3.refs_0_, bf16[2048,512]{1,0:T(8,128)(2,1)S(1)} %collective-permute-done.18.refs_1_, bf16[2048,512]{1,0:T(8,128)(2,1)S(1)} %collective-permute-done.19.refs_2_), custom_call_target="tpu_custom_call" | custom-call | tf_op jit(solution)/shard_map/begin/pallas_call | solution.py:123
  66.1 1.0 collective-permute-done.20.refs_0_
  67.1 1.9 %middle.1.refs_0_ = bf16[512,512]{1,0:T(8,128)(2,1)S(1)} custom-call(s32[33]{0:T(128)S(1)} %stack.135.where_ref, bf16[8,512,1024]{2,1,0:T(8,128)(2,1)S(1)} %arrange.1.panel_ref, f32[512,512]{1,0:T(8,128)S(1)} %begin.2.sum_ref, bf16[1024,512]{1,0:T(8,128)(2,1)S(1)} %collective-permute-done.20.refs_0_, bf16[1024,512]{1,0:T(8,128)(2,1)S(1)} %collective-permute-done.21.refs_1_, ...), custom_call_target="tpu_custom_call" | custom-call | flops 1073741824 | bytes 4194304 | tf_op jit(solution)/shard_map/middle/pallas_call | solution.py:140
  69.0 0.9 collective-permute-start.22
  70.0 1.8 %collective-permute-start.23 = (bf16[512,512]{1,0:T(8,128)(2,1)S(1)}, bf16[512,512]{1,0:T(8,128)(2,1)S(1)}, u32[]{:S(2)}, u32[]{:S(2)}) collective-permute-start(bf16[512,512]{1,0:T(8,128)(2,1)S(1)} %middle.1.refs_0_), channel_id=1, source_target_pairs={{0,48},{1,193},{2,50},{3,195},{4,52},{5,197},{6,54},{7,199},{8,56}... | collective-permute-start | bytes 1572872 | tf_op jit(solution)/shard_map/ppermute | solution.py:42
  71.8 6.7 %collective-permute-done.22.refs_1_ = bf16[512,512]{1,0:T(8,128)(2,1)S(1)} collective-permute-done((bf16[512,512]{1,0:T(8,128)(2,1)S(1)}, bf16[512,512]{1,0:T(8,128)(2,1)S(1)}, u32[]{:S(2)}, u32[]{:S(2)}) %collective-permute-start.22) | collective-permute-done | bytes 524320 | tf_op jit(solution)/shard_map/ppermute | solution.py:42
  78.5 0.1 collective-permute-start.24
  78.6 2.8 %collective-permute-start.25 = (bf16[256,512]{1,0:T(8,128)(2,1)S(1)}, bf16[256,512]{1,0:T(8,128)(2,1)S(1)}, u32[]{:S(2)}, u32[]{:S(2)}) collective-permute-start(bf16[256,512]{1,0:T(8,128)(2,1)S(1)} %slice.35), channel_id=1, source_target_pairs={{0,48},{1,193},{2,50},{3,195},{4,52},{5,197},{6,54},{7,199},{8,56}... | collective-permute-start | bytes 786440 | tf_op jit(solution)/shard_map/ppermute | solution.py:42
  81.4 0.1 join.4.refs_0_
  81.5 0.1 collective-permute-start.26
  81.6 2.9 %collective-permute-start.27 = (bf16[1024,512]{1,0:T(8,128)(2,1)S(1)}, bf16[1024,512]{1,0:T(8,128)(2,1)S(1)}, u32[]{:S(2)}, u32[]{:S(2)}) collective-permute-start(bf16[1024,512]{1,0:T(8,128)(2,1)S(1)} %join.4.refs_0_), channel_id=1, source_target_pairs={{0,192},{1,49},{2,194},{3,51},{4,196},{5,53},{6,198},{7,55},{8,200... | collective-permute-start | bytes 3145736 | tf_op jit(solution)/shard_map/ppermute | solution.py:42
  84.5 0.7 collective-permute-done.24.refs_1_
  85.3 0.1 join.5.refs_1_
  85.4 0.1 collective-permute-start.28
  85.5 4.7 %collective-permute-start.29 = (bf16[1024,512]{1,0:T(8,128)(2,1)S(1)}, bf16[1024,512]{1,0:T(8,128)(2,1)S(1)}, u32[]{:S(2)}, u32[]{:S(2)}) collective-permute-start(bf16[1024,512]{1,0:T(8,128)(2,1)S(1)} %join.5.refs_1_), channel_id=1, source_target_pairs={{0,192},{1,49},{2,194},{3,51},{4,196},{5,53},{6,198},{7,55},{8,200... | collective-permute-start | bytes 3145736 | tf_op jit(solution)/shard_map/ppermute | solution.py:42
  90.2 7.2 %collective-permute-done.26.refs_2_ = bf16[1024,512]{1,0:T(8,128)(2,1)S(1)} collective-permute-done((bf16[1024,512]{1,0:T(8,128)(2,1)S(1)}, bf16[1024,512]{1,0:T(8,128)(2,1)S(1)}, u32[]{:S(2)}, u32[]{:S(2)}) %collective-permute-start.26) | collective-permute-done | bytes 1048608 | tf_op jit(solution)/shard_map/ppermute | solution.py:42
  97.4 0.5 collective-permute-start.30
  97.9 2.7 %collective-permute-start.31 = (bf16[512,512]{1,0:T(8,128)(2,1)S(1)}, bf16[512,512]{1,0:T(8,128)(2,1)S(1)}, u32[]{:S(2)}, u32[]{:S(2)}) collective-permute-start(bf16[512,512]{1,0:T(8,128)(2,1)S(1)} %slice.29), channel_id=1, source_target_pairs={{0,192},{1,49},{2,194},{3,51},{4,196},{5,53},{6,198},{7,55},{8,200... | collective-permute-start | bytes 1572872 | tf_op jit(solution)/shard_map/ppermute | solution.py:42
  100.7 7.9 %collective-permute-done.28.refs_3_ = bf16[1024,512]{1,0:T(8,128)(2,1)S(1)} collective-permute-done((bf16[1024,512]{1,0:T(8,128)(2,1)S(1)}, bf16[1024,512]{1,0:T(8,128)(2,1)S(1)}, u32[]{:S(2)}, u32[]{:S(2)}) %collective-permute-start.28) | collective-permute-done | bytes 1048608 | tf_op jit(solution)/shard_map/ppermute | solution.py:42
  108.7 0.5 collective-permute-start.32
  109.2 2.7 %collective-permute-start.33 = (bf16[512,512]{1,0:T(8,128)(2,1)S(1)}, bf16[512,512]{1,0:T(8,128)(2,1)S(1)}, u32[]{:S(2)}, u32[]{:S(2)}) collective-permute-start(bf16[512,512]{1,0:T(8,128)(2,1)S(1)} %slice.31), channel_id=1, source_target_pairs={{0,192},{1,49},{2,194},{3,51},{4,196},{5,53},{6,198},{7,55},{8,200... | collective-permute-start | bytes 1572872 | tf_op jit(solution)/shard_map/ppermute | solution.py:42
  111.9 2.3 %collective-permute-done.30.refs_6_ = bf16[512,512]{1,0:T(8,128)(2,1)S(1)} collective-permute-done((bf16[512,512]{1,0:T(8,128)(2,1)S(1)}, bf16[512,512]{1,0:T(8,128)(2,1)S(1)}, u32[]{:S(2)}, u32[]{:S(2)}) %collective-permute-start.30) | collective-permute-done | bytes 524320 | tf_op jit(solution)/shard_map/ppermute | solution.py:42
  114.2 3.9 %begin.3.sum_ref = f32[512,512]{1,0:T(8,128)S(1)} custom-call(bf16[8,512,1024]{2,1,0:T(8,128)(2,1)S(1)} %arrange.1.panel_ref, bf16[1024,512]{1,0:T(8,128)(2,1)S(1)} %join.4.refs_0_, bf16[1024,512]{1,0:T(8,128)(2,1)S(1)} %join.5.refs_1_, bf16[1024,512]{1,0:T(8,128)(2,1)S(1)} %collective-permute-done.26.refs_2_, ...), custom_call_target="tpu_custom_call" | custom-call | tf_op jit(solution)/shard_map/begin/pallas_call | solution.py:123
  118.2 1.7 %collective-permute-done.32.refs_0_ = bf16[512,512]{1,0:T(8,128)(2,1)S(1)} collective-permute-done((bf16[512,512]{1,0:T(8,128)(2,1)S(1)}, bf16[512,512]{1,0:T(8,128)(2,1)S(1)}, u32[]{:S(2)}, u32[]{:S(2)}) %collective-permute-start.32) | collective-permute-done | bytes 524320 | tf_op jit(solution)/shard_map/ppermute | solution.py:42
  119.9 1.4 %last.1 = bf16[512,512]{1,0:T(8,128)(2,1)} custom-call(bf16[8,512,1024]{2,1,0:T(8,128)(2,1)S(1)} %arrange.1.panel_ref, f32[512,512]{1,0:T(8,128)S(1)} %begin.3.sum_ref, bf16[512,512]{1,0:T(8,128)(2,1)S(1)} %collective-permute-done.32.refs_0_, bf16[512,512]{1,0:T(8,128)(2,1)S(1)} %collective-permute-done.33.refs_1_, ...), custom_call_target="tpu_custom_call" | custom-call | flops 536870912 | bytes 2097152 | tf_op jit(solution)/shard_map/last/pallas_call | solution.py:163
  (26 shorter events, 0.2 us)
Async XLA Ops:
  0.1 1.0 copy-start
  1.2 0.7 copy-start.1
  2.2 11.6 %collective-permute-start.1 = (bf16[512,512]{1,0:T(8,128)(2,1)S(1)}, bf16[512,512]{1,0:T(8,128)(2,1)S(1)}, u32[]{:S(2)}, u32[]{:S(2)}) collective-permute-start(bf16[512,512]{1,0:T(8,128)(2,1)S(1)} %get-tuple-element.29.refs_0_), channel_id=1, source_target_pairs={{0,1},{1,0},{2,3},{3,2},{4,5},{5,4},{6,7},{7,6},{8,9},{9,8},{10,11... | collective-permute-start | bytes 1572872 | tf_op jit(solution)/shard_map/ppermute | solution.py:42
  5.6 10.0 %collective-permute-start = (bf16[512,512]{1,0:T(8,128)(2,1)S(1)}, bf16[512,512]{1,0:T(8,128)(2,1)S(1)}, u32[]{:S(2)}, u32[]{:S(2)}) collective-permute-start(bf16[512,512]{1,0:T(8,128)(2,1)S(1)} %get-tuple-element.29.refs_0_), channel_id=1, source_target_pairs={{0,2},{1,15},{2,4},{3,1},{4,6},{5,3},{6,8},{7,5},{8,10},{9,7},{10,... | collective-permute-start | bytes 1572872 | tf_op jit(solution)/shard_map/ppermute | solution.py:42
  9.4 9.6 %collective-permute-start.3 = (bf16[512,512]{1,0:T(8,128)(2,1)S(1)}, bf16[512,512]{1,0:T(8,128)(2,1)S(1)}, u32[]{:S(2)}, u32[]{:S(2)}) collective-permute-start(bf16[512,512]{1,0:T(8,128)(2,1)S(1)} %get-tuple-element.29.refs_0_), channel_id=1, source_target_pairs={{0,16},{1,65},{2,18},{3,67},{4,20},{5,69},{6,22},{7,71},{8,24},{9,... | collective-permute-start | bytes 1572872 | tf_op jit(solution)/shard_map/ppermute | solution.py:42
  10.7 8.3 %collective-permute-start.4 = (bf16[512,512]{1,0:T(8,128)(2,1)S(1)}, bf16[512,512]{1,0:T(8,128)(2,1)S(1)}, u32[]{:S(2)}, u32[]{:S(2)}) collective-permute-start(bf16[512,512]{1,0:T(8,128)(2,1)S(1)} %get-tuple-element.29.refs_0_), channel_id=1, source_target_pairs={{0,48},{1,193},{2,50},{3,195},{4,52},{5,197},{6,54},{7,199},{8,56}... | collective-permute-start | bytes 1572872 | tf_op jit(solution)/shard_map/ppermute | solution.py:42
  12.1 13.4 %collective-permute-start.5 = (bf16[512,512]{1,0:T(8,128)(2,1)S(1)}, bf16[512,512]{1,0:T(8,128)(2,1)S(1)}, u32[]{:S(2)}, u32[]{:S(2)}) collective-permute-start(bf16[512,512]{1,0:T(8,128)(2,1)S(1)} %get-tuple-element.29.refs_0_), channel_id=1, source_target_pairs={{0,32},{1,129},{2,34},{3,131},{4,36},{5,133},{6,38},{7,135},{8,40}... | collective-permute-start | bytes 1572872 | tf_op jit(solution)/shard_map/ppermute | solution.py:42
  13.8 11.7 %collective-permute-start.2 = (bf16[512,512]{1,0:T(8,128)(2,1)S(1)}, bf16[512,512]{1,0:T(8,128)(2,1)S(1)}, u32[]{:S(2)}, u32[]{:S(2)}) collective-permute-start(bf16[512,512]{1,0:T(8,128)(2,1)S(1)} %collective-permute-done.1.refs_5_), channel_id=1, source_target_pairs={{0,2},{1,15},{2,4},{3,1},{4,6},{5,3},{6,8},{7,5},{8,10},{9,7},{10,... | collective-permute-start | bytes 1572872 | tf_op jit(solution)/shard_map/ppermute | solution.py:42
  25.7 26.5 %collective-permute-start.18 = (bf16[2048,512]{1,0:T(8,128)(2,1)S(1)}, bf16[2048,512]{1,0:T(8,128)(2,1)S(1)}, u32[]{:S(2)}, u32[]{:S(2)}) collective-permute-start(bf16[2048,512]{1,0:T(8,128)(2,1)S(1)} %join.3.refs_0_), channel_id=1, source_target_pairs={{0,64},{1,17},{2,66},{3,19},{4,68},{5,21},{6,70},{7,23},{8,72},{9,... | collective-permute-start | bytes 6291464 | tf_op jit(solution)/shard_map/ppermute | solution.py:42
  26.9 25.3 %collective-permute-start.19 = (bf16[2048,512]{1,0:T(8,128)(2,1)S(1)}, bf16[2048,512]{1,0:T(8,128)(2,1)S(1)}, u32[]{:S(2)}, u32[]{:S(2)}) collective-permute-start(bf16[2048,512]{1,0:T(8,128)(2,1)S(1)} %join.3.refs_0_), channel_id=1, source_target_pairs={{0,192},{1,49},{2,194},{3,51},{4,196},{5,53},{6,198},{7,55},{8,200... | collective-permute-start | bytes 6291464 | tf_op jit(solution)/shard_map/ppermute | solution.py:42
  28.4 8.3 %collective-permute-start.6 = (bf16[512,512]{1,0:T(8,128)(2,1)S(1)}, bf16[512,512]{1,0:T(8,128)(2,1)S(1)}, u32[]{:S(2)}, u32[]{:S(2)}) collective-permute-start(bf16[512,512]{1,0:T(8,128)(2,1)S(1)} %collective-permute-done.refs_1_), channel_id=1, source_target_pairs={{0,2},{1,15},{2,4},{3,1},{4,6},{5,3},{6,8},{7,5},{8,10},{9,7},{10,... | collective-permute-start | bytes 1572872 | tf_op jit(solution)/shard_map/ppermute | solution.py:42
  29.1 8.3 %collective-permute-start.7 = (bf16[512,512]{1,0:T(8,128)(2,1)S(1)}, bf16[512,512]{1,0:T(8,128)(2,1)S(1)}, u32[]{:S(2)}, u32[]{:S(2)}) collective-permute-start(bf16[512,512]{1,0:T(8,128)(2,1)S(1)} %collective-permute-done.refs_1_), channel_id=1, source_target_pairs={{0,1},{1,0},{2,3},{3,2},{4,5},{5,4},{6,7},{7,6},{8,9},{9,8},{10,11... | collective-permute-start | bytes 1572872 | tf_op jit(solution)/shard_map/ppermute | solution.py:42
  29.1 13.2 %collective-permute-start.11 = (bf16[512,512]{1,0:T(8,128)(2,1)S(1)}, bf16[512,512]{1,0:T(8,128)(2,1)S(1)}, u32[]{:S(2)}, u32[]{:S(2)}) collective-permute-start(bf16[512,512]{1,0:T(8,128)(2,1)S(1)} %collective-permute-done.2.refs_6_), channel_id=1, source_target_pairs={{0,2},{1,15},{2,4},{3,1},{4,6},{5,3},{6,8},{7,5},{8,10},{9,7},{10,... | collective-permute-start | bytes 1572872 | tf_op jit(solution)/shard_map/ppermute | solution.py:42
  36.7 6.4 %collective-permute-start.12 = (bf16[512,512]{1,0:T(8,128)(2,1)S(1)}, bf16[512,512]{1,0:T(8,128)(2,1)S(1)}, u32[]{:S(2)}, u32[]{:S(2)}) collective-permute-start(bf16[512,512]{1,0:T(8,128)(2,1)S(1)} %collective-permute-done.2.refs_6_), channel_id=1, source_target_pairs={{0,1},{1,0},{2,3},{3,2},{4,5},{5,4},{6,7},{7,6},{8,9},{9,8},{10,11... | collective-permute-start | bytes 1572872 | tf_op jit(solution)/shard_map/ppermute | solution.py:42
  37.5 10.5 %collective-permute-start.8 = (bf16[512,512]{1,0:T(8,128)(2,1)S(1)}, bf16[512,512]{1,0:T(8,128)(2,1)S(1)}, u32[]{:S(2)}, u32[]{:S(2)}) collective-permute-start(bf16[512,512]{1,0:T(8,128)(2,1)S(1)} %collective-permute-done.6.refs_2_), channel_id=1, source_target_pairs={{0,2},{1,15},{2,4},{3,1},{4,6},{5,3},{6,8},{7,5},{8,10},{9,7},{10,... | collective-permute-start | bytes 1572872 | tf_op jit(solution)/shard_map/ppermute | solution.py:42
  42.4 6.4 %collective-permute-start.9 = (bf16[512,512]{1,0:T(8,128)(2,1)S(1)}, bf16[512,512]{1,0:T(8,128)(2,1)S(1)}, u32[]{:S(2)}, u32[]{:S(2)}) collective-permute-start(bf16[512,512]{1,0:T(8,128)(2,1)S(1)} %collective-permute-done.6.refs_2_), channel_id=1, source_target_pairs={{0,1},{1,0},{2,3},{3,2},{4,5},{5,4},{6,7},{7,6},{8,9},{9,8},{10,11... | collective-permute-start | bytes 1572872 | tf_op jit(solution)/shard_map/ppermute | solution.py:42
  43.1 12.0 %collective-permute-start.13 = (bf16[512,512]{1,0:T(8,128)(2,1)S(1)}, bf16[512,512]{1,0:T(8,128)(2,1)S(1)}, u32[]{:S(2)}, u32[]{:S(2)}) collective-permute-start(bf16[512,512]{1,0:T(8,128)(2,1)S(1)} %collective-permute-done.11.refs_7_), channel_id=1, source_target_pairs={{0,2},{1,15},{2,4},{3,1},{4,6},{5,3},{6,8},{7,5},{8,10},{9,7},{10,... | collective-permute-start | bytes 1572872 | tf_op jit(solution)/shard_map/ppermute | solution.py:42
  48.0 7.1 %collective-permute-start.16 = (bf16[512,512]{1,0:T(8,128)(2,1)S(1)}, bf16[512,512]{1,0:T(8,128)(2,1)S(1)}, u32[]{:S(2)}, u32[]{:S(2)}) collective-permute-start(bf16[512,512]{1,0:T(8,128)(2,1)S(1)} %collective-permute-done.11.refs_7_), channel_id=1, source_target_pairs={{0,1},{1,0},{2,3},{3,2},{4,5},{5,4},{6,7},{7,6},{8,9},{9,8},{10,11... | collective-permute-start | bytes 1572872 | tf_op jit(solution)/shard_map/ppermute | solution.py:42
  48.7 10.5 %collective-permute-start.10 = (bf16[512,512]{1,0:T(8,128)(2,1)S(1)}, bf16[512,512]{1,0:T(8,128)(2,1)S(1)}, u32[]{:S(2)}, u32[]{:S(2)}) collective-permute-start(bf16[512,512]{1,0:T(8,128)(2,1)S(1)} %collective-permute-done.8.refs_3_), channel_id=1, source_target_pairs={{0,2},{1,15},{2,4},{3,1},{4,6},{5,3},{6,8},{7,5},{8,10},{9,7},{10,... | collective-permute-start | bytes 1572872 | tf_op jit(solution)/shard_map/ppermute | solution.py:42
  52.2 14.9 %collective-permute-start.20 = (bf16[1024,512]{1,0:T(8,128)(2,1)S(1)}, bf16[1024,512]{1,0:T(8,128)(2,1)S(1)}, u32[]{:S(2)}, u32[]{:S(2)}) collective-permute-start(bf16[1024,512]{1,0:T(8,128)(2,1)S(1)} %slice.32), channel_id=1, source_target_pairs={{0,64},{1,17},{2,66},{3,19},{4,68},{5,21},{6,70},{7,23},{8,72},{9,... | collective-permute-start | bytes 3145736 | tf_op jit(solution)/shard_map/ppermute | solution.py:42
  52.4 14.8 %collective-permute-start.21 = (bf16[1024,512]{1,0:T(8,128)(2,1)S(1)}, bf16[1024,512]{1,0:T(8,128)(2,1)S(1)}, u32[]{:S(2)}, u32[]{:S(2)}) collective-permute-start(bf16[1024,512]{1,0:T(8,128)(2,1)S(1)} %slice.33), channel_id=1, source_target_pairs={{0,192},{1,49},{2,194},{3,51},{4,196},{5,53},{6,198},{7,55},{8,200... | collective-permute-start | bytes 3145736 | tf_op jit(solution)/shard_map/ppermute | solution.py:42
  55.1 4.9 %collective-permute-start.14 = (bf16[512,512]{1,0:T(8,128)(2,1)S(1)}, bf16[512,512]{1,0:T(8,128)(2,1)S(1)}, u32[]{:S(2)}, u32[]{:S(2)}) collective-permute-start(bf16[512,512]{1,0:T(8,128)(2,1)S(1)} %collective-permute-done.8.refs_3_), channel_id=1, source_target_pairs={{0,1},{1,0},{2,3},{3,2},{4,5},{5,4},{6,7},{7,6},{8,9},{9,8},{10,11... | collective-permute-start | bytes 1572872 | tf_op jit(solution)/shard_map/ppermute | solution.py:42
  55.1 4.8 %collective-permute-start.17 = (bf16[512,512]{1,0:T(8,128)(2,1)S(1)}, bf16[512,512]{1,0:T(8,128)(2,1)S(1)}, u32[]{:S(2)}, u32[]{:S(2)}) collective-permute-start(bf16[512,512]{1,0:T(8,128)(2,1)S(1)} %collective-permute-done.13.refs_8_), channel_id=1, source_target_pairs={{0,1},{1,0},{2,3},{3,2},{4,5},{5,4},{6,7},{7,6},{8,9},{9,8},{10,11... | collective-permute-start | bytes 1572872 | tf_op jit(solution)/shard_map/ppermute | solution.py:42
  59.2 2.3 %collective-permute-start.15 = (bf16[512,512]{1,0:T(8,128)(2,1)S(1)}, bf16[512,512]{1,0:T(8,128)(2,1)S(1)}, u32[]{:S(2)}, u32[]{:S(2)}) collective-permute-start(bf16[512,512]{1,0:T(8,128)(2,1)S(1)} %collective-permute-done.10.refs_4_), channel_id=1, source_target_pairs={{0,1},{1,0},{2,3},{3,2},{4,5},{5,4},{6,7},{7,6},{8,9},{9,8},{10,11... | collective-permute-start | bytes 1572872 | tf_op jit(solution)/shard_map/ppermute | solution.py:42
  69.0 9.4 %collective-permute-start.22 = (bf16[512,512]{1,0:T(8,128)(2,1)S(1)}, bf16[512,512]{1,0:T(8,128)(2,1)S(1)}, u32[]{:S(2)}, u32[]{:S(2)}) collective-permute-start(bf16[512,512]{1,0:T(8,128)(2,1)S(1)} %middle.1.refs_0_), channel_id=1, source_target_pairs={{0,16},{1,65},{2,18},{3,67},{4,20},{5,69},{6,22},{7,71},{8,24},{9,... | collective-permute-start | bytes 1572872 | tf_op jit(solution)/shard_map/ppermute | solution.py:42
  70.0 8.6 %collective-permute-start.23 = (bf16[512,512]{1,0:T(8,128)(2,1)S(1)}, bf16[512,512]{1,0:T(8,128)(2,1)S(1)}, u32[]{:S(2)}, u32[]{:S(2)}) collective-permute-start(bf16[512,512]{1,0:T(8,128)(2,1)S(1)} %middle.1.refs_0_), channel_id=1, source_target_pairs={{0,48},{1,193},{2,50},{3,195},{4,52},{5,197},{6,54},{7,199},{8,56}... | collective-permute-start | bytes 1572872 | tf_op jit(solution)/shard_map/ppermute | solution.py:42
  78.5 6.8 %collective-permute-start.24 = (bf16[256,512]{1,0:T(8,128)(2,1)S(1)}, bf16[256,512]{1,0:T(8,128)(2,1)S(1)}, u32[]{:S(2)}, u32[]{:S(2)}) collective-permute-start(bf16[256,512]{1,0:T(8,128)(2,1)S(1)} %slice.34), channel_id=1, source_target_pairs={{0,16},{1,65},{2,18},{3,67},{4,20},{5,69},{6,22},{7,71},{8,24},{9,... | collective-permute-start | bytes 786440 | tf_op jit(solution)/shard_map/ppermute | solution.py:42
  78.6 6.7 %collective-permute-start.25 = (bf16[256,512]{1,0:T(8,128)(2,1)S(1)}, bf16[256,512]{1,0:T(8,128)(2,1)S(1)}, u32[]{:S(2)}, u32[]{:S(2)}) collective-permute-start(bf16[256,512]{1,0:T(8,128)(2,1)S(1)} %slice.35), channel_id=1, source_target_pairs={{0,48},{1,193},{2,50},{3,195},{4,52},{5,197},{6,54},{7,199},{8,56}... | collective-permute-start | bytes 786440 | tf_op jit(solution)/shard_map/ppermute | solution.py:42
  81.5 15.9 %collective-permute-start.26 = (bf16[1024,512]{1,0:T(8,128)(2,1)S(1)}, bf16[1024,512]{1,0:T(8,128)(2,1)S(1)}, u32[]{:S(2)}, u32[]{:S(2)}) collective-permute-start(bf16[1024,512]{1,0:T(8,128)(2,1)S(1)} %join.4.refs_0_), channel_id=1, source_target_pairs={{0,64},{1,17},{2,66},{3,19},{4,68},{5,21},{6,70},{7,23},{8,72},{9,... | collective-permute-start | bytes 3145736 | tf_op jit(solution)/shard_map/ppermute | solution.py:42
  81.6 15.8 %collective-permute-start.27 = (bf16[1024,512]{1,0:T(8,128)(2,1)S(1)}, bf16[1024,512]{1,0:T(8,128)(2,1)S(1)}, u32[]{:S(2)}, u32[]{:S(2)}) collective-permute-start(bf16[1024,512]{1,0:T(8,128)(2,1)S(1)} %join.4.refs_0_), channel_id=1, source_target_pairs={{0,192},{1,49},{2,194},{3,51},{4,196},{5,53},{6,198},{7,55},{8,200... | collective-permute-start | bytes 3145736 | tf_op jit(solution)/shard_map/ppermute | solution.py:42
  85.4 23.2 %collective-permute-start.28 = (bf16[1024,512]{1,0:T(8,128)(2,1)S(1)}, bf16[1024,512]{1,0:T(8,128)(2,1)S(1)}, u32[]{:S(2)}, u32[]{:S(2)}) collective-permute-start(bf16[1024,512]{1,0:T(8,128)(2,1)S(1)} %join.5.refs_1_), channel_id=1, source_target_pairs={{0,64},{1,17},{2,66},{3,19},{4,68},{5,21},{6,70},{7,23},{8,72},{9,... | collective-permute-start | bytes 3145736 | tf_op jit(solution)/shard_map/ppermute | solution.py:42
  85.5 23.2 %collective-permute-start.29 = (bf16[1024,512]{1,0:T(8,128)(2,1)S(1)}, bf16[1024,512]{1,0:T(8,128)(2,1)S(1)}, u32[]{:S(2)}, u32[]{:S(2)}) collective-permute-start(bf16[1024,512]{1,0:T(8,128)(2,1)S(1)} %join.5.refs_1_), channel_id=1, source_target_pairs={{0,192},{1,49},{2,194},{3,51},{4,196},{5,53},{6,198},{7,55},{8,200... | collective-permute-start | bytes 3145736 | tf_op jit(solution)/shard_map/ppermute | solution.py:42
  97.4 16.8 %collective-permute-start.30 = (bf16[512,512]{1,0:T(8,128)(2,1)S(1)}, bf16[512,512]{1,0:T(8,128)(2,1)S(1)}, u32[]{:S(2)}, u32[]{:S(2)}) collective-permute-start(bf16[512,512]{1,0:T(8,128)(2,1)S(1)} %slice.28), channel_id=1, source_target_pairs={{0,64},{1,17},{2,66},{3,19},{4,68},{5,21},{6,70},{7,23},{8,72},{9,... | collective-permute-start | bytes 1572872 | tf_op jit(solution)/shard_map/ppermute | solution.py:42
  97.9 16.3 %collective-permute-start.31 = (bf16[512,512]{1,0:T(8,128)(2,1)S(1)}, bf16[512,512]{1,0:T(8,128)(2,1)S(1)}, u32[]{:S(2)}, u32[]{:S(2)}) collective-permute-start(bf16[512,512]{1,0:T(8,128)(2,1)S(1)} %slice.29), channel_id=1, source_target_pairs={{0,192},{1,49},{2,194},{3,51},{4,196},{5,53},{6,198},{7,55},{8,200... | collective-permute-start | bytes 1572872 | tf_op jit(solution)/shard_map/ppermute | solution.py:42
  108.7 11.2 %collective-permute-start.32 = (bf16[512,512]{1,0:T(8,128)(2,1)S(1)}, bf16[512,512]{1,0:T(8,128)(2,1)S(1)}, u32[]{:S(2)}, u32[]{:S(2)}) collective-permute-start(bf16[512,512]{1,0:T(8,128)(2,1)S(1)} %slice.30), channel_id=1, source_target_pairs={{0,64},{1,17},{2,66},{3,19},{4,68},{5,21},{6,70},{7,23},{8,72},{9,... | collective-permute-start | bytes 1572872 | tf_op jit(solution)/shard_map/ppermute | solution.py:42
  109.2 10.7 %collective-permute-start.33 = (bf16[512,512]{1,0:T(8,128)(2,1)S(1)}, bf16[512,512]{1,0:T(8,128)(2,1)S(1)}, u32[]{:S(2)}, u32[]{:S(2)}) collective-permute-start(bf16[512,512]{1,0:T(8,128)(2,1)S(1)} %slice.31), channel_id=1, source_target_pairs={{0,192},{1,49},{2,194},{3,51},{4,196},{5,53},{6,198},{7,55},{8,200... | collective-permute-start | bytes 1572872 | tf_op jit(solution)/shard_map/ppermute | solution.py:42

commit v5 on v4

--- a/solution.py
+++ b/solution.py
@@ -128,19 +128,22 @@
 
 
 def middle_kernel(places, where_ref, panel_ref, sum_ref, *refs):
-    keep_ref, out_ref = refs[-2:]
-    total = sum_ref[...] + total_of(panel_ref, refs[:-2], places)
+    keep_ref, top_ref, low_ref = refs[-3:]
+    total = sum_ref[...] + total_of(panel_ref, refs[:-3], places)
     total = keep_ref[...].astype(F32) * total
     diagonal = (lax.broadcasted_iota(jnp.int32, total.shape, 0) + where_ref[2 * TILES]
                 == lax.broadcasted_iota(jnp.int32, total.shape, 1))
-    out_ref[...] = (jnp.where(diagonal, 1.5, 0.0) - 0.5 * total).astype(BF16)
+    out = (jnp.where(diagonal, 1.5, 0.0) - 0.5 * total).astype(BF16)
+    half = top_ref.shape[0]
+    top_ref[...], low_ref[...] = out[:half, :], out[half:, :]
 
 
 def finish_middle(where, panel, begun, rights, places, keep):
+    half = jax.ShapeDtypeStruct((keep.shape[0] // 2, keep.shape[1]), BF16)
     return pl.pallas_call(
         functools.partial(middle_kernel, places),
-        in_specs=[SMEM] + [VMEM] * (3 + len(rights)), out_specs=VMEM,
-        out_shape=jax.ShapeDtypeStruct(keep.shape, BF16),
+        in_specs=[SMEM] + [VMEM] * (3 + len(rights)), out_specs=[VMEM, VMEM],
+        out_shape=[half, half],
         compiler_params=LARGE, cost_estimate=cost(2, panel, rights[0]), name="middle",
     )(where, panel, begun, *rights, keep)
 
@@ -182,17 +185,19 @@
     return lax.optimization_barrier(arrays)
 
 
-def gather(block):
-    f1, f3 = around(block, first_axis)
-    near = join(block, f1)
+def gather(top, low):
+    size = 2 * top.shape[0]
+    f1_top, f3_low = send(top, first_axis(1)), send(low, first_axis(3))
+    f1_low, f3_top = send(low, first_axis(1)), send(top, first_axis(3))
+    f2_top, f2_low = send(f1_top, first_axis(1)), send(f3_low, first_axis(3))
+    near = join(top, low, f1_top, f1_low)
     near1, near3 = together(*around(near, second_axis))
-    far = join(f3, *opposite(f1, f3, first_axis))
+    far = join(f3_top, f3_low, f2_top, f2_low)
     near2 = opposite(near1, near3, second_axis)
     far1, far3 = together(*around(far, second_axis))
-    half = block.shape[0]
     early = [near, far, near1, far1, near3, far3, *near2]
-    places = [(0, 0), (1, 0), (2, 0), (3, 0), (6, 0), (7, 0), (4, 0), (4, half)]
-    return early, places, opposite(far1, far3, second_axis), [(5, 0), (5, half)]
+    places = [(0, 0), (1, 0), (2, 0), (3, 0), (6, 0), (7, 0), (4, 0), (4, size)]
+    return early, places, opposite(far1, far3, second_axis), [(5, 0), (5, size)]
 
 
 def local(matrix, pattern):
@@ -234,8 +239,8 @@
     panel = arrange(where, own + other + swapped)
     begun = begin(panel, [full, full1, full3], [(0, 0), (2, 0), (6, 0)])
     begun, *late = together(begun, *late)
-    middle = finish_middle(where, panel, begun, late, [(4, 0), (5, 0)], keep)
-    early, places, late, late_places = gather(middle)
+    top, low = finish_middle(where, panel, begun, late, [(4, 0), (5, 0)], keep)
+    early, places, late, late_places = gather(top, low)
     return finish_last(panel, begin(panel, early, places), late, late_places, keep)
 
 

time: 123 us -> 122 us (level)
  the two profiles are of different devices: /device:TPU:1 before, /device:TPU:120 now
where the time goes in v5:
time: 122 us
  waiting for transfers between devices  65.8 us (54%)
  starting transfers between devices  41.1 us (34%)
  Pallas kernels  12.5 us (10%)
  local copies, waits for them, and re-layouts  2.11 us (2%)
    ppermute x36, waiting for transfers between devices, send(): return lax.ppermute(block, AXES, pairs)  65.8 us
    ppermute x36, starting transfers between devices, send(): return lax.ppermute(block, AXES, pairs)  41.1 us
    pallas_call x2, Pallas kernels, begin(): pl.pallas_call(functools.partial(begin_kernel, places), in_specs=[VMEM] *...  7.34 us
  transfers between devices with their start and end apart: 36, of which 23 were waited for; matrix products, arithmetic and copies ran while one was open for 0% of the time, Pallas kernels for 7%

profile of v5, /device:TPU:120, one launch (start us, length us, event | category | flops | bytes accessed | tf_op | source)
XLA Modules:
  0.0 121.8 jit_solution(13395297308341703165)
XLA Ops:
  0.0 0.1 stack.135.where_ref
  0.1 1.0 copy-done
  1.2 0.7 copy-done.1
  1.8 0.4 mask.1
  2.2 0.1 collective-permute-start.1
  2.3 3.2 %collective-permute-start = (bf16[512,512]{1,0:T(8,128)(2,1)S(1)}, bf16[512,512]{1,0:T(8,128)(2,1)S(1)}, u32[]{:S(2)}, u32[]{:S(2)}) collective-permute-start(bf16[512,512]{1,0:T(8,128)(2,1)S(1)} %get-tuple-element.31.refs_0_), channel_id=1, source_target_pairs={{0,2},{1,15},{2,4},{3,1},{4,6},{5,3},{6,8},{7,5},{8,10},{9,7},{10,... | collective-permute-start | bytes 1572872 | tf_op jit(solution)/shard_map/ppermute | solution.py:42
  5.5 1.5 %collective-permute-start.3 = (bf16[512,512]{1,0:T(8,128)(2,1)S(1)}, bf16[512,512]{1,0:T(8,128)(2,1)S(1)}, u32[]{:S(2)}, u32[]{:S(2)}) collective-permute-start(bf16[512,512]{1,0:T(8,128)(2,1)S(1)} %get-tuple-element.31.refs_0_), channel_id=1, source_target_pairs={{0,16},{1,65},{2,18},{3,67},{4,20},{5,69},{6,22},{7,71},{8,24},{9,... | collective-permute-start | bytes 1572872 | tf_op jit(solution)/shard_map/ppermute | solution.py:42
  7.0 1.7 %collective-permute-start.4 = (bf16[512,512]{1,0:T(8,128)(2,1)S(1)}, bf16[512,512]{1,0:T(8,128)(2,1)S(1)}, u32[]{:S(2)}, u32[]{:S(2)}) collective-permute-start(bf16[512,512]{1,0:T(8,128)(2,1)S(1)} %get-tuple-element.31.refs_0_), channel_id=1, source_target_pairs={{0,48},{1,193},{2,50},{3,195},{4,52},{5,197},{6,54},{7,199},{8,56}... | collective-permute-start | bytes 1572872 | tf_op jit(solution)/shard_map/ppermute | solution.py:42
  8.8 1.8 %collective-permute-start.5 = (bf16[512,512]{1,0:T(8,128)(2,1)S(1)}, bf16[512,512]{1,0:T(8,128)(2,1)S(1)}, u32[]{:S(2)}, u32[]{:S(2)}) collective-permute-start(bf16[512,512]{1,0:T(8,128)(2,1)S(1)} %get-tuple-element.31.refs_0_), channel_id=1, source_target_pairs={{0,32},{1,129},{2,34},{3,131},{4,36},{5,133},{6,38},{7,135},{8,40}... | collective-permute-start | bytes 1572872 | tf_op jit(solution)/shard_map/ppermute | solution.py:42
  10.6 1.0 collective-permute-start.2
  11.6 0.6 collective-permute-done.refs_1_
  12.2 3.7 %collective-permute-done.3.refs_1_ = bf16[512,512]{1,0:T(8,128)(2,1)S(1)} collective-permute-done((bf16[512,512]{1,0:T(8,128)(2,1)S(1)}, bf16[512,512]{1,0:T(8,128)(2,1)S(1)}, u32[]{:S(2)}, u32[]{:S(2)}) %collective-permute-start.3) | collective-permute-done | bytes 524320 | tf_op jit(solution)/shard_map/ppermute | solution.py:42
  15.9 5.2 %collective-permute-done.4.refs_2_ = bf16[512,512]{1,0:T(8,128)(2,1)S(1)} collective-permute-done((bf16[512,512]{1,0:T(8,128)(2,1)S(1)}, bf16[512,512]{1,0:T(8,128)(2,1)S(1)}, u32[]{:S(2)}, u32[]{:S(2)}) %collective-permute-start.4) | collective-permute-done | bytes 524320 | tf_op jit(solution)/shard_map/ppermute | solution.py:42
  21.1 1.4 %collective-permute-done.5.refs_3_ = bf16[512,512]{1,0:T(8,128)(2,1)S(1)} collective-permute-done((bf16[512,512]{1,0:T(8,128)(2,1)S(1)}, bf16[512,512]{1,0:T(8,128)(2,1)S(1)}, u32[]{:S(2)}, u32[]{:S(2)}) %collective-permute-start.5) | collective-permute-done | bytes 524320 | tf_op jit(solution)/shard_map/ppermute | solution.py:42
  22.6 0.1 join.3.refs_0_
  22.7 0.3 collective-permute-start.18
  23.0 1.8 %collective-permute-start.19 = (bf16[2048,512]{1,0:T(8,128)(2,1)S(1)}, bf16[2048,512]{1,0:T(8,128)(2,1)S(1)}, u32[]{:S(2)}, u32[]{:S(2)}) collective-permute-start(bf16[2048,512]{1,0:T(8,128)(2,1)S(1)} %join.3.refs_0_), channel_id=1, source_target_pairs={{0,192},{1,49},{2,194},{3,51},{4,196},{5,53},{6,198},{7,55},{8,200... | collective-permute-start | bytes 6291464 | tf_op jit(solution)/shard_map/ppermute | solution.py:42
  24.8 1.0 collective-permute-start.6
  25.8 1.0 collective-permute-start.11
  26.8 7.2 %collective-permute-done.6.refs_2_ = bf16[512,512]{1,0:T(8,128)(2,1)S(1)} collective-permute-done((bf16[512,512]{1,0:T(8,128)(2,1)S(1)}, bf16[512,512]{1,0:T(8,128)(2,1)S(1)}, u32[]{:S(2)}, u32[]{:S(2)}) %collective-permute-start.6) | collective-permute-done | bytes 524320 | tf_op jit(solution)/shard_map/ppermute | solution.py:42
  34.0 2.2 %collective-permute-start.8 = (bf16[512,512]{1,0:T(8,128)(2,1)S(1)}, bf16[512,512]{1,0:T(8,128)(2,1)S(1)}, u32[]{:S(2)}, u32[]{:S(2)}) collective-permute-start(bf16[512,512]{1,0:T(8,128)(2,1)S(1)} %collective-permute-done.6.refs_2_), channel_id=1, source_target_pairs={{0,2},{1,15},{2,4},{3,1},{4,6},{5,3},{6,8},{7,5},{8,10},{9,7},{10,... | collective-permute-start | bytes 1572872 | tf_op jit(solution)/shard_map/ppermute | solution.py:42
  36.2 3.4 %collective-permute-done.11.refs_7_ = bf16[512,512]{1,0:T(8,128)(2,1)S(1)} collective-permute-done((bf16[512,512]{1,0:T(8,128)(2,1)S(1)}, bf16[512,512]{1,0:T(8,128)(2,1)S(1)}, u32[]{:S(2)}, u32[]{:S(2)}) %collective-permute-start.11) | collective-permute-done | bytes 524320 | tf_op jit(solution)/shard_map/ppermute | solution.py:42
  39.6 2.2 %collective-permute-start.13 = (bf16[512,512]{1,0:T(8,128)(2,1)S(1)}, bf16[512,512]{1,0:T(8,128)(2,1)S(1)}, u32[]{:S(2)}, u32[]{:S(2)}) collective-permute-start(bf16[512,512]{1,0:T(8,128)(2,1)S(1)} %collective-permute-done.11.refs_7_), channel_id=1, source_target_pairs={{0,2},{1,15},{2,4},{3,1},{4,6},{5,3},{6,8},{7,5},{8,10},{9,7},{10,... | collective-permute-start | bytes 1572872 | tf_op jit(solution)/shard_map/ppermute | solution.py:42
  41.8 3.4 %collective-permute-done.8.refs_3_ = bf16[512,512]{1,0:T(8,128)(2,1)S(1)} collective-permute-done((bf16[512,512]{1,0:T(8,128)(2,1)S(1)}, bf16[512,512]{1,0:T(8,128)(2,1)S(1)}, u32[]{:S(2)}, u32[]{:S(2)}) %collective-permute-start.8) | collective-permute-done | bytes 524320 | tf_op jit(solution)/shard_map/ppermute | solution.py:42
  45.2 2.2 %collective-permute-start.10 = (bf16[512,512]{1,0:T(8,128)(2,1)S(1)}, bf16[512,512]{1,0:T(8,128)(2,1)S(1)}, u32[]{:S(2)}, u32[]{:S(2)}) collective-permute-start(bf16[512,512]{1,0:T(8,128)(2,1)S(1)} %collective-permute-done.8.refs_3_), channel_id=1, source_target_pairs={{0,2},{1,15},{2,4},{3,1},{4,6},{5,3},{6,8},{7,5},{8,10},{9,7},{10,... | collective-permute-start | bytes 1572872 | tf_op jit(solution)/shard_map/ppermute | solution.py:42
  47.5 1.4 %collective-permute-done.18.refs_1_ = bf16[2048,512]{1,0:T(8,128)(2,1)S(1)} collective-permute-done((bf16[2048,512]{1,0:T(8,128)(2,1)S(1)}, bf16[2048,512]{1,0:T(8,128)(2,1)S(1)}, u32[]{:S(2)}, u32[]{:S(2)}) %collective-permute-start.18) | collective-permute-done | bytes 2097184 | tf_op jit(solution)/shard_map/ppermute | solution.py:42
  48.8 0.1 slice.24
  48.9 1.5 %collective-permute-start.20 = (bf16[1024,512]{1,0:T(8,128)(2,1)S(1)}, bf16[1024,512]{1,0:T(8,128)(2,1)S(1)}, u32[]{:S(2)}, u32[]{:S(2)}) collective-permute-start(bf16[1024,512]{1,0:T(8,128)(2,1)S(1)} %slice.24), channel_id=1, source_target_pairs={{0,64},{1,17},{2,66},{3,19},{4,68},{5,21},{6,70},{7,23},{8,72},{9,... | collective-permute-start | bytes 3145736 | tf_op jit(solution)/shard_map/ppermute | solution.py:42
  50.5 0.7 collective-permute-start.21
  51.2 0.5 collective-permute-start.17
  51.7 4.8 %collective-permute-done.10.refs_4_ = bf16[512,512]{1,0:T(8,128)(2,1)S(1)} collective-permute-done((bf16[512,512]{1,0:T(8,128)(2,1)S(1)}, bf16[512,512]{1,0:T(8,128)(2,1)S(1)}, u32[]{:S(2)}, u32[]{:S(2)}) %collective-permute-start.10) | collective-permute-done | bytes 524320 | tf_op jit(solution)/shard_map/ppermute | solution.py:42
  56.5 1.9 %collective-permute-done.15.refs_12_ = bf16[512,512]{1,0:T(8,128)(2,1)S(1)} collective-permute-done((bf16[512,512]{1,0:T(8,128)(2,1)S(1)}, bf16[512,512]{1,0:T(8,128)(2,1)S(1)}, u32[]{:S(2)}, u32[]{:S(2)}) %collective-permute-start.15) | collective-permute-done | bytes 524320 | tf_op jit(solution)/shard_map/ppermute | solution.py:42
  58.4 1.2 arrange.1.panel_ref
  59.6 3.4 %begin.2.sum_ref = f32[512,512]{1,0:T(8,128)S(1)} custom-call(bf16[8,512,1024]{2,1,0:T(8,128)(2,1)S(1)} %arrange.1.panel_ref, bf16[2048,512]{1,0:T(8,128)(2,1)S(1)} %join.3.refs_0_, bf16[2048,512]{1,0:T(8,128)(2,1)S(1)} %collective-permute-done.18.refs_1_, bf16[2048,512]{1,0:T(8,128)(2,1)S(1)} %collective-permute-done.19.refs_2_), custom_call_target="tpu_custom_call" | custom-call | tf_op jit(solution)/shard_map/begin/pallas_call | solution.py:123
  63.0 0.8 collective-permute-done.20.refs_0_
  63.8 2.8 %collective-permute-done.21.refs_1_ = bf16[1024,512]{1,0:T(8,128)(2,1)S(1)} collective-permute-done((bf16[1024,512]{1,0:T(8,128)(2,1)S(1)}, bf16[1024,512]{1,0:T(8,128)(2,1)S(1)}, u32[]{:S(2)}, u32[]{:S(2)}) %collective-permute-start.21) | collective-permute-done | bytes 1048608 | tf_op jit(solution)/shard_map/ppermute | solution.py:42
  66.5 1.9 %middle.1 = (bf16[256,512]{1,0:T(8,128)(2,1)S(1)}, bf16[256,512]{1,0:T(8,128)(2,1)S(1)}) custom-call(s32[33]{0:T(128)S(1)} %stack.135.where_ref, bf16[8,512,1024]{2,1,0:T(8,128)(2,1)S(1)} %arrange.1.panel_ref, f32[512,512]{1,0:T(8,128)S(1)} %begin.2.sum_ref, bf16[1024,512]{1,0:T(8,128)(2,1)S(1)} %collective-permute-done.20.refs_0_, ...), custom_call_target="tpu_custom_call" | custom-call | flops 1073741824 | bytes 4194304 | tf_op jit(solution)/shard_map/middle/pallas_call | solution.py:143
  68.4 1.5 %collective-permute-start.22 = (bf16[256,512]{1,0:T(8,128)(2,1)S(1)}, bf16[256,512]{1,0:T(8,128)(2,1)S(1)}, u32[]{:S(2)}, u32[]{:S(2)}) collective-permute-start(bf16[256,512]{1,0:T(8,128)(2,1)S(1)} %get-tuple-element.47.refs_0_), channel_id=1, source_target_pairs={{0,16},{1,65},{2,18},{3,67},{4,20},{5,69},{6,22},{7,71},{8,24},{9,... | collective-permute-start | bytes 786440 | tf_op jit(solution)/shard_map/ppermute | solution.py:42
  69.9 1.8 %collective-permute-start.25 = (bf16[256,512]{1,0:T(8,128)(2,1)S(1)}, bf16[256,512]{1,0:T(8,128)(2,1)S(1)}, u32[]{:S(2)}, u32[]{:S(2)}) collective-permute-start(bf16[256,512]{1,0:T(8,128)(2,1)S(1)} %get-tuple-element.48.refs_1_), channel_id=1, source_target_pairs={{0,48},{1,193},{2,50},{3,195},{4,52},{5,197},{6,54},{7,199},{8,56}... | collective-permute-start | bytes 786440 | tf_op jit(solution)/shard_map/ppermute | solution.py:42
  71.8 0.2 collective-permute-start.23
  72.0 3.0 %collective-permute-start.24 = (bf16[256,512]{1,0:T(8,128)(2,1)S(1)}, bf16[256,512]{1,0:T(8,128)(2,1)S(1)}, u32[]{:S(2)}, u32[]{:S(2)}) collective-permute-start(bf16[256,512]{1,0:T(8,128)(2,1)S(1)} %get-tuple-element.47.refs_0_), channel_id=1, source_target_pairs={{0,48},{1,193},{2,50},{3,195},{4,52},{5,197},{6,54},{7,199},{8,56}... | collective-permute-start | bytes 786440 | tf_op jit(solution)/shard_map/ppermute | solution.py:42
  75.0 1.1 collective-permute-done.22.refs_2_
  76.1 0.2 collective-permute-start.26
  76.3 3.0 %collective-permute-start.27 = (bf16[256,512]{1,0:T(8,128)(2,1)S(1)}, bf16[256,512]{1,0:T(8,128)(2,1)S(1)}, u32[]{:S(2)}, u32[]{:S(2)}) collective-permute-start(bf16[256,512]{1,0:T(8,128)(2,1)S(1)} %collective-permute-done.25.refs_1_), channel_id=1, source_target_pairs={{0,48},{1,193},{2,50},{3,195},{4,52},{5,197},{6,54},{7,199},{8,56}... | collective-permute-start | bytes 786440 | tf_op jit(solution)/shard_map/ppermute | solution.py:42
  79.3 1.9 %collective-permute-done.23.refs_3_ = bf16[256,512]{1,0:T(8,128)(2,1)S(1)} collective-permute-done((bf16[256,512]{1,0:T(8,128)(2,1)S(1)}, bf16[256,512]{1,0:T(8,128)(2,1)S(1)}, u32[]{:S(2)}, u32[]{:S(2)}) %collective-permute-start.23) | collective-permute-done | bytes 262176 | tf_op jit(solution)/shard_map/ppermute | solution.py:42
  81.4 0.1 collective-permute-start.28
  81.4 2.0 %collective-permute-start.29 = (bf16[1024,512]{1,0:T(8,128)(2,1)S(1)}, bf16[1024,512]{1,0:T(8,128)(2,1)S(1)}, u32[]{:S(2)}, u32[]{:S(2)}) collective-permute-start(bf16[1024,512]{1,0:T(8,128)(2,1)S(1)} %join.4.refs_0_), channel_id=1, source_target_pairs={{0,192},{1,49},{2,194},{3,51},{4,196},{5,53},{6,198},{7,55},{8,200... | collective-permute-start | bytes 3145736 | tf_op jit(solution)/shard_map/ppermute | solution.py:42
  83.5 3.4 %collective-permute-done.26.refs_2_ = bf16[256,512]{1,0:T(8,128)(2,1)S(1)} collective-permute-done((bf16[256,512]{1,0:T(8,128)(2,1)S(1)}, bf16[256,512]{1,0:T(8,128)(2,1)S(1)}, u32[]{:S(2)}, u32[]{:S(2)}) %collective-permute-start.26) | collective-permute-done | bytes 262176 | tf_op jit(solution)/shard_map/ppermute | solution.py:42
  87.0 0.1 collective-permute-start.30
  87.1 2.0 %collective-permute-start.31 = (bf16[1024,512]{1,0:T(8,128)(2,1)S(1)}, bf16[1024,512]{1,0:T(8,128)(2,1)S(1)}, u32[]{:S(2)}, u32[]{:S(2)}) collective-permute-start(bf16[1024,512]{1,0:T(8,128)(2,1)S(1)} %join.5.refs_1_), channel_id=1, source_target_pairs={{0,192},{1,49},{2,194},{3,51},{4,196},{5,53},{6,198},{7,55},{8,200... | collective-permute-start | bytes 3145736 | tf_op jit(solution)/shard_map/ppermute | solution.py:42
  89.1 7.2 %collective-permute-done.28.refs_2_ = bf16[1024,512]{1,0:T(8,128)(2,1)S(1)} collective-permute-done((bf16[1024,512]{1,0:T(8,128)(2,1)S(1)}, bf16[1024,512]{1,0:T(8,128)(2,1)S(1)}, u32[]{:S(2)}, u32[]{:S(2)}) %collective-permute-start.28) | collective-permute-done | bytes 1048608 | tf_op jit(solution)/shard_map/ppermute | solution.py:42
  96.2 1.5 %collective-permute-done.29.refs_4_ = bf16[1024,512]{1,0:T(8,128)(2,1)S(1)} collective-permute-done((bf16[1024,512]{1,0:T(8,128)(2,1)S(1)}, bf16[1024,512]{1,0:T(8,128)(2,1)S(1)}, u32[]{:S(2)}, u32[]{:S(2)}) %collective-permute-start.29) | collective-permute-done | bytes 1048608 | tf_op jit(solution)/shard_map/ppermute | solution.py:42
  97.8 0.1 collective-permute-start.32
  97.9 2.1 %collective-permute-start.33 = (bf16[512,512]{1,0:T(8,128)(2,1)S(1)}, bf16[512,512]{1,0:T(8,128)(2,1)S(1)}, u32[]{:S(2)}, u32[]{:S(2)}) collective-permute-start(bf16[512,512]{1,0:T(8,128)(2,1)S(1)} %slice.21), channel_id=1, source_target_pairs={{0,192},{1,49},{2,194},{3,51},{4,196},{5,53},{6,198},{7,55},{8,200... | collective-permute-start | bytes 1572872 | tf_op jit(solution)/shard_map/ppermute | solution.py:42
  100.0 7.5 %collective-permute-done.30.refs_3_ = bf16[1024,512]{1,0:T(8,128)(2,1)S(1)} collective-permute-done((bf16[1024,512]{1,0:T(8,128)(2,1)S(1)}, bf16[1024,512]{1,0:T(8,128)(2,1)S(1)}, u32[]{:S(2)}, u32[]{:S(2)}) %collective-permute-start.30) | collective-permute-done | bytes 1048608 | tf_op jit(solution)/shard_map/ppermute | solution.py:42
  107.5 1.5 %collective-permute-done.31.refs_5_ = bf16[1024,512]{1,0:T(8,128)(2,1)S(1)} collective-permute-done((bf16[1024,512]{1,0:T(8,128)(2,1)S(1)}, bf16[1024,512]{1,0:T(8,128)(2,1)S(1)}, u32[]{:S(2)}, u32[]{:S(2)}) %collective-permute-start.31) | collective-permute-done | bytes 1048608 | tf_op jit(solution)/shard_map/ppermute | solution.py:42
  109.0 0.1 collective-permute-start.34
  109.2 2.1 %collective-permute-start.35 = (bf16[512,512]{1,0:T(8,128)(2,1)S(1)}, bf16[512,512]{1,0:T(8,128)(2,1)S(1)}, u32[]{:S(2)}, u32[]{:S(2)}) collective-permute-start(bf16[512,512]{1,0:T(8,128)(2,1)S(1)} %slice.23), channel_id=1, source_target_pairs={{0,192},{1,49},{2,194},{3,51},{4,196},{5,53},{6,198},{7,55},{8,200... | collective-permute-start | bytes 1572872 | tf_op jit(solution)/shard_map/ppermute | solution.py:42
  111.2 1.8 %collective-permute-done.32.refs_6_ = bf16[512,512]{1,0:T(8,128)(2,1)S(1)} collective-permute-done((bf16[512,512]{1,0:T(8,128)(2,1)S(1)}, bf16[512,512]{1,0:T(8,128)(2,1)S(1)}, u32[]{:S(2)}, u32[]{:S(2)}) %collective-permute-start.32) | collective-permute-done | bytes 524320 | tf_op jit(solution)/shard_map/ppermute | solution.py:42
  113.1 1.5 %collective-permute-done.33.refs_7_ = bf16[512,512]{1,0:T(8,128)(2,1)S(1)} collective-permute-done((bf16[512,512]{1,0:T(8,128)(2,1)S(1)}, bf16[512,512]{1,0:T(8,128)(2,1)S(1)}, u32[]{:S(2)}, u32[]{:S(2)}) %collective-permute-start.33) | collective-permute-done | bytes 524320 | tf_op jit(solution)/shard_map/ppermute | solution.py:42
  114.6 3.9 %begin.3.sum_ref = f32[512,512]{1,0:T(8,128)S(1)} custom-call(bf16[8,512,1024]{2,1,0:T(8,128)(2,1)S(1)} %arrange.1.panel_ref, bf16[1024,512]{1,0:T(8,128)(2,1)S(1)} %join.4.refs_0_, bf16[1024,512]{1,0:T(8,128)(2,1)S(1)} %join.5.refs_1_, bf16[1024,512]{1,0:T(8,128)(2,1)S(1)} %collective-permute-done.28.refs_2_, ...), custom_call_target="tpu_custom_call" | custom-call | tf_op jit(solution)/shard_map/begin/pallas_call | solution.py:123
  118.5 0.2 collective-permute-done.34.refs_0_
  118.7 1.5 %collective-permute-done.35.refs_1_ = bf16[512,512]{1,0:T(8,128)(2,1)S(1)} collective-permute-done((bf16[512,512]{1,0:T(8,128)(2,1)S(1)}, bf16[512,512]{1,0:T(8,128)(2,1)S(1)}, u32[]{:S(2)}, u32[]{:S(2)}) %collective-permute-start.35) | collective-permute-done | bytes 524320 | tf_op jit(solution)/shard_map/ppermute | solution.py:42
  120.2 1.4 %last.1 = bf16[512,512]{1,0:T(8,128)(2,1)} custom-call(bf16[8,512,1024]{2,1,0:T(8,128)(2,1)S(1)} %arrange.1.panel_ref, f32[512,512]{1,0:T(8,128)S(1)} %begin.3.sum_ref, bf16[512,512]{1,0:T(8,128)(2,1)S(1)} %collective-permute-done.34.refs_0_, bf16[512,512]{1,0:T(8,128)(2,1)S(1)} %collective-permute-done.35.refs_1_, ...), custom_call_target="tpu_custom_call" | custom-call | flops 536870912 | bytes 2097152 | tf_op jit(solution)/shard_map/last/pallas_call | solution.py:166
  (28 shorter events, 0.4 us)
Async XLA Ops:
  0.1 1.0 copy-start
  1.2 0.7 copy-start.1
  2.2 8.4 %collective-permute-start.1 = (bf16[512,512]{1,0:T(8,128)(2,1)S(1)}, bf16[512,512]{1,0:T(8,128)(2,1)S(1)}, u32[]{:S(2)}, u32[]{:S(2)}) collective-permute-start(bf16[512,512]{1,0:T(8,128)(2,1)S(1)} %get-tuple-element.31.refs_0_), channel_id=1, source_target_pairs={{0,1},{1,0},{2,3},{3,2},{4,5},{5,4},{6,7},{7,6},{8,9},{9,8},{10,11... | collective-permute-start | bytes 1572872 | tf_op jit(solution)/shard_map/ppermute | solution.py:42
  2.3 9.9 %collective-permute-start = (bf16[512,512]{1,0:T(8,128)(2,1)S(1)}, bf16[512,512]{1,0:T(8,128)(2,1)S(1)}, u32[]{:S(2)}, u32[]{:S(2)}) collective-permute-start(bf16[512,512]{1,0:T(8,128)(2,1)S(1)} %get-tuple-element.31.refs_0_), channel_id=1, source_target_pairs={{0,2},{1,15},{2,4},{3,1},{4,6},{5,3},{6,8},{7,5},{8,10},{9,7},{10,... | collective-permute-start | bytes 1572872 | tf_op jit(solution)/shard_map/ppermute | solution.py:42
  5.5 10.4 %collective-permute-start.3 = (bf16[512,512]{1,0:T(8,128)(2,1)S(1)}, bf16[512,512]{1,0:T(8,128)(2,1)S(1)}, u32[]{:S(2)}, u32[]{:S(2)}) collective-permute-start(bf16[512,512]{1,0:T(8,128)(2,1)S(1)} %get-tuple-element.31.refs_0_), channel_id=1, source_target_pairs={{0,16},{1,65},{2,18},{3,67},{4,20},{5,69},{6,22},{7,71},{8,24},{9,... | collective-permute-start | bytes 1572872 | tf_op jit(solution)/shard_map/ppermute | solution.py:42
  7.0 14.1 %collective-permute-start.4 = (bf16[512,512]{1,0:T(8,128)(2,1)S(1)}, bf16[512,512]{1,0:T(8,128)(2,1)S(1)}, u32[]{:S(2)}, u32[]{:S(2)}) collective-permute-start(bf16[512,512]{1,0:T(8,128)(2,1)S(1)} %get-tuple-element.31.refs_0_), channel_id=1, source_target_pairs={{0,48},{1,193},{2,50},{3,195},{4,52},{5,197},{6,54},{7,199},{8,56}... | collective-permute-start | bytes 1572872 | tf_op jit(solution)/shard_map/ppermute | solution.py:42
  8.8 13.8 %collective-permute-start.5 = (bf16[512,512]{1,0:T(8,128)(2,1)S(1)}, bf16[512,512]{1,0:T(8,128)(2,1)S(1)}, u32[]{:S(2)}, u32[]{:S(2)}) collective-permute-start(bf16[512,512]{1,0:T(8,128)(2,1)S(1)} %get-tuple-element.31.refs_0_), channel_id=1, source_target_pairs={{0,32},{1,129},{2,34},{3,131},{4,36},{5,133},{6,38},{7,135},{8,40}... | collective-permute-start | bytes 1572872 | tf_op jit(solution)/shard_map/ppermute | solution.py:42
  10.6 12.0 %collective-permute-start.2 = (bf16[512,512]{1,0:T(8,128)(2,1)S(1)}, bf16[512,512]{1,0:T(8,128)(2,1)S(1)}, u32[]{:S(2)}, u32[]{:S(2)}) collective-permute-start(bf16[512,512]{1,0:T(8,128)(2,1)S(1)} %collective-permute-done.1.refs_5_), channel_id=1, source_target_pairs={{0,2},{1,15},{2,4},{3,1},{4,6},{5,3},{6,8},{7,5},{8,10},{9,7},{10,... | collective-permute-start | bytes 1572872 | tf_op jit(solution)/shard_map/ppermute | solution.py:42
  22.7 26.1 %collective-permute-start.18 = (bf16[2048,512]{1,0:T(8,128)(2,1)S(1)}, bf16[2048,512]{1,0:T(8,128)(2,1)S(1)}, u32[]{:S(2)}, u32[]{:S(2)}) collective-permute-start(bf16[2048,512]{1,0:T(8,128)(2,1)S(1)} %join.3.refs_0_), channel_id=1, source_target_pairs={{0,64},{1,17},{2,66},{3,19},{4,68},{5,21},{6,70},{7,23},{8,72},{9,... | collective-permute-start | bytes 6291464 | tf_op jit(solution)/shard_map/ppermute | solution.py:42
  23.0 27.4 %collective-permute-start.19 = (bf16[2048,512]{1,0:T(8,128)(2,1)S(1)}, bf16[2048,512]{1,0:T(8,128)(2,1)S(1)}, u32[]{:S(2)}, u32[]{:S(2)}) collective-permute-start(bf16[2048,512]{1,0:T(8,128)(2,1)S(1)} %join.3.refs_0_), channel_id=1, source_target_pairs={{0,192},{1,49},{2,194},{3,51},{4,196},{5,53},{6,198},{7,55},{8,200... | collective-permute-start | bytes 6291464 | tf_op jit(solution)/shard_map/ppermute | solution.py:42
  24.8 9.2 %collective-permute-start.6 = (bf16[512,512]{1,0:T(8,128)(2,1)S(1)}, bf16[512,512]{1,0:T(8,128)(2,1)S(1)}, u32[]{:S(2)}, u32[]{:S(2)}) collective-permute-start(bf16[512,512]{1,0:T(8,128)(2,1)S(1)} %collective-permute-done.refs_1_), channel_id=1, source_target_pairs={{0,2},{1,15},{2,4},{3,1},{4,6},{5,3},{6,8},{7,5},{8,10},{9,7},{10,... | collective-permute-start | bytes 1572872 | tf_op jit(solution)/shard_map/ppermute | solution.py:42
  25.8 8.2 %collective-permute-start.7 = (bf16[512,512]{1,0:T(8,128)(2,1)S(1)}, bf16[512,512]{1,0:T(8,128)(2,1)S(1)}, u32[]{:S(2)}, u32[]{:S(2)}) collective-permute-start(bf16[512,512]{1,0:T(8,128)(2,1)S(1)} %collective-permute-done.refs_1_), channel_id=1, source_target_pairs={{0,1},{1,0},{2,3},{3,2},{4,5},{5,4},{6,7},{7,6},{8,9},{9,8},{10,11... | collective-permute-start | bytes 1572872 | tf_op jit(solution)/shard_map/ppermute | solution.py:42
  25.8 13.8 %collective-permute-start.11 = (bf16[512,512]{1,0:T(8,128)(2,1)S(1)}, bf16[512,512]{1,0:T(8,128)(2,1)S(1)}, u32[]{:S(2)}, u32[]{:S(2)}) collective-permute-start(bf16[512,512]{1,0:T(8,128)(2,1)S(1)} %collective-permute-done.2.refs_6_), channel_id=1, source_target_pairs={{0,2},{1,15},{2,4},{3,1},{4,6},{5,3},{6,8},{7,5},{8,10},{9,7},{10,... | collective-permute-start | bytes 1572872 | tf_op jit(solution)/shard_map/ppermute | solution.py:42
  34.0 5.6 %collective-permute-start.12 = (bf16[512,512]{1,0:T(8,128)(2,1)S(1)}, bf16[512,512]{1,0:T(8,128)(2,1)S(1)}, u32[]{:S(2)}, u32[]{:S(2)}) collective-permute-start(bf16[512,512]{1,0:T(8,128)(2,1)S(1)} %collective-permute-done.2.refs_6_), channel_id=1, source_target_pairs={{0,1},{1,0},{2,3},{3,2},{4,5},{5,4},{6,7},{7,6},{8,9},{9,8},{10,11... | collective-permute-start | bytes 1572872 | tf_op jit(solution)/shard_map/ppermute | solution.py:42
  34.0 11.2 %collective-permute-start.8 = (bf16[512,512]{1,0:T(8,128)(2,1)S(1)}, bf16[512,512]{1,0:T(8,128)(2,1)S(1)}, u32[]{:S(2)}, u32[]{:S(2)}) collective-permute-start(bf16[512,512]{1,0:T(8,128)(2,1)S(1)} %collective-permute-done.6.refs_2_), channel_id=1, source_target_pairs={{0,2},{1,15},{2,4},{3,1},{4,6},{5,3},{6,8},{7,5},{8,10},{9,7},{10,... | collective-permute-start | bytes 1572872 | tf_op jit(solution)/shard_map/ppermute | solution.py:42
  39.6 5.6 %collective-permute-start.9 = (bf16[512,512]{1,0:T(8,128)(2,1)S(1)}, bf16[512,512]{1,0:T(8,128)(2,1)S(1)}, u32[]{:S(2)}, u32[]{:S(2)}) collective-permute-start(bf16[512,512]{1,0:T(8,128)(2,1)S(1)} %collective-permute-done.6.refs_2_), channel_id=1, source_target_pairs={{0,1},{1,0},{2,3},{3,2},{4,5},{5,4},{6,7},{7,6},{8,9},{9,8},{10,11... | collective-permute-start | bytes 1572872 | tf_op jit(solution)/shard_map/ppermute | solution.py:42
  39.6 11.5 %collective-permute-start.13 = (bf16[512,512]{1,0:T(8,128)(2,1)S(1)}, bf16[512,512]{1,0:T(8,128)(2,1)S(1)}, u32[]{:S(2)}, u32[]{:S(2)}) collective-permute-start(bf16[512,512]{1,0:T(8,128)(2,1)S(1)} %collective-permute-done.11.refs_7_), channel_id=1, source_target_pairs={{0,2},{1,15},{2,4},{3,1},{4,6},{5,3},{6,8},{7,5},{8,10},{9,7},{10,... | collective-permute-start | bytes 1572872 | tf_op jit(solution)/shard_map/ppermute | solution.py:42
  45.2 5.9 %collective-permute-start.16 = (bf16[512,512]{1,0:T(8,128)(2,1)S(1)}, bf16[512,512]{1,0:T(8,128)(2,1)S(1)}, u32[]{:S(2)}, u32[]{:S(2)}) collective-permute-start(bf16[512,512]{1,0:T(8,128)(2,1)S(1)} %collective-permute-done.11.refs_7_), channel_id=1, source_target_pairs={{0,1},{1,0},{2,3},{3,2},{4,5},{5,4},{6,7},{7,6},{8,9},{9,8},{10,11... | collective-permute-start | bytes 1572872 | tf_op jit(solution)/shard_map/ppermute | solution.py:42
  45.2 11.2 %collective-permute-start.10 = (bf16[512,512]{1,0:T(8,128)(2,1)S(1)}, bf16[512,512]{1,0:T(8,128)(2,1)S(1)}, u32[]{:S(2)}, u32[]{:S(2)}) collective-permute-start(bf16[512,512]{1,0:T(8,128)(2,1)S(1)} %collective-permute-done.8.refs_3_), channel_id=1, source_target_pairs={{0,2},{1,15},{2,4},{3,1},{4,6},{5,3},{6,8},{7,5},{8,10},{9,7},{10,... | collective-permute-start | bytes 1572872 | tf_op jit(solution)/shard_map/ppermute | solution.py:42
  48.9 14.9 %collective-permute-start.20 = (bf16[1024,512]{1,0:T(8,128)(2,1)S(1)}, bf16[1024,512]{1,0:T(8,128)(2,1)S(1)}, u32[]{:S(2)}, u32[]{:S(2)}) collective-permute-start(bf16[1024,512]{1,0:T(8,128)(2,1)S(1)} %slice.24), channel_id=1, source_target_pairs={{0,64},{1,17},{2,66},{3,19},{4,68},{5,21},{6,70},{7,23},{8,72},{9,... | collective-permute-start | bytes 3145736 | tf_op jit(solution)/shard_map/ppermute | solution.py:42
  50.5 16.1 %collective-permute-start.21 = (bf16[1024,512]{1,0:T(8,128)(2,1)S(1)}, bf16[1024,512]{1,0:T(8,128)(2,1)S(1)}, u32[]{:S(2)}, u32[]{:S(2)}) collective-permute-start(bf16[1024,512]{1,0:T(8,128)(2,1)S(1)} %slice.25), channel_id=1, source_target_pairs={{0,192},{1,49},{2,194},{3,51},{4,196},{5,53},{6,198},{7,55},{8,200... | collective-permute-start | bytes 3145736 | tf_op jit(solution)/shard_map/ppermute | solution.py:42
  51.2 5.3 %collective-permute-start.14 = (bf16[512,512]{1,0:T(8,128)(2,1)S(1)}, bf16[512,512]{1,0:T(8,128)(2,1)S(1)}, u32[]{:S(2)}, u32[]{:S(2)}) collective-permute-start(bf16[512,512]{1,0:T(8,128)(2,1)S(1)} %collective-permute-done.8.refs_3_), channel_id=1, source_target_pairs={{0,1},{1,0},{2,3},{3,2},{4,5},{5,4},{6,7},{7,6},{8,9},{9,8},{10,11... | collective-permute-start | bytes 1572872 | tf_op jit(solution)/shard_map/ppermute | solution.py:42
  51.2 5.3 %collective-permute-start.17 = (bf16[512,512]{1,0:T(8,128)(2,1)S(1)}, bf16[512,512]{1,0:T(8,128)(2,1)S(1)}, u32[]{:S(2)}, u32[]{:S(2)}) collective-permute-start(bf16[512,512]{1,0:T(8,128)(2,1)S(1)} %collective-permute-done.13.refs_8_), channel_id=1, source_target_pairs={{0,1},{1,0},{2,3},{3,2},{4,5},{5,4},{6,7},{7,6},{8,9},{9,8},{10,11... | collective-permute-start | bytes 1572872 | tf_op jit(solution)/shard_map/ppermute | solution.py:42
  56.5 1.9 %collective-permute-start.15 = (bf16[512,512]{1,0:T(8,128)(2,1)S(1)}, bf16[512,512]{1,0:T(8,128)(2,1)S(1)}, u32[]{:S(2)}, u32[]{:S(2)}) collective-permute-start(bf16[512,512]{1,0:T(8,128)(2,1)S(1)} %collective-permute-done.10.refs_4_), channel_id=1, source_target_pairs={{0,1},{1,0},{2,3},{3,2},{4,5},{5,4},{6,7},{7,6},{8,9},{9,8},{10,11... | collective-permute-start | bytes 1572872 | tf_op jit(solution)/shard_map/ppermute | solution.py:42
  68.4 7.7 %collective-permute-start.22 = (bf16[256,512]{1,0:T(8,128)(2,1)S(1)}, bf16[256,512]{1,0:T(8,128)(2,1)S(1)}, u32[]{:S(2)}, u32[]{:S(2)}) collective-permute-start(bf16[256,512]{1,0:T(8,128)(2,1)S(1)} %get-tuple-element.47.refs_0_), channel_id=1, source_target_pairs={{0,16},{1,65},{2,18},{3,67},{4,20},{5,69},{6,22},{7,71},{8,24},{9,... | collective-permute-start | bytes 786440 | tf_op jit(solution)/shard_map/ppermute | solution.py:42
  69.9 6.4 %collective-permute-start.25 = (bf16[256,512]{1,0:T(8,128)(2,1)S(1)}, bf16[256,512]{1,0:T(8,128)(2,1)S(1)}, u32[]{:S(2)}, u32[]{:S(2)}) collective-permute-start(bf16[256,512]{1,0:T(8,128)(2,1)S(1)} %get-tuple-element.48.refs_1_), channel_id=1, source_target_pairs={{0,48},{1,193},{2,50},{3,195},{4,52},{5,197},{6,54},{7,199},{8,56}... | collective-permute-start | bytes 786440 | tf_op jit(solution)/shard_map/ppermute | solution.py:42
  71.8 9.5 %collective-permute-start.23 = (bf16[256,512]{1,0:T(8,128)(2,1)S(1)}, bf16[256,512]{1,0:T(8,128)(2,1)S(1)}, u32[]{:S(2)}, u32[]{:S(2)}) collective-permute-start(bf16[256,512]{1,0:T(8,128)(2,1)S(1)} %get-tuple-element.48.refs_1_), channel_id=1, source_target_pairs={{0,16},{1,65},{2,18},{3,67},{4,20},{5,69},{6,22},{7,71},{8,24},{9,... | collective-permute-start | bytes 786440 | tf_op jit(solution)/shard_map/ppermute | solution.py:42
  72.0 11.5 %collective-permute-start.24 = (bf16[256,512]{1,0:T(8,128)(2,1)S(1)}, bf16[256,512]{1,0:T(8,128)(2,1)S(1)}, u32[]{:S(2)}, u32[]{:S(2)}) collective-permute-start(bf16[256,512]{1,0:T(8,128)(2,1)S(1)} %get-tuple-element.47.refs_0_), channel_id=1, source_target_pairs={{0,48},{1,193},{2,50},{3,195},{4,52},{5,197},{6,54},{7,199},{8,56}... | collective-permute-start | bytes 786440 | tf_op jit(solution)/shard_map/ppermute | solution.py:42
  76.1 10.8 %collective-permute-start.26 = (bf16[256,512]{1,0:T(8,128)(2,1)S(1)}, bf16[256,512]{1,0:T(8,128)(2,1)S(1)}, u32[]{:S(2)}, u32[]{:S(2)}) collective-permute-start(bf16[256,512]{1,0:T(8,128)(2,1)S(1)} %collective-permute-done.22.refs_2_), channel_id=1, source_target_pairs={{0,16},{1,65},{2,18},{3,67},{4,20},{5,69},{6,22},{7,71},{8,24},{9,... | collective-permute-start | bytes 786440 | tf_op jit(solution)/shard_map/ppermute | solution.py:42
  76.3 10.6 %collective-permute-start.27 = (bf16[256,512]{1,0:T(8,128)(2,1)S(1)}, bf16[256,512]{1,0:T(8,128)(2,1)S(1)}, u32[]{:S(2)}, u32[]{:S(2)}) collective-permute-start(bf16[256,512]{1,0:T(8,128)(2,1)S(1)} %collective-permute-done.25.refs_1_), channel_id=1, source_target_pairs={{0,48},{1,193},{2,50},{3,195},{4,52},{5,197},{6,54},{7,199},{8,56}... | collective-permute-start | bytes 786440 | tf_op jit(solution)/shard_map/ppermute | solution.py:42
  81.4 14.9 %collective-permute-start.28 = (bf16[1024,512]{1,0:T(8,128)(2,1)S(1)}, bf16[1024,512]{1,0:T(8,128)(2,1)S(1)}, u32[]{:S(2)}, u32[]{:S(2)}) collective-permute-start(bf16[1024,512]{1,0:T(8,128)(2,1)S(1)} %join.4.refs_0_), channel_id=1, source_target_pairs={{0,64},{1,17},{2,66},{3,19},{4,68},{5,21},{6,70},{7,23},{8,72},{9,... | collective-permute-start | bytes 3145736 | tf_op jit(solution)/shard_map/ppermute | solution.py:42
  81.4 16.3 %collective-permute-start.29 = (bf16[1024,512]{1,0:T(8,128)(2,1)S(1)}, bf16[1024,512]{1,0:T(8,128)(2,1)S(1)}, u32[]{:S(2)}, u32[]{:S(2)}) collective-permute-start(bf16[1024,512]{1,0:T(8,128)(2,1)S(1)} %join.4.refs_0_), channel_id=1, source_target_pairs={{0,192},{1,49},{2,194},{3,51},{4,196},{5,53},{6,198},{7,55},{8,200... | collective-permute-start | bytes 3145736 | tf_op jit(solution)/shard_map/ppermute | solution.py:42
  87.0 20.5 %collective-permute-start.30 = (bf16[1024,512]{1,0:T(8,128)(2,1)S(1)}, bf16[1024,512]{1,0:T(8,128)(2,1)S(1)}, u32[]{:S(2)}, u32[]{:S(2)}) collective-permute-start(bf16[1024,512]{1,0:T(8,128)(2,1)S(1)} %join.5.refs_1_), channel_id=1, source_target_pairs={{0,64},{1,17},{2,66},{3,19},{4,68},{5,21},{6,70},{7,23},{8,72},{9,... | collective-permute-start | bytes 3145736 | tf_op jit(solution)/shard_map/ppermute | solution.py:42
  87.1 21.9 %collective-permute-start.31 = (bf16[1024,512]{1,0:T(8,128)(2,1)S(1)}, bf16[1024,512]{1,0:T(8,128)(2,1)S(1)}, u32[]{:S(2)}, u32[]{:S(2)}) collective-permute-start(bf16[1024,512]{1,0:T(8,128)(2,1)S(1)} %join.5.refs_1_), channel_id=1, source_target_pairs={{0,192},{1,49},{2,194},{3,51},{4,196},{5,53},{6,198},{7,55},{8,200... | collective-permute-start | bytes 3145736 | tf_op jit(solution)/shard_map/ppermute | solution.py:42
  97.8 15.3 %collective-permute-start.32 = (bf16[512,512]{1,0:T(8,128)(2,1)S(1)}, bf16[512,512]{1,0:T(8,128)(2,1)S(1)}, u32[]{:S(2)}, u32[]{:S(2)}) collective-permute-start(bf16[512,512]{1,0:T(8,128)(2,1)S(1)} %slice.20), channel_id=1, source_target_pairs={{0,64},{1,17},{2,66},{3,19},{4,68},{5,21},{6,70},{7,23},{8,72},{9,... | collective-permute-start | bytes 1572872 | tf_op jit(solution)/shard_map/ppermute | solution.py:42
  97.9 16.7 %collective-permute-start.33 = (bf16[512,512]{1,0:T(8,128)(2,1)S(1)}, bf16[512,512]{1,0:T(8,128)(2,1)S(1)}, u32[]{:S(2)}, u32[]{:S(2)}) collective-permute-start(bf16[512,512]{1,0:T(8,128)(2,1)S(1)} %slice.21), channel_id=1, source_target_pairs={{0,192},{1,49},{2,194},{3,51},{4,196},{5,53},{6,198},{7,55},{8,200... | collective-permute-start | bytes 1572872 | tf_op jit(solution)/shard_map/ppermute | solution.py:42
  109.0 9.7 %collective-permute-start.34 = (bf16[512,512]{1,0:T(8,128)(2,1)S(1)}, bf16[512,512]{1,0:T(8,128)(2,1)S(1)}, u32[]{:S(2)}, u32[]{:S(2)}) collective-permute-start(bf16[512,512]{1,0:T(8,128)(2,1)S(1)} %slice.22), channel_id=1, source_target_pairs={{0,64},{1,17},{2,66},{3,19},{4,68},{5,21},{6,70},{7,23},{8,72},{9,... | collective-permute-start | bytes 1572872 | tf_op jit(solution)/shard_map/ppermute | solution.py:42
  109.2 11.1 %collective-permute-start.35 = (bf16[512,512]{1,0:T(8,128)(2,1)S(1)}, bf16[512,512]{1,0:T(8,128)(2,1)S(1)}, u32[]{:S(2)}, u32[]{:S(2)}) collective-permute-start(bf16[512,512]{1,0:T(8,128)(2,1)S(1)} %slice.23), channel_id=1, source_target_pairs={{0,192},{1,49},{2,194},{3,51},{4,196},{5,53},{6,198},{7,55},{8,200... | collective-permute-start | bytes 1572872 | tf_op jit(solution)/shard_map/ppermute | solution.py:42

commit v6 on v5

--- a/solution.py
+++ b/solution.py
@@ -125,6 +125,18 @@
         out_shape=jax.ShapeDtypeStruct((panel.shape[1], rights[0].shape[1]), F32),
         compiler_params=LARGE, cost_estimate=cost(0, panel, rights[0]), name="begin",
     )(panel, *rights)
+
+
+def more_kernel(places, panel_ref, sum_ref, *refs):
+    refs[-1][...] = sum_ref[...] + total_of(panel_ref, refs[:-1], places)
+
+
+def more(panel, begun, rights, places):
+    return pl.pallas_call(
+        functools.partial(more_kernel, places), in_specs=[VMEM] * (2 + len(rights)), out_specs=VMEM,
+        out_shape=jax.ShapeDtypeStruct(begun.shape, F32),
+        compiler_params=LARGE, cost_estimate=cost(0, panel, rights[0]), name="more",
+    )(panel, begun, *rights)
 
 
 def middle_kernel(places, where_ref, panel_ref, sum_ref, *refs):
@@ -234,14 +246,17 @@
     other.append(send(other[2], RING))
     own[3], own2 = together(own[3], send(own[2], SWAP))
     own.append(send(own[3], RING))
-    late = opposite(full1, full3, second_axis)
+    late = list(opposite(full1, full3, second_axis))
     swapped = [own1, own2, send(own[3], SWAP), send(own[4], SWAP), other1, send(other[2], SWAP), send(other[3], SWAP)]
     panel = arrange(where, own + other + swapped)
     begun = begin(panel, [full, full1, full3], [(0, 0), (2, 0), (6, 0)])
-    begun, *late = together(begun, *late)
-    top, low = finish_middle(where, panel, begun, late, [(4, 0), (5, 0)], keep)
+    begun, late[0] = together(begun, late[0])
+    begun = more(panel, begun, late[:1], [(4, 0)])
+    begun, late[1] = together(begun, late[1])
+    top, low = finish_middle(where, panel, begun, late[1:], [(5, 0)], keep)
     early, places, late, late_places = gather(top, low)
-    return finish_last(panel, begin(panel, early, places), late, late_places, keep)
+    begun = more(panel, begin(panel, early, places), late[:1], late_places[:1])
+    return finish_last(panel, begun, late[1:], late_places[1:], keep)
 
 
 def solution(mesh):

time: 122 us -> 120 us (0.984)
  the two profiles are of different devices: /device:TPU:120 before, /device:TPU:1 now
where the time goes in v6:
time: 120 us; the launch traced here: 119 us
  waiting for transfers between devices  55.2 us (46%)
  starting transfers between devices  48.3 us (40%)
  Pallas kernels  12.9 us (11%)
  local copies, waits for them, and re-layouts  2.11 us (2%)
    ppermute x36, waiting for transfers between devices, send(): return lax.ppermute(block, AXES, pairs)  55.2 us
    ppermute x36, starting transfers between devices, send(): return lax.ppermute(block, AXES, pairs)  48.3 us
    pallas_call x2, Pallas kernels, begin(): pl.pallas_call(functools.partial(begin_kernel, places), in_specs=[VMEM] *...  7.34 us
  transfers between devices with their start and end apart: 36, of which 17 were waited for; matrix products, arithmetic and copies ran while one was open for 0% of the time, Pallas kernels for 8%

profile of v6, /device:TPU:1, one launch (start us, length us, event | category | flops | bytes accessed | tf_op | source)
XLA Modules:
  0.0 118.9 jit_solution(4750631851107768044)
XLA Ops:
  0.0 0.1 stack.135.where_ref
  0.1 1.0 copy-done
  1.2 0.7 copy-done.1
  1.8 0.4 mask.1
  2.2 3.3 %collective-permute-start.1 = (bf16[512,512]{1,0:T(8,128)(2,1)S(1)}, bf16[512,512]{1,0:T(8,128)(2,1)S(1)}, u32[]{:S(2)}, u32[]{:S(2)}) collective-permute-start(bf16[512,512]{1,0:T(8,128)(2,1)S(1)} %get-tuple-element.32.refs_0_), channel_id=1, source_target_pairs={{0,1},{1,0},{2,3},{3,2},{4,5},{5,4},{6,7},{7,6},{8,9},{9,8},{10,11... | collective-permute-start | bytes 1572872 | tf_op jit(solution)/shard_map/ppermute | solution.py:42
  5.6 3.8 %collective-permute-start = (bf16[512,512]{1,0:T(8,128)(2,1)S(1)}, bf16[512,512]{1,0:T(8,128)(2,1)S(1)}, u32[]{:S(2)}, u32[]{:S(2)}) collective-permute-start(bf16[512,512]{1,0:T(8,128)(2,1)S(1)} %get-tuple-element.32.refs_0_), channel_id=1, source_target_pairs={{0,2},{1,15},{2,4},{3,1},{4,6},{5,3},{6,8},{7,5},{8,10},{9,7},{10,... | collective-permute-start | bytes 1572872 | tf_op jit(solution)/shard_map/ppermute | solution.py:42
  9.4 1.3 %collective-permute-start.3 = (bf16[512,512]{1,0:T(8,128)(2,1)S(1)}, bf16[512,512]{1,0:T(8,128)(2,1)S(1)}, u32[]{:S(2)}, u32[]{:S(2)}) collective-permute-start(bf16[512,512]{1,0:T(8,128)(2,1)S(1)} %get-tuple-element.32.refs_0_), channel_id=1, source_target_pairs={{0,16},{1,65},{2,18},{3,67},{4,20},{5,69},{6,22},{7,71},{8,24},{9,... | collective-permute-start | bytes 1572872 | tf_op jit(solution)/shard_map/ppermute | solution.py:42
  10.7 1.4 %collective-permute-start.4 = (bf16[512,512]{1,0:T(8,128)(2,1)S(1)}, bf16[512,512]{1,0:T(8,128)(2,1)S(1)}, u32[]{:S(2)}, u32[]{:S(2)}) collective-permute-start(bf16[512,512]{1,0:T(8,128)(2,1)S(1)} %get-tuple-element.32.refs_0_), channel_id=1, source_target_pairs={{0,48},{1,193},{2,50},{3,195},{4,52},{5,197},{6,54},{7,199},{8,56}... | collective-permute-start | bytes 1572872 | tf_op jit(solution)/shard_map/ppermute | solution.py:42
  12.1 1.6 %collective-permute-start.5 = (bf16[512,512]{1,0:T(8,128)(2,1)S(1)}, bf16[512,512]{1,0:T(8,128)(2,1)S(1)}, u32[]{:S(2)}, u32[]{:S(2)}) collective-permute-start(bf16[512,512]{1,0:T(8,128)(2,1)S(1)} %get-tuple-element.32.refs_0_), channel_id=1, source_target_pairs={{0,32},{1,129},{2,34},{3,131},{4,36},{5,133},{6,38},{7,135},{8,40}... | collective-permute-start | bytes 1572872 | tf_op jit(solution)/shard_map/ppermute | solution.py:42
  13.8 0.7 collective-permute-start.2
  14.5 1.0 collective-permute-done.refs_1_
  15.5 3.5 %collective-permute-done.3.refs_1_ = bf16[512,512]{1,0:T(8,128)(2,1)S(1)} collective-permute-done((bf16[512,512]{1,0:T(8,128)(2,1)S(1)}, bf16[512,512]{1,0:T(8,128)(2,1)S(1)}, u32[]{:S(2)}, u32[]{:S(2)}) %collective-permute-start.3) | collective-permute-done | bytes 524320 | tf_op jit(solution)/shard_map/ppermute | solution.py:42
  19.0 6.5 %collective-permute-done.5.refs_3_ = bf16[512,512]{1,0:T(8,128)(2,1)S(1)} collective-permute-done((bf16[512,512]{1,0:T(8,128)(2,1)S(1)}, bf16[512,512]{1,0:T(8,128)(2,1)S(1)}, u32[]{:S(2)}, u32[]{:S(2)}) %collective-permute-start.5) | collective-permute-done | bytes 524320 | tf_op jit(solution)/shard_map/ppermute | solution.py:42
  25.5 0.1 join.3.refs_0_
  25.7 1.3 %collective-permute-start.18 = (bf16[2048,512]{1,0:T(8,128)(2,1)S(1)}, bf16[2048,512]{1,0:T(8,128)(2,1)S(1)}, u32[]{:S(2)}, u32[]{:S(2)}) collective-permute-start(bf16[2048,512]{1,0:T(8,128)(2,1)S(1)} %join.3.refs_0_), channel_id=1, source_target_pairs={{0,64},{1,17},{2,66},{3,19},{4,68},{5,21},{6,70},{7,23},{8,72},{9,... | collective-permute-start | bytes 6291464 | tf_op jit(solution)/shard_map/ppermute | solution.py:42
  26.9 1.5 %collective-permute-start.19 = (bf16[2048,512]{1,0:T(8,128)(2,1)S(1)}, bf16[2048,512]{1,0:T(8,128)(2,1)S(1)}, u32[]{:S(2)}, u32[]{:S(2)}) collective-permute-start(bf16[2048,512]{1,0:T(8,128)(2,1)S(1)} %join.3.refs_0_), channel_id=1, source_target_pairs={{0,192},{1,49},{2,194},{3,51},{4,196},{5,53},{6,198},{7,55},{8,200... | collective-permute-start | bytes 6291464 | tf_op jit(solution)/shard_map/ppermute | solution.py:42
  28.4 0.7 collective-permute-start.6
  29.1 1.0 collective-permute-start.11
  30.2 6.6 %collective-permute-done.6.refs_2_ = bf16[512,512]{1,0:T(8,128)(2,1)S(1)} collective-permute-done((bf16[512,512]{1,0:T(8,128)(2,1)S(1)}, bf16[512,512]{1,0:T(8,128)(2,1)S(1)}, u32[]{:S(2)}, u32[]{:S(2)}) %collective-permute-start.6) | collective-permute-done | bytes 524320 | tf_op jit(solution)/shard_map/ppermute | solution.py:42
  36.7 0.7 collective-permute-start.12
  37.5 1.7 %collective-permute-start.8 = (bf16[512,512]{1,0:T(8,128)(2,1)S(1)}, bf16[512,512]{1,0:T(8,128)(2,1)S(1)}, u32[]{:S(2)}, u32[]{:S(2)}) collective-permute-start(bf16[512,512]{1,0:T(8,128)(2,1)S(1)} %collective-permute-done.6.refs_2_), channel_id=1, source_target_pairs={{0,2},{1,15},{2,4},{3,1},{4,6},{5,3},{6,8},{7,5},{8,10},{9,7},{10,... | collective-permute-start | bytes 1572872 | tf_op jit(solution)/shard_map/ppermute | solution.py:42
  39.2 3.1 %collective-permute-done.11.refs_7_ = bf16[512,512]{1,0:T(8,128)(2,1)S(1)} collective-permute-done((bf16[512,512]{1,0:T(8,128)(2,1)S(1)}, bf16[512,512]{1,0:T(8,128)(2,1)S(1)}, u32[]{:S(2)}, u32[]{:S(2)}) %collective-permute-start.11) | collective-permute-done | bytes 524320 | tf_op jit(solution)/shard_map/ppermute | solution.py:42
  42.4 0.7 collective-permute-start.9
  43.1 1.7 %collective-permute-start.13 = (bf16[512,512]{1,0:T(8,128)(2,1)S(1)}, bf16[512,512]{1,0:T(8,128)(2,1)S(1)}, u32[]{:S(2)}, u32[]{:S(2)}) collective-permute-start(bf16[512,512]{1,0:T(8,128)(2,1)S(1)} %collective-permute-done.11.refs_7_), channel_id=1, source_target_pairs={{0,2},{1,15},{2,4},{3,1},{4,6},{5,3},{6,8},{7,5},{8,10},{9,7},{10,... | collective-permute-start | bytes 1572872 | tf_op jit(solution)/shard_map/ppermute | solution.py:42
  44.8 3.1 %collective-permute-done.8.refs_3_ = bf16[512,512]{1,0:T(8,128)(2,1)S(1)} collective-permute-done((bf16[512,512]{1,0:T(8,128)(2,1)S(1)}, bf16[512,512]{1,0:T(8,128)(2,1)S(1)}, u32[]{:S(2)}, u32[]{:S(2)}) %collective-permute-start.8) | collective-permute-done | bytes 524320 | tf_op jit(solution)/shard_map/ppermute | solution.py:42
  48.0 0.7 collective-permute-start.16
  48.7 1.7 %collective-permute-start.10 = (bf16[512,512]{1,0:T(8,128)(2,1)S(1)}, bf16[512,512]{1,0:T(8,128)(2,1)S(1)}, u32[]{:S(2)}, u32[]{:S(2)}) collective-permute-start(bf16[512,512]{1,0:T(8,128)(2,1)S(1)} %collective-permute-done.8.refs_3_), channel_id=1, source_target_pairs={{0,2},{1,15},{2,4},{3,1},{4,6},{5,3},{6,8},{7,5},{8,10},{9,7},{10,... | collective-permute-start | bytes 1572872 | tf_op jit(solution)/shard_map/ppermute | solution.py:42
  50.5 1.7 %collective-permute-done.18.refs_1_ = bf16[2048,512]{1,0:T(8,128)(2,1)S(1)} collective-permute-done((bf16[2048,512]{1,0:T(8,128)(2,1)S(1)}, bf16[2048,512]{1,0:T(8,128)(2,1)S(1)}, u32[]{:S(2)}, u32[]{:S(2)}) %collective-permute-start.18) | collective-permute-done | bytes 2097184 | tf_op jit(solution)/shard_map/ppermute | solution.py:42
  52.2 0.1 collective-permute-start.20
  52.3 0.1 slice.25
  52.4 2.7 %collective-permute-start.21 = (bf16[1024,512]{1,0:T(8,128)(2,1)S(1)}, bf16[1024,512]{1,0:T(8,128)(2,1)S(1)}, u32[]{:S(2)}, u32[]{:S(2)}) collective-permute-start(bf16[1024,512]{1,0:T(8,128)(2,1)S(1)} %slice.25), channel_id=1, source_target_pairs={{0,192},{1,49},{2,194},{3,51},{4,196},{5,53},{6,198},{7,55},{8,200... | collective-permute-start | bytes 3145736 | tf_op jit(solution)/shard_map/ppermute | solution.py:42
  55.1 0.5 collective-permute-start.17
  55.6 3.6 %collective-permute-done.10.refs_4_ = bf16[512,512]{1,0:T(8,128)(2,1)S(1)} collective-permute-done((bf16[512,512]{1,0:T(8,128)(2,1)S(1)}, bf16[512,512]{1,0:T(8,128)(2,1)S(1)}, u32[]{:S(2)}, u32[]{:S(2)}) %collective-permute-start.10) | collective-permute-done | bytes 524320 | tf_op jit(solution)/shard_map/ppermute | solution.py:42
  59.2 0.7 collective-permute-start.15
  60.0 1.5 %collective-permute-done.15.refs_12_ = bf16[512,512]{1,0:T(8,128)(2,1)S(1)} collective-permute-done((bf16[512,512]{1,0:T(8,128)(2,1)S(1)}, bf16[512,512]{1,0:T(8,128)(2,1)S(1)}, u32[]{:S(2)}, u32[]{:S(2)}) %collective-permute-start.15) | collective-permute-done | bytes 524320 | tf_op jit(solution)/shard_map/ppermute | solution.py:42
  61.5 1.2 %arrange.1.panel_ref = bf16[8,512,1024]{2,1,0:T(8,128)(2,1)S(1)} custom-call(s32[33]{0:T(128)S(1)} %stack.135.where_ref, bf16[512,512]{1,0:T(8,128)(2,1)S(1)} %get-tuple-element.32.refs_0_, bf16[512,512]{1,0:T(8,128)(2,1)S(1)} %collective-permute-done.refs_1_, bf16[512,512]{1,0:T(8,128)(2,1)S(1)} %collective-permute-done.6.refs_2_, ...), custom_call_target="tpu_custom_call" | custom-call | tf_op jit(solution)/shard_map/arrange/pallas_call | solution.py:93
  62.7 3.4 %begin.2.sum_ref = f32[512,512]{1,0:T(8,128)S(1)} custom-call(bf16[8,512,1024]{2,1,0:T(8,128)(2,1)S(1)} %arrange.1.panel_ref, bf16[2048,512]{1,0:T(8,128)(2,1)S(1)} %join.3.refs_0_, bf16[2048,512]{1,0:T(8,128)(2,1)S(1)} %collective-permute-done.18.refs_1_, bf16[2048,512]{1,0:T(8,128)(2,1)S(1)} %collective-permute-done.19.refs_2_), custom_call_target="tpu_custom_call" | custom-call | tf_op jit(solution)/shard_map/begin/pallas_call | solution.py:123
  66.1 1.0 collective-permute-done.20.refs_0_
  67.1 0.7 more.2.sum_ref
  67.9 1.4 %middle.1 = (bf16[256,512]{1,0:T(8,128)(2,1)S(1)}, bf16[256,512]{1,0:T(8,128)(2,1)S(1)}) custom-call(s32[33]{0:T(128)S(1)} %stack.135.where_ref, bf16[8,512,1024]{2,1,0:T(8,128)(2,1)S(1)} %arrange.1.panel_ref, f32[512,512]{1,0:T(8,128)S(1)} %more.2.sum_ref, bf16[1024,512]{1,0:T(8,128)(2,1)S(1)} %collective-permute-done.21.refs_0_, ...), custom_call_target="tpu_custom_call" | custom-call | flops 1073741824 | bytes 4194304 | tf_op jit(solution)/shard_map/middle/pallas_call | solution.py:155
  69.2 0.9 collective-permute-start.22
  70.2 1.8 %collective-permute-start.25 = (bf16[256,512]{1,0:T(8,128)(2,1)S(1)}, bf16[256,512]{1,0:T(8,128)(2,1)S(1)}, u32[]{:S(2)}, u32[]{:S(2)}) collective-permute-start(bf16[256,512]{1,0:T(8,128)(2,1)S(1)} %get-tuple-element.50.refs_1_), channel_id=1, source_target_pairs={{0,48},{1,193},{2,50},{3,195},{4,52},{5,197},{6,54},{7,199},{8,56}... | collective-permute-start | bytes 786440 | tf_op jit(solution)/shard_map/ppermute | solution.py:42
  72.0 2.7 %collective-permute-start.24 = (bf16[256,512]{1,0:T(8,128)(2,1)S(1)}, bf16[256,512]{1,0:T(8,128)(2,1)S(1)}, u32[]{:S(2)}, u32[]{:S(2)}) collective-permute-start(bf16[256,512]{1,0:T(8,128)(2,1)S(1)} %get-tuple-element.49.refs_0_), channel_id=1, source_target_pairs={{0,48},{1,193},{2,50},{3,195},{4,52},{5,197},{6,54},{7,199},{8,56}... | collective-permute-start | bytes 786440 | tf_op jit(solution)/shard_map/ppermute | solution.py:42
  74.7 1.2 collective-permute-done.22.refs_2_
  75.9 2.9 %collective-permute-start.27 = (bf16[256,512]{1,0:T(8,128)(2,1)S(1)}, bf16[256,512]{1,0:T(8,128)(2,1)S(1)}, u32[]{:S(2)}, u32[]{:S(2)}) collective-permute-start(bf16[256,512]{1,0:T(8,128)(2,1)S(1)} %collective-permute-done.25.refs_1_), channel_id=1, source_target_pairs={{0,48},{1,193},{2,50},{3,195},{4,52},{5,197},{6,54},{7,199},{8,56}... | collective-permute-start | bytes 786440 | tf_op jit(solution)/shard_map/ppermute | solution.py:42
  78.7 0.1 collective-permute-done.23.refs_3_
  78.9 0.1 join.4.refs_0_
  78.9 0.1 collective-permute-start.28
  79.0 2.7 %collective-permute-start.29 = (bf16[1024,512]{1,0:T(8,128)(2,1)S(1)}, bf16[1024,512]{1,0:T(8,128)(2,1)S(1)}, u32[]{:S(2)}, u32[]{:S(2)}) collective-permute-start(bf16[1024,512]{1,0:T(8,128)(2,1)S(1)} %join.4.refs_0_), channel_id=1, source_target_pairs={{0,192},{1,49},{2,194},{3,51},{4,196},{5,53},{6,198},{7,55},{8,200... | collective-permute-start | bytes 3145736 | tf_op jit(solution)/shard_map/ppermute | solution.py:42
  81.7 0.9 collective-permute-done.26.refs_2_
  82.6 0.1 join.5.refs_1_
  82.7 0.1 collective-permute-start.30
  82.7 2.7 %collective-permute-start.31 = (bf16[1024,512]{1,0:T(8,128)(2,1)S(1)}, bf16[1024,512]{1,0:T(8,128)(2,1)S(1)}, u32[]{:S(2)}, u32[]{:S(2)}) collective-permute-start(bf16[1024,512]{1,0:T(8,128)(2,1)S(1)} %join.5.refs_1_), channel_id=1, source_target_pairs={{0,192},{1,49},{2,194},{3,51},{4,196},{5,53},{6,198},{7,55},{8,200... | collective-permute-start | bytes 3145736 | tf_op jit(solution)/shard_map/ppermute | solution.py:42
  85.4 9.3 %collective-permute-done.28.refs_2_ = bf16[1024,512]{1,0:T(8,128)(2,1)S(1)} collective-permute-done((bf16[1024,512]{1,0:T(8,128)(2,1)S(1)}, bf16[1024,512]{1,0:T(8,128)(2,1)S(1)}, u32[]{:S(2)}, u32[]{:S(2)}) %collective-permute-start.28) | collective-permute-done | bytes 1048608 | tf_op jit(solution)/shard_map/ppermute | solution.py:42
  94.7 0.1 collective-permute-start.32
  94.8 3.0 %collective-permute-start.33 = (bf16[512,512]{1,0:T(8,128)(2,1)S(1)}, bf16[512,512]{1,0:T(8,128)(2,1)S(1)}, u32[]{:S(2)}, u32[]{:S(2)}) collective-permute-start(bf16[512,512]{1,0:T(8,128)(2,1)S(1)} %slice.21), channel_id=1, source_target_pairs={{0,192},{1,49},{2,194},{3,51},{4,196},{5,53},{6,198},{7,55},{8,200... | collective-permute-start | bytes 1572872 | tf_op jit(solution)/shard_map/ppermute | solution.py:42
  97.9 8.0 %collective-permute-done.30.refs_3_ = bf16[1024,512]{1,0:T(8,128)(2,1)S(1)} collective-permute-done((bf16[1024,512]{1,0:T(8,128)(2,1)S(1)}, bf16[1024,512]{1,0:T(8,128)(2,1)S(1)}, u32[]{:S(2)}, u32[]{:S(2)}) %collective-permute-start.30) | collective-permute-done | bytes 1048608 | tf_op jit(solution)/shard_map/ppermute | solution.py:42
  105.9 0.1 collective-permute-start.34
  106.1 3.0 %collective-permute-start.35 = (bf16[512,512]{1,0:T(8,128)(2,1)S(1)}, bf16[512,512]{1,0:T(8,128)(2,1)S(1)}, u32[]{:S(2)}, u32[]{:S(2)}) collective-permute-start(bf16[512,512]{1,0:T(8,128)(2,1)S(1)} %slice.23), channel_id=1, source_target_pairs={{0,192},{1,49},{2,194},{3,51},{4,196},{5,53},{6,198},{7,55},{8,200... | collective-permute-start | bytes 1572872 | tf_op jit(solution)/shard_map/ppermute | solution.py:42
  109.1 2.4 %collective-permute-done.32.refs_6_ = bf16[512,512]{1,0:T(8,128)(2,1)S(1)} collective-permute-done((bf16[512,512]{1,0:T(8,128)(2,1)S(1)}, bf16[512,512]{1,0:T(8,128)(2,1)S(1)}, u32[]{:S(2)}, u32[]{:S(2)}) %collective-permute-start.32) | collective-permute-done | bytes 524320 | tf_op jit(solution)/shard_map/ppermute | solution.py:42
  111.5 3.9 %begin.3.sum_ref = f32[512,512]{1,0:T(8,128)S(1)} custom-call(bf16[8,512,1024]{2,1,0:T(8,128)(2,1)S(1)} %arrange.1.panel_ref, bf16[1024,512]{1,0:T(8,128)(2,1)S(1)} %join.4.refs_0_, bf16[1024,512]{1,0:T(8,128)(2,1)S(1)} %join.5.refs_1_, bf16[1024,512]{1,0:T(8,128)(2,1)S(1)} %collective-permute-done.28.refs_2_, ...), custom_call_target="tpu_custom_call" | custom-call | tf_op jit(solution)/shard_map/begin/pallas_call | solution.py:123
  115.5 1.7 %collective-permute-done.34.refs_0_ = bf16[512,512]{1,0:T(8,128)(2,1)S(1)} collective-permute-done((bf16[512,512]{1,0:T(8,128)(2,1)S(1)}, bf16[512,512]{1,0:T(8,128)(2,1)S(1)}, u32[]{:S(2)}, u32[]{:S(2)}) %collective-permute-start.34) | collective-permute-done | bytes 524320 | tf_op jit(solution)/shard_map/ppermute | solution.py:42
  117.1 0.4 more.3.sum_ref
  117.6 1.2 last.1
  (30 shorter events, 0.3 us)
Async XLA Ops:
  0.1 1.0 copy-start
  1.2 0.7 copy-start.1
  2.2 11.6 %collective-permute-start.1 = (bf16[512,512]{1,0:T(8,128)(2,1)S(1)}, bf16[512,512]{1,0:T(8,128)(2,1)S(1)}, u32[]{:S(2)}, u32[]{:S(2)}) collective-permute-start(bf16[512,512]{1,0:T(8,128)(2,1)S(1)} %get-tuple-element.32.refs_0_), channel_id=1, source_target_pairs={{0,1},{1,0},{2,3},{3,2},{4,5},{5,4},{6,7},{7,6},{8,9},{9,8},{10,11... | collective-permute-start | bytes 1572872 | tf_op jit(solution)/shard_map/ppermute | solution.py:42
  5.6 10.0 %collective-permute-start = (bf16[512,512]{1,0:T(8,128)(2,1)S(1)}, bf16[512,512]{1,0:T(8,128)(2,1)S(1)}, u32[]{:S(2)}, u32[]{:S(2)}) collective-permute-start(bf16[512,512]{1,0:T(8,128)(2,1)S(1)} %get-tuple-element.32.refs_0_), channel_id=1, source_target_pairs={{0,2},{1,15},{2,4},{3,1},{4,6},{5,3},{6,8},{7,5},{8,10},{9,7},{10,... | collective-permute-start | bytes 1572872 | tf_op jit(solution)/shard_map/ppermute | solution.py:42
  9.4 9.6 %collective-permute-start.3 = (bf16[512,512]{1,0:T(8,128)(2,1)S(1)}, bf16[512,512]{1,0:T(8,128)(2,1)S(1)}, u32[]{:S(2)}, u32[]{:S(2)}) collective-permute-start(bf16[512,512]{1,0:T(8,128)(2,1)S(1)} %get-tuple-element.32.refs_0_), channel_id=1, source_target_pairs={{0,16},{1,65},{2,18},{3,67},{4,20},{5,69},{6,22},{7,71},{8,24},{9,... | collective-permute-start | bytes 1572872 | tf_op jit(solution)/shard_map/ppermute | solution.py:42
  10.7 8.3 %collective-permute-start.4 = (bf16[512,512]{1,0:T(8,128)(2,1)S(1)}, bf16[512,512]{1,0:T(8,128)(2,1)S(1)}, u32[]{:S(2)}, u32[]{:S(2)}) collective-permute-start(bf16[512,512]{1,0:T(8,128)(2,1)S(1)} %get-tuple-element.32.refs_0_), channel_id=1, source_target_pairs={{0,48},{1,193},{2,50},{3,195},{4,52},{5,197},{6,54},{7,199},{8,56}... | collective-permute-start | bytes 1572872 | tf_op jit(solution)/shard_map/ppermute | solution.py:42
  12.1 13.4 %collective-permute-start.5 = (bf16[512,512]{1,0:T(8,128)(2,1)S(1)}, bf16[512,512]{1,0:T(8,128)(2,1)S(1)}, u32[]{:S(2)}, u32[]{:S(2)}) collective-permute-start(bf16[512,512]{1,0:T(8,128)(2,1)S(1)} %get-tuple-element.32.refs_0_), channel_id=1, source_target_pairs={{0,32},{1,129},{2,34},{3,131},{4,36},{5,133},{6,38},{7,135},{8,40}... | collective-permute-start | bytes 1572872 | tf_op jit(solution)/shard_map/ppermute | solution.py:42
  13.8 11.7 %collective-permute-start.2 = (bf16[512,512]{1,0:T(8,128)(2,1)S(1)}, bf16[512,512]{1,0:T(8,128)(2,1)S(1)}, u32[]{:S(2)}, u32[]{:S(2)}) collective-permute-start(bf16[512,512]{1,0:T(8,128)(2,1)S(1)} %collective-permute-done.1.refs_5_), channel_id=1, source_target_pairs={{0,2},{1,15},{2,4},{3,1},{4,6},{5,3},{6,8},{7,5},{8,10},{9,7},{10,... | collective-permute-start | bytes 1572872 | tf_op jit(solution)/shard_map/ppermute | solution.py:42
  25.7 26.5 %collective-permute-start.18 = (bf16[2048,512]{1,0:T(8,128)(2,1)S(1)}, bf16[2048,512]{1,0:T(8,128)(2,1)S(1)}, u32[]{:S(2)}, u32[]{:S(2)}) collective-permute-start(bf16[2048,512]{1,0:T(8,128)(2,1)S(1)} %join.3.refs_0_), channel_id=1, source_target_pairs={{0,64},{1,17},{2,66},{3,19},{4,68},{5,21},{6,70},{7,23},{8,72},{9,... | collective-permute-start | bytes 6291464 | tf_op jit(solution)/shard_map/ppermute | solution.py:42
  26.9 25.3 %collective-permute-start.19 = (bf16[2048,512]{1,0:T(8,128)(2,1)S(1)}, bf16[2048,512]{1,0:T(8,128)(2,1)S(1)}, u32[]{:S(2)}, u32[]{:S(2)}) collective-permute-start(bf16[2048,512]{1,0:T(8,128)(2,1)S(1)} %join.3.refs_0_), channel_id=1, source_target_pairs={{0,192},{1,49},{2,194},{3,51},{4,196},{5,53},{6,198},{7,55},{8,200... | collective-permute-start | bytes 6291464 | tf_op jit(solution)/shard_map/ppermute | solution.py:42
  28.4 8.3 %collective-permute-start.6 = (bf16[512,512]{1,0:T(8,128)(2,1)S(1)}, bf16[512,512]{1,0:T(8,128)(2,1)S(1)}, u32[]{:S(2)}, u32[]{:S(2)}) collective-permute-start(bf16[512,512]{1,0:T(8,128)(2,1)S(1)} %collective-permute-done.refs_1_), channel_id=1, source_target_pairs={{0,2},{1,15},{2,4},{3,1},{4,6},{5,3},{6,8},{7,5},{8,10},{9,7},{10,... | collective-permute-start | bytes 1572872 | tf_op jit(solution)/shard_map/ppermute | solution.py:42
  29.1 8.3 %collective-permute-start.7 = (bf16[512,512]{1,0:T(8,128)(2,1)S(1)}, bf16[512,512]{1,0:T(8,128)(2,1)S(1)}, u32[]{:S(2)}, u32[]{:S(2)}) collective-permute-start(bf16[512,512]{1,0:T(8,128)(2,1)S(1)} %collective-permute-done.refs_1_), channel_id=1, source_target_pairs={{0,1},{1,0},{2,3},{3,2},{4,5},{5,4},{6,7},{7,6},{8,9},{9,8},{10,11... | collective-permute-start | bytes 1572872 | tf_op jit(solution)/shard_map/ppermute | solution.py:42
  29.1 13.2 %collective-permute-start.11 = (bf16[512,512]{1,0:T(8,128)(2,1)S(1)}, bf16[512,512]{1,0:T(8,128)(2,1)S(1)}, u32[]{:S(2)}, u32[]{:S(2)}) collective-permute-start(bf16[512,512]{1,0:T(8,128)(2,1)S(1)} %collective-permute-done.2.refs_6_), channel_id=1, source_target_pairs={{0,2},{1,15},{2,4},{3,1},{4,6},{5,3},{6,8},{7,5},{8,10},{9,7},{10,... | collective-permute-start | bytes 1572872 | tf_op jit(solution)/shard_map/ppermute | solution.py:42
  36.7 6.4 %collective-permute-start.12 = (bf16[512,512]{1,0:T(8,128)(2,1)S(1)}, bf16[512,512]{1,0:T(8,128)(2,1)S(1)}, u32[]{:S(2)}, u32[]{:S(2)}) collective-permute-start(bf16[512,512]{1,0:T(8,128)(2,1)S(1)} %collective-permute-done.2.refs_6_), channel_id=1, source_target_pairs={{0,1},{1,0},{2,3},{3,2},{4,5},{5,4},{6,7},{7,6},{8,9},{9,8},{10,11... | collective-permute-start | bytes 1572872 | tf_op jit(solution)/shard_map/ppermute | solution.py:42
  37.5 10.5 %collective-permute-start.8 = (bf16[512,512]{1,0:T(8,128)(2,1)S(1)}, bf16[512,512]{1,0:T(8,128)(2,1)S(1)}, u32[]{:S(2)}, u32[]{:S(2)}) collective-permute-start(bf16[512,512]{1,0:T(8,128)(2,1)S(1)} %collective-permute-done.6.refs_2_), channel_id=1, source_target_pairs={{0,2},{1,15},{2,4},{3,1},{4,6},{5,3},{6,8},{7,5},{8,10},{9,7},{10,... | collective-permute-start | bytes 1572872 | tf_op jit(solution)/shard_map/ppermute | solution.py:42
  42.4 6.4 %collective-permute-start.9 = (bf16[512,512]{1,0:T(8,128)(2,1)S(1)}, bf16[512,512]{1,0:T(8,128)(2,1)S(1)}, u32[]{:S(2)}, u32[]{:S(2)}) collective-permute-start(bf16[512,512]{1,0:T(8,128)(2,1)S(1)} %collective-permute-done.6.refs_2_), channel_id=1, source_target_pairs={{0,1},{1,0},{2,3},{3,2},{4,5},{5,4},{6,7},{7,6},{8,9},{9,8},{10,11... | collective-permute-start | bytes 1572872 | tf_op jit(solution)/shard_map/ppermute | solution.py:42
  43.1 12.0 %collective-permute-start.13 = (bf16[512,512]{1,0:T(8,128)(2,1)S(1)}, bf16[512,512]{1,0:T(8,128)(2,1)S(1)}, u32[]{:S(2)}, u32[]{:S(2)}) collective-permute-start(bf16[512,512]{1,0:T(8,128)(2,1)S(1)} %collective-permute-done.11.refs_7_), channel_id=1, source_target_pairs={{0,2},{1,15},{2,4},{3,1},{4,6},{5,3},{6,8},{7,5},{8,10},{9,7},{10,... | collective-permute-start | bytes 1572872 | tf_op jit(solution)/shard_map/ppermute | solution.py:42
  48.0 7.1 %collective-permute-start.16 = (bf16[512,512]{1,0:T(8,128)(2,1)S(1)}, bf16[512,512]{1,0:T(8,128)(2,1)S(1)}, u32[]{:S(2)}, u32[]{:S(2)}) collective-permute-start(bf16[512,512]{1,0:T(8,128)(2,1)S(1)} %collective-permute-done.11.refs_7_), channel_id=1, source_target_pairs={{0,1},{1,0},{2,3},{3,2},{4,5},{5,4},{6,7},{7,6},{8,9},{9,8},{10,11... | collective-permute-start | bytes 1572872 | tf_op jit(solution)/shard_map/ppermute | solution.py:42
  48.7 10.5 %collective-permute-start.10 = (bf16[512,512]{1,0:T(8,128)(2,1)S(1)}, bf16[512,512]{1,0:T(8,128)(2,1)S(1)}, u32[]{:S(2)}, u32[]{:S(2)}) collective-permute-start(bf16[512,512]{1,0:T(8,128)(2,1)S(1)} %collective-permute-done.8.refs_3_), channel_id=1, source_target_pairs={{0,2},{1,15},{2,4},{3,1},{4,6},{5,3},{6,8},{7,5},{8,10},{9,7},{10,... | collective-permute-start | bytes 1572872 | tf_op jit(solution)/shard_map/ppermute | solution.py:42
  52.2 14.9 %collective-permute-start.20 = (bf16[1024,512]{1,0:T(8,128)(2,1)S(1)}, bf16[1024,512]{1,0:T(8,128)(2,1)S(1)}, u32[]{:S(2)}, u32[]{:S(2)}) collective-permute-start(bf16[1024,512]{1,0:T(8,128)(2,1)S(1)} %slice.24), channel_id=1, source_target_pairs={{0,64},{1,17},{2,66},{3,19},{4,68},{5,21},{6,70},{7,23},{8,72},{9,... | collective-permute-start | bytes 3145736 | tf_op jit(solution)/shard_map/ppermute | solution.py:42
  52.4 15.5 %collective-permute-start.21 = (bf16[1024,512]{1,0:T(8,128)(2,1)S(1)}, bf16[1024,512]{1,0:T(8,128)(2,1)S(1)}, u32[]{:S(2)}, u32[]{:S(2)}) collective-permute-start(bf16[1024,512]{1,0:T(8,128)(2,1)S(1)} %slice.25), channel_id=1, source_target_pairs={{0,192},{1,49},{2,194},{3,51},{4,196},{5,53},{6,198},{7,55},{8,200... | collective-permute-start | bytes 3145736 | tf_op jit(solution)/shard_map/ppermute | solution.py:42
  55.1 4.9 %collective-permute-start.14 = (bf16[512,512]{1,0:T(8,128)(2,1)S(1)}, bf16[512,512]{1,0:T(8,128)(2,1)S(1)}, u32[]{:S(2)}, u32[]{:S(2)}) collective-permute-start(bf16[512,512]{1,0:T(8,128)(2,1)S(1)} %collective-permute-done.8.refs_3_), channel_id=1, source_target_pairs={{0,1},{1,0},{2,3},{3,2},{4,5},{5,4},{6,7},{7,6},{8,9},{9,8},{10,11... | collective-permute-start | bytes 1572872 | tf_op jit(solution)/shard_map/ppermute | solution.py:42
  55.1 4.8 %collective-permute-start.17 = (bf16[512,512]{1,0:T(8,128)(2,1)S(1)}, bf16[512,512]{1,0:T(8,128)(2,1)S(1)}, u32[]{:S(2)}, u32[]{:S(2)}) collective-permute-start(bf16[512,512]{1,0:T(8,128)(2,1)S(1)} %collective-permute-done.13.refs_8_), channel_id=1, source_target_pairs={{0,1},{1,0},{2,3},{3,2},{4,5},{5,4},{6,7},{7,6},{8,9},{9,8},{10,11... | collective-permute-start | bytes 1572872 | tf_op jit(solution)/shard_map/ppermute | solution.py:42
  59.2 2.3 %collective-permute-start.15 = (bf16[512,512]{1,0:T(8,128)(2,1)S(1)}, bf16[512,512]{1,0:T(8,128)(2,1)S(1)}, u32[]{:S(2)}, u32[]{:S(2)}) collective-permute-start(bf16[512,512]{1,0:T(8,128)(2,1)S(1)} %collective-permute-done.10.refs_4_), channel_id=1, source_target_pairs={{0,1},{1,0},{2,3},{3,2},{4,5},{5,4},{6,7},{7,6},{8,9},{9,8},{10,11... | collective-permute-start | bytes 1572872 | tf_op jit(solution)/shard_map/ppermute | solution.py:42
  69.2 6.6 %collective-permute-start.22 = (bf16[256,512]{1,0:T(8,128)(2,1)S(1)}, bf16[256,512]{1,0:T(8,128)(2,1)S(1)}, u32[]{:S(2)}, u32[]{:S(2)}) collective-permute-start(bf16[256,512]{1,0:T(8,128)(2,1)S(1)} %get-tuple-element.49.refs_0_), channel_id=1, source_target_pairs={{0,16},{1,65},{2,18},{3,67},{4,20},{5,69},{6,22},{7,71},{8,24},{9,... | collective-permute-start | bytes 786440 | tf_op jit(solution)/shard_map/ppermute | solution.py:42
  70.2 5.7 %collective-permute-start.25 = (bf16[256,512]{1,0:T(8,128)(2,1)S(1)}, bf16[256,512]{1,0:T(8,128)(2,1)S(1)}, u32[]{:S(2)}, u32[]{:S(2)}) collective-permute-start(bf16[256,512]{1,0:T(8,128)(2,1)S(1)} %get-tuple-element.50.refs_1_), channel_id=1, source_target_pairs={{0,48},{1,193},{2,50},{3,195},{4,52},{5,197},{6,54},{7,199},{8,56}... | collective-permute-start | bytes 786440 | tf_op jit(solution)/shard_map/ppermute | solution.py:42
  72.0 6.9 %collective-permute-start.23 = (bf16[256,512]{1,0:T(8,128)(2,1)S(1)}, bf16[256,512]{1,0:T(8,128)(2,1)S(1)}, u32[]{:S(2)}, u32[]{:S(2)}) collective-permute-start(bf16[256,512]{1,0:T(8,128)(2,1)S(1)} %get-tuple-element.50.refs_1_), channel_id=1, source_target_pairs={{0,16},{1,65},{2,18},{3,67},{4,20},{5,69},{6,22},{7,71},{8,24},{9,... | collective-permute-start | bytes 786440 | tf_op jit(solution)/shard_map/ppermute | solution.py:42
  72.0 9.7 %collective-permute-start.24 = (bf16[256,512]{1,0:T(8,128)(2,1)S(1)}, bf16[256,512]{1,0:T(8,128)(2,1)S(1)}, u32[]{:S(2)}, u32[]{:S(2)}) collective-permute-start(bf16[256,512]{1,0:T(8,128)(2,1)S(1)} %get-tuple-element.49.refs_0_), channel_id=1, source_target_pairs={{0,48},{1,193},{2,50},{3,195},{4,52},{5,197},{6,54},{7,199},{8,56}... | collective-permute-start | bytes 786440 | tf_op jit(solution)/shard_map/ppermute | solution.py:42
  75.8 6.7 %collective-permute-start.26 = (bf16[256,512]{1,0:T(8,128)(2,1)S(1)}, bf16[256,512]{1,0:T(8,128)(2,1)S(1)}, u32[]{:S(2)}, u32[]{:S(2)}) collective-permute-start(bf16[256,512]{1,0:T(8,128)(2,1)S(1)} %collective-permute-done.22.refs_2_), channel_id=1, source_target_pairs={{0,16},{1,65},{2,18},{3,67},{4,20},{5,69},{6,22},{7,71},{8,24},{9,... | collective-permute-start | bytes 786440 | tf_op jit(solution)/shard_map/ppermute | solution.py:42
  75.9 6.7 %collective-permute-start.27 = (bf16[256,512]{1,0:T(8,128)(2,1)S(1)}, bf16[256,512]{1,0:T(8,128)(2,1)S(1)}, u32[]{:S(2)}, u32[]{:S(2)}) collective-permute-start(bf16[256,512]{1,0:T(8,128)(2,1)S(1)} %collective-permute-done.25.refs_1_), channel_id=1, source_target_pairs={{0,48},{1,193},{2,50},{3,195},{4,52},{5,197},{6,54},{7,199},{8,56}... | collective-permute-start | bytes 786440 | tf_op jit(solution)/shard_map/ppermute | solution.py:42
  78.9 15.7 %collective-permute-start.28 = (bf16[1024,512]{1,0:T(8,128)(2,1)S(1)}, bf16[1024,512]{1,0:T(8,128)(2,1)S(1)}, u32[]{:S(2)}, u32[]{:S(2)}) collective-permute-start(bf16[1024,512]{1,0:T(8,128)(2,1)S(1)} %join.4.refs_0_), channel_id=1, source_target_pairs={{0,64},{1,17},{2,66},{3,19},{4,68},{5,21},{6,70},{7,23},{8,72},{9,... | collective-permute-start | bytes 3145736 | tf_op jit(solution)/shard_map/ppermute | solution.py:42
  79.0 15.7 %collective-permute-start.29 = (bf16[1024,512]{1,0:T(8,128)(2,1)S(1)}, bf16[1024,512]{1,0:T(8,128)(2,1)S(1)}, u32[]{:S(2)}, u32[]{:S(2)}) collective-permute-start(bf16[1024,512]{1,0:T(8,128)(2,1)S(1)} %join.4.refs_0_), channel_id=1, source_target_pairs={{0,192},{1,49},{2,194},{3,51},{4,196},{5,53},{6,198},{7,55},{8,200... | collective-permute-start | bytes 3145736 | tf_op jit(solution)/shard_map/ppermute | solution.py:42
  82.7 23.2 %collective-permute-start.30 = (bf16[1024,512]{1,0:T(8,128)(2,1)S(1)}, bf16[1024,512]{1,0:T(8,128)(2,1)S(1)}, u32[]{:S(2)}, u32[]{:S(2)}) collective-permute-start(bf16[1024,512]{1,0:T(8,128)(2,1)S(1)} %join.5.refs_1_), channel_id=1, source_target_pairs={{0,64},{1,17},{2,66},{3,19},{4,68},{5,21},{6,70},{7,23},{8,72},{9,... | collective-permute-start | bytes 3145736 | tf_op jit(solution)/shard_map/ppermute | solution.py:42
  82.7 23.2 %collective-permute-start.31 = (bf16[1024,512]{1,0:T(8,128)(2,1)S(1)}, bf16[1024,512]{1,0:T(8,128)(2,1)S(1)}, u32[]{:S(2)}, u32[]{:S(2)}) collective-permute-start(bf16[1024,512]{1,0:T(8,128)(2,1)S(1)} %join.5.refs_1_), channel_id=1, source_target_pairs={{0,192},{1,49},{2,194},{3,51},{4,196},{5,53},{6,198},{7,55},{8,200... | collective-permute-start | bytes 3145736 | tf_op jit(solution)/shard_map/ppermute | solution.py:42
  94.7 16.8 %collective-permute-start.32 = (bf16[512,512]{1,0:T(8,128)(2,1)S(1)}, bf16[512,512]{1,0:T(8,128)(2,1)S(1)}, u32[]{:S(2)}, u32[]{:S(2)}) collective-permute-start(bf16[512,512]{1,0:T(8,128)(2,1)S(1)} %slice.20), channel_id=1, source_target_pairs={{0,64},{1,17},{2,66},{3,19},{4,68},{5,21},{6,70},{7,23},{8,72},{9,... | collective-permute-start | bytes 1572872 | tf_op jit(solution)/shard_map/ppermute | solution.py:42
  94.8 16.7 %collective-permute-start.33 = (bf16[512,512]{1,0:T(8,128)(2,1)S(1)}, bf16[512,512]{1,0:T(8,128)(2,1)S(1)}, u32[]{:S(2)}, u32[]{:S(2)}) collective-permute-start(bf16[512,512]{1,0:T(8,128)(2,1)S(1)} %slice.21), channel_id=1, source_target_pairs={{0,192},{1,49},{2,194},{3,51},{4,196},{5,53},{6,198},{7,55},{8,200... | collective-permute-start | bytes 1572872 | tf_op jit(solution)/shard_map/ppermute | solution.py:42
  105.9 11.2 %collective-permute-start.34 = (bf16[512,512]{1,0:T(8,128)(2,1)S(1)}, bf16[512,512]{1,0:T(8,128)(2,1)S(1)}, u32[]{:S(2)}, u32[]{:S(2)}) collective-permute-start(bf16[512,512]{1,0:T(8,128)(2,1)S(1)} %slice.22), channel_id=1, source_target_pairs={{0,64},{1,17},{2,66},{3,19},{4,68},{5,21},{6,70},{7,23},{8,72},{9,... | collective-permute-start | bytes 1572872 | tf_op jit(solution)/shard_map/ppermute | solution.py:42
  106.1 11.5 %collective-permute-start.35 = (bf16[512,512]{1,0:T(8,128)(2,1)S(1)}, bf16[512,512]{1,0:T(8,128)(2,1)S(1)}, u32[]{:S(2)}, u32[]{:S(2)}) collective-permute-start(bf16[512,512]{1,0:T(8,128)(2,1)S(1)} %slice.23), channel_id=1, source_target_pairs={{0,192},{1,49},{2,194},{3,51},{4,196},{5,53},{6,198},{7,55},{8,200... | collective-permute-start | bytes 1572872 | tf_op jit(solution)/shard_map/ppermute | solution.py:42

commit v7 on v6

--- a/solution.py
+++ b/solution.py
@@ -139,25 +139,37 @@
     )(panel, begun, *rights)
 
 
-def middle_kernel(places, where_ref, panel_ref, sum_ref, *refs):
-    keep_ref, top_ref, low_ref = refs[-3:]
-    total = sum_ref[...] + total_of(panel_ref, refs[:-3], places)
-    total = keep_ref[...].astype(F32) * total
+def base_kernel(places, where_ref, panel_ref, sum_ref, keep_ref, part_ref, out_ref):
+    total = keep_ref[...].astype(F32) * (sum_ref[...] + total_of(panel_ref, [part_ref], places))
     diagonal = (lax.broadcasted_iota(jnp.int32, total.shape, 0) + where_ref[2 * TILES]
                 == lax.broadcasted_iota(jnp.int32, total.shape, 1))
-    out = (jnp.where(diagonal, 1.5, 0.0) - 0.5 * total).astype(BF16)
+    out_ref[...] = jnp.where(diagonal, 1.5, 0.0) - 0.5 * total
+
+
+def middle_base(where, panel, begun, part, place, keep):
+    return pl.pallas_call(
+        functools.partial(base_kernel, [place]),
+        in_specs=[SMEM] + [VMEM] * 4, out_specs=VMEM,
+        out_shape=jax.ShapeDtypeStruct(begun.shape, F32),
+        compiler_params=LARGE, cost_estimate=cost(0, panel, part), name="more",
+    )(where, panel, begun, keep, part)
+
+
+def middle_kernel(places, panel_ref, base_ref, part_ref, keep_ref, top_ref, low_ref):
+    total = total_of(panel_ref, [part_ref], places)
+    out = (base_ref[...] - 0.5 * (keep_ref[...].astype(F32) * total)).astype(BF16)
     half = top_ref.shape[0]
     top_ref[...], low_ref[...] = out[:half, :], out[half:, :]
 
 
-def finish_middle(where, panel, begun, rights, places, keep):
+def finish_middle(panel, base, part, place, keep):
     half = jax.ShapeDtypeStruct((keep.shape[0] // 2, keep.shape[1]), BF16)
     return pl.pallas_call(
-        functools.partial(middle_kernel, places),
-        in_specs=[SMEM] + [VMEM] * (3 + len(rights)), out_specs=[VMEM, VMEM],
+        functools.partial(middle_kernel, [place]),
+        in_specs=[VMEM] * 4, out_specs=[VMEM, VMEM],
         out_shape=[half, half],
-        compiler_params=LARGE, cost_estimate=cost(2, panel, rights[0]), name="middle",
-    )(where, panel, begun, *rights, keep)
+        compiler_params=LARGE, cost_estimate=cost(2, panel, part), name="middle",
+    )(panel, base, part, keep)
 
 
 def last_kernel(places, panel_ref, sum_ref, *refs):
@@ -251,9 +263,9 @@
     panel = arrange(where, own + other + swapped)
     begun = begin(panel, [full, full1, full3], [(0, 0), (2, 0), (6, 0)])
     begun, late[0] = together(begun, late[0])
-    begun = more(panel, begun, late[:1], [(4, 0)])
-    begun, late[1] = together(begun, late[1])
-    top, low = finish_middle(where, panel, begun, late[1:], [(5, 0)], keep)
+    base = middle_base(where, panel, begun, late[0], (4, 0), keep)
+    base, late[1] = together(base, late[1])
+    top, low = finish_middle(panel, base, late[1], (5, 0), keep)
     early, places, late, late_places = gather(top, low)
     begun = more(panel, begin(panel, early, places), late[:1], late_places[:1])
     return finish_last(panel, begun, late[1:], late_places[1:], keep)

time: 120 us -> 120 us (level)
  transfers between devices with their start and end apart: 36 -> 36, of which waited for: 17 -> 17; matrix products, arithmetic and copies ran while one was open for 0% -> 0% of each run, Pallas kernels for 8% -> 9%
where the time goes in v7:
time: 120 us; the launch traced here: 119 us
  waiting for transfers between devices  55.2 us (46%)
  starting transfers between devices  48.3 us (40%)
  Pallas kernels  12.9 us (11%)
  local copies, waits for them, and re-layouts  2.11 us (2%)
    ppermute x36, waiting for transfers between devices, send(): return lax.ppermute(block, AXES, pairs)  55.2 us
    ppermute x36, starting transfers between devices, send(): return lax.ppermute(block, AXES, pairs)  48.3 us
    pallas_call x2, Pallas kernels, begin(): pl.pallas_call(functools.partial(begin_kernel, places), in_specs=[VMEM] *...  7.34 us
  transfers between devices with their start and end apart: 36, of which 17 were waited for; matrix products, arithmetic and copies ran while one was open for 0% of the time, Pallas kernels for 9%

profile of v7, /device:TPU:1, one launch (start us, length us, event | category | flops | bytes accessed | tf_op | source)
XLA Modules:
  0.0 118.9 jit_solution(4628591002883344600)
XLA Ops:
  0.0 0.1 stack.135.where_ref
  0.1 1.0 copy-done
  1.2 0.7 copy-done.1
  1.8 0.4 mask.1
  2.2 3.3 %collective-permute-start.1 = (bf16[512,512]{1,0:T(8,128)(2,1)S(1)}, bf16[512,512]{1,0:T(8,128)(2,1)S(1)}, u32[]{:S(2)}, u32[]{:S(2)}) collective-permute-start(bf16[512,512]{1,0:T(8,128)(2,1)S(1)} %get-tuple-element.32.refs_0_), channel_id=1, source_target_pairs={{0,1},{1,0},{2,3},{3,2},{4,5},{5,4},{6,7},{7,6},{8,9},{9,8},{10,11... | collective-permute-start | bytes 1572872 | tf_op jit(solution)/shard_map/ppermute | solution.py:42
  5.6 3.8 %collective-permute-start = (bf16[512,512]{1,0:T(8,128)(2,1)S(1)}, bf16[512,512]{1,0:T(8,128)(2,1)S(1)}, u32[]{:S(2)}, u32[]{:S(2)}) collective-permute-start(bf16[512,512]{1,0:T(8,128)(2,1)S(1)} %get-tuple-element.32.refs_0_), channel_id=1, source_target_pairs={{0,2},{1,15},{2,4},{3,1},{4,6},{5,3},{6,8},{7,5},{8,10},{9,7},{10,... | collective-permute-start | bytes 1572872 | tf_op jit(solution)/shard_map/ppermute | solution.py:42
  9.4 1.3 %collective-permute-start.3 = (bf16[512,512]{1,0:T(8,128)(2,1)S(1)}, bf16[512,512]{1,0:T(8,128)(2,1)S(1)}, u32[]{:S(2)}, u32[]{:S(2)}) collective-permute-start(bf16[512,512]{1,0:T(8,128)(2,1)S(1)} %get-tuple-element.32.refs_0_), channel_id=1, source_target_pairs={{0,16},{1,65},{2,18},{3,67},{4,20},{5,69},{6,22},{7,71},{8,24},{9,... | collective-permute-start | bytes 1572872 | tf_op jit(solution)/shard_map/ppermute | solution.py:42
  10.7 1.4 %collective-permute-start.4 = (bf16[512,512]{1,0:T(8,128)(2,1)S(1)}, bf16[512,512]{1,0:T(8,128)(2,1)S(1)}, u32[]{:S(2)}, u32[]{:S(2)}) collective-permute-start(bf16[512,512]{1,0:T(8,128)(2,1)S(1)} %get-tuple-element.32.refs_0_), channel_id=1, source_target_pairs={{0,48},{1,193},{2,50},{3,195},{4,52},{5,197},{6,54},{7,199},{8,56}... | collective-permute-start | bytes 1572872 | tf_op jit(solution)/shard_map/ppermute | solution.py:42
  12.1 1.6 %collective-permute-start.5 = (bf16[512,512]{1,0:T(8,128)(2,1)S(1)}, bf16[512,512]{1,0:T(8,128)(2,1)S(1)}, u32[]{:S(2)}, u32[]{:S(2)}) collective-permute-start(bf16[512,512]{1,0:T(8,128)(2,1)S(1)} %get-tuple-element.32.refs_0_), channel_id=1, source_target_pairs={{0,32},{1,129},{2,34},{3,131},{4,36},{5,133},{6,38},{7,135},{8,40}... | collective-permute-start | bytes 1572872 | tf_op jit(solution)/shard_map/ppermute | solution.py:42
  13.8 0.7 collective-permute-start.2
  14.5 1.0 collective-permute-done.refs_1_
  15.5 3.5 %collective-permute-done.3.refs_1_ = bf16[512,512]{1,0:T(8,128)(2,1)S(1)} collective-permute-done((bf16[512,512]{1,0:T(8,128)(2,1)S(1)}, bf16[512,512]{1,0:T(8,128)(2,1)S(1)}, u32[]{:S(2)}, u32[]{:S(2)}) %collective-permute-start.3) | collective-permute-done | bytes 524320 | tf_op jit(solution)/shard_map/ppermute | solution.py:42
  19.0 6.5 %collective-permute-done.5.refs_3_ = bf16[512,512]{1,0:T(8,128)(2,1)S(1)} collective-permute-done((bf16[512,512]{1,0:T(8,128)(2,1)S(1)}, bf16[512,512]{1,0:T(8,128)(2,1)S(1)}, u32[]{:S(2)}, u32[]{:S(2)}) %collective-permute-start.5) | collective-permute-done | bytes 524320 | tf_op jit(solution)/shard_map/ppermute | solution.py:42
  25.5 0.1 join.3.refs_0_
  25.7 1.3 %collective-permute-start.18 = (bf16[2048,512]{1,0:T(8,128)(2,1)S(1)}, bf16[2048,512]{1,0:T(8,128)(2,1)S(1)}, u32[]{:S(2)}, u32[]{:S(2)}) collective-permute-start(bf16[2048,512]{1,0:T(8,128)(2,1)S(1)} %join.3.refs_0_), channel_id=1, source_target_pairs={{0,64},{1,17},{2,66},{3,19},{4,68},{5,21},{6,70},{7,23},{8,72},{9,... | collective-permute-start | bytes 6291464 | tf_op jit(solution)/shard_map/ppermute | solution.py:42
  26.9 1.5 %collective-permute-start.19 = (bf16[2048,512]{1,0:T(8,128)(2,1)S(1)}, bf16[2048,512]{1,0:T(8,128)(2,1)S(1)}, u32[]{:S(2)}, u32[]{:S(2)}) collective-permute-start(bf16[2048,512]{1,0:T(8,128)(2,1)S(1)} %join.3.refs_0_), channel_id=1, source_target_pairs={{0,192},{1,49},{2,194},{3,51},{4,196},{5,53},{6,198},{7,55},{8,200... | collective-permute-start | bytes 6291464 | tf_op jit(solution)/shard_map/ppermute | solution.py:42
  28.4 0.7 collective-permute-start.6
  29.1 1.0 collective-permute-start.11
  30.2 6.6 %collective-permute-done.6.refs_2_ = bf16[512,512]{1,0:T(8,128)(2,1)S(1)} collective-permute-done((bf16[512,512]{1,0:T(8,128)(2,1)S(1)}, bf16[512,512]{1,0:T(8,128)(2,1)S(1)}, u32[]{:S(2)}, u32[]{:S(2)}) %collective-permute-start.6) | collective-permute-done | bytes 524320 | tf_op jit(solution)/shard_map/ppermute | solution.py:42
  36.7 0.7 collective-permute-start.12
  37.5 1.7 %collective-permute-start.8 = (bf16[512,512]{1,0:T(8,128)(2,1)S(1)}, bf16[512,512]{1,0:T(8,128)(2,1)S(1)}, u32[]{:S(2)}, u32[]{:S(2)}) collective-permute-start(bf16[512,512]{1,0:T(8,128)(2,1)S(1)} %collective-permute-done.6.refs_2_), channel_id=1, source_target_pairs={{0,2},{1,15},{2,4},{3,1},{4,6},{5,3},{6,8},{7,5},{8,10},{9,7},{10,... | collective-permute-start | bytes 1572872 | tf_op jit(solution)/shard_map/ppermute | solution.py:42
  39.2 3.1 %collective-permute-done.11.refs_7_ = bf16[512,512]{1,0:T(8,128)(2,1)S(1)} collective-permute-done((bf16[512,512]{1,0:T(8,128)(2,1)S(1)}, bf16[512,512]{1,0:T(8,128)(2,1)S(1)}, u32[]{:S(2)}, u32[]{:S(2)}) %collective-permute-start.11) | collective-permute-done | bytes 524320 | tf_op jit(solution)/shard_map/ppermute | solution.py:42
  42.4 0.7 collective-permute-start.9
  43.1 1.7 %collective-permute-start.13 = (bf16[512,512]{1,0:T(8,128)(2,1)S(1)}, bf16[512,512]{1,0:T(8,128)(2,1)S(1)}, u32[]{:S(2)}, u32[]{:S(2)}) collective-permute-start(bf16[512,512]{1,0:T(8,128)(2,1)S(1)} %collective-permute-done.11.refs_7_), channel_id=1, source_target_pairs={{0,2},{1,15},{2,4},{3,1},{4,6},{5,3},{6,8},{7,5},{8,10},{9,7},{10,... | collective-permute-start | bytes 1572872 | tf_op jit(solution)/shard_map/ppermute | solution.py:42
  44.8 3.1 %collective-permute-done.8.refs_3_ = bf16[512,512]{1,0:T(8,128)(2,1)S(1)} collective-permute-done((bf16[512,512]{1,0:T(8,128)(2,1)S(1)}, bf16[512,512]{1,0:T(8,128)(2,1)S(1)}, u32[]{:S(2)}, u32[]{:S(2)}) %collective-permute-start.8) | collective-permute-done | bytes 524320 | tf_op jit(solution)/shard_map/ppermute | solution.py:42
  48.0 0.7 collective-permute-start.16
  48.7 1.7 %collective-permute-start.10 = (bf16[512,512]{1,0:T(8,128)(2,1)S(1)}, bf16[512,512]{1,0:T(8,128)(2,1)S(1)}, u32[]{:S(2)}, u32[]{:S(2)}) collective-permute-start(bf16[512,512]{1,0:T(8,128)(2,1)S(1)} %collective-permute-done.8.refs_3_), channel_id=1, source_target_pairs={{0,2},{1,15},{2,4},{3,1},{4,6},{5,3},{6,8},{7,5},{8,10},{9,7},{10,... | collective-permute-start | bytes 1572872 | tf_op jit(solution)/shard_map/ppermute | solution.py:42
  50.5 1.7 %collective-permute-done.18.refs_1_ = bf16[2048,512]{1,0:T(8,128)(2,1)S(1)} collective-permute-done((bf16[2048,512]{1,0:T(8,128)(2,1)S(1)}, bf16[2048,512]{1,0:T(8,128)(2,1)S(1)}, u32[]{:S(2)}, u32[]{:S(2)}) %collective-permute-start.18) | collective-permute-done | bytes 2097184 | tf_op jit(solution)/shard_map/ppermute | solution.py:42
  52.1 0.1 slice.24
  52.2 0.1 collective-permute-start.20
  52.3 0.1 slice.25
  52.4 2.7 %collective-permute-start.21 = (bf16[1024,512]{1,0:T(8,128)(2,1)S(1)}, bf16[1024,512]{1,0:T(8,128)(2,1)S(1)}, u32[]{:S(2)}, u32[]{:S(2)}) collective-permute-start(bf16[1024,512]{1,0:T(8,128)(2,1)S(1)} %slice.25), channel_id=1, source_target_pairs={{0,192},{1,49},{2,194},{3,51},{4,196},{5,53},{6,198},{7,55},{8,200... | collective-permute-start | bytes 3145736 | tf_op jit(solution)/shard_map/ppermute | solution.py:42
  55.1 0.5 collective-permute-start.17
  55.6 3.6 %collective-permute-done.10.refs_4_ = bf16[512,512]{1,0:T(8,128)(2,1)S(1)} collective-permute-done((bf16[512,512]{1,0:T(8,128)(2,1)S(1)}, bf16[512,512]{1,0:T(8,128)(2,1)S(1)}, u32[]{:S(2)}, u32[]{:S(2)}) %collective-permute-start.10) | collective-permute-done | bytes 524320 | tf_op jit(solution)/shard_map/ppermute | solution.py:42
  59.2 0.7 collective-permute-start.15
  60.0 1.5 %collective-permute-done.15.refs_12_ = bf16[512,512]{1,0:T(8,128)(2,1)S(1)} collective-permute-done((bf16[512,512]{1,0:T(8,128)(2,1)S(1)}, bf16[512,512]{1,0:T(8,128)(2,1)S(1)}, u32[]{:S(2)}, u32[]{:S(2)}) %collective-permute-start.15) | collective-permute-done | bytes 524320 | tf_op jit(solution)/shard_map/ppermute | solution.py:42
  61.5 1.2 %arrange.1.panel_ref = bf16[8,512,1024]{2,1,0:T(8,128)(2,1)S(1)} custom-call(s32[33]{0:T(128)S(1)} %stack.135.where_ref, bf16[512,512]{1,0:T(8,128)(2,1)S(1)} %get-tuple-element.32.refs_0_, bf16[512,512]{1,0:T(8,128)(2,1)S(1)} %collective-permute-done.refs_1_, bf16[512,512]{1,0:T(8,128)(2,1)S(1)} %collective-permute-done.6.refs_2_, ...), custom_call_target="tpu_custom_call" | custom-call | tf_op jit(solution)/shard_map/arrange/pallas_call | solution.py:93
  62.7 3.4 %begin.2.sum_ref = f32[512,512]{1,0:T(8,128)S(1)} custom-call(bf16[8,512,1024]{2,1,0:T(8,128)(2,1)S(1)} %arrange.1.panel_ref, bf16[2048,512]{1,0:T(8,128)(2,1)S(1)} %join.3.refs_0_, bf16[2048,512]{1,0:T(8,128)(2,1)S(1)} %collective-permute-done.18.refs_1_, bf16[2048,512]{1,0:T(8,128)(2,1)S(1)} %collective-permute-done.19.refs_2_), custom_call_target="tpu_custom_call" | custom-call | tf_op jit(solution)/shard_map/begin/pallas_call | solution.py:123
  66.1 1.0 collective-permute-done.20.part_ref
  67.1 1.3 %more.2.base_ref = f32[512,512]{1,0:T(8,128)S(1)} custom-call(s32[33]{0:T(128)S(1)} %stack.135.where_ref, bf16[8,512,1024]{2,1,0:T(8,128)(2,1)S(1)} %arrange.1.panel_ref, f32[512,512]{1,0:T(8,128)S(1)} %begin.2.sum_ref, bf16[512,512]{1,0:T(8,128)(2,1)S(1)} %get-tuple-element.45.keep_ref.refs_1_, bf16[1024,512]{1,0:T(8,128)(2,1)S(1)} %collective-permute-done.20.part_ref), custom_call_target="tpu_custom_call" | custom-call | tf_op jit(solution)/shard_map/more/pallas_call | solution.py:150
  68.5 0.7 middle.1
  69.2 0.9 collective-permute-start.22
  70.2 1.8 %collective-permute-start.25 = (bf16[256,512]{1,0:T(8,128)(2,1)S(1)}, bf16[256,512]{1,0:T(8,128)(2,1)S(1)}, u32[]{:S(2)}, u32[]{:S(2)}) collective-permute-start(bf16[256,512]{1,0:T(8,128)(2,1)S(1)} %get-tuple-element.50.refs_1_), channel_id=1, source_target_pairs={{0,48},{1,193},{2,50},{3,195},{4,52},{5,197},{6,54},{7,199},{8,56}... | collective-permute-start | bytes 786440 | tf_op jit(solution)/shard_map/ppermute | solution.py:42
  72.0 2.7 %collective-permute-start.24 = (bf16[256,512]{1,0:T(8,128)(2,1)S(1)}, bf16[256,512]{1,0:T(8,128)(2,1)S(1)}, u32[]{:S(2)}, u32[]{:S(2)}) collective-permute-start(bf16[256,512]{1,0:T(8,128)(2,1)S(1)} %get-tuple-element.49.refs_0_), channel_id=1, source_target_pairs={{0,48},{1,193},{2,50},{3,195},{4,52},{5,197},{6,54},{7,199},{8,56}... | collective-permute-start | bytes 786440 | tf_op jit(solution)/shard_map/ppermute | solution.py:42
  74.7 1.2 collective-permute-done.22.refs_2_
  75.8 2.9 %collective-permute-start.27 = (bf16[256,512]{1,0:T(8,128)(2,1)S(1)}, bf16[256,512]{1,0:T(8,128)(2,1)S(1)}, u32[]{:S(2)}, u32[]{:S(2)}) collective-permute-start(bf16[256,512]{1,0:T(8,128)(2,1)S(1)} %collective-permute-done.25.refs_1_), channel_id=1, source_target_pairs={{0,48},{1,193},{2,50},{3,195},{4,52},{5,197},{6,54},{7,199},{8,56}... | collective-permute-start | bytes 786440 | tf_op jit(solution)/shard_map/ppermute | solution.py:42
  78.7 0.1 collective-permute-done.23.refs_3_
  78.8 0.1 join.4.refs_0_
  78.9 0.1 collective-permute-start.28
  79.0 2.7 %collective-permute-start.29 = (bf16[1024,512]{1,0:T(8,128)(2,1)S(1)}, bf16[1024,512]{1,0:T(8,128)(2,1)S(1)}, u32[]{:S(2)}, u32[]{:S(2)}) collective-permute-start(bf16[1024,512]{1,0:T(8,128)(2,1)S(1)} %join.4.refs_0_), channel_id=1, source_target_pairs={{0,192},{1,49},{2,194},{3,51},{4,196},{5,53},{6,198},{7,55},{8,200... | collective-permute-start | bytes 3145736 | tf_op jit(solution)/shard_map/ppermute | solution.py:42
  81.7 0.9 collective-permute-done.26.refs_2_
  82.6 0.1 collective-permute-start.30
  82.7 2.7 %collective-permute-start.31 = (bf16[1024,512]{1,0:T(8,128)(2,1)S(1)}, bf16[1024,512]{1,0:T(8,128)(2,1)S(1)}, u32[]{:S(2)}, u32[]{:S(2)}) collective-permute-start(bf16[1024,512]{1,0:T(8,128)(2,1)S(1)} %join.5.refs_1_), channel_id=1, source_target_pairs={{0,192},{1,49},{2,194},{3,51},{4,196},{5,53},{6,198},{7,55},{8,200... | collective-permute-start | bytes 3145736 | tf_op jit(solution)/shard_map/ppermute | solution.py:42
  85.4 9.3 %collective-permute-done.28.refs_2_ = bf16[1024,512]{1,0:T(8,128)(2,1)S(1)} collective-permute-done((bf16[1024,512]{1,0:T(8,128)(2,1)S(1)}, bf16[1024,512]{1,0:T(8,128)(2,1)S(1)}, u32[]{:S(2)}, u32[]{:S(2)}) %collective-permute-start.28) | collective-permute-done | bytes 1048608 | tf_op jit(solution)/shard_map/ppermute | solution.py:42
  94.7 0.1 collective-permute-start.32
  94.8 3.0 %collective-permute-start.33 = (bf16[512,512]{1,0:T(8,128)(2,1)S(1)}, bf16[512,512]{1,0:T(8,128)(2,1)S(1)}, u32[]{:S(2)}, u32[]{:S(2)}) collective-permute-start(bf16[512,512]{1,0:T(8,128)(2,1)S(1)} %slice.21), channel_id=1, source_target_pairs={{0,192},{1,49},{2,194},{3,51},{4,196},{5,53},{6,198},{7,55},{8,200... | collective-permute-start | bytes 1572872 | tf_op jit(solution)/shard_map/ppermute | solution.py:42
  97.9 8.0 %collective-permute-done.30.refs_3_ = bf16[1024,512]{1,0:T(8,128)(2,1)S(1)} collective-permute-done((bf16[1024,512]{1,0:T(8,128)(2,1)S(1)}, bf16[1024,512]{1,0:T(8,128)(2,1)S(1)}, u32[]{:S(2)}, u32[]{:S(2)}) %collective-permute-start.30) | collective-permute-done | bytes 1048608 | tf_op jit(solution)/shard_map/ppermute | solution.py:42
  105.9 0.1 collective-permute-start.34
  106.1 3.0 %collective-permute-start.35 = (bf16[512,512]{1,0:T(8,128)(2,1)S(1)}, bf16[512,512]{1,0:T(8,128)(2,1)S(1)}, u32[]{:S(2)}, u32[]{:S(2)}) collective-permute-start(bf16[512,512]{1,0:T(8,128)(2,1)S(1)} %slice.23), channel_id=1, source_target_pairs={{0,192},{1,49},{2,194},{3,51},{4,196},{5,53},{6,198},{7,55},{8,200... | collective-permute-start | bytes 1572872 | tf_op jit(solution)/shard_map/ppermute | solution.py:42
  109.1 2.4 %collective-permute-done.32.refs_6_ = bf16[512,512]{1,0:T(8,128)(2,1)S(1)} collective-permute-done((bf16[512,512]{1,0:T(8,128)(2,1)S(1)}, bf16[512,512]{1,0:T(8,128)(2,1)S(1)}, u32[]{:S(2)}, u32[]{:S(2)}) %collective-permute-start.32) | collective-permute-done | bytes 524320 | tf_op jit(solution)/shard_map/ppermute | solution.py:42
  111.5 3.9 %begin.3.sum_ref = f32[512,512]{1,0:T(8,128)S(1)} custom-call(bf16[8,512,1024]{2,1,0:T(8,128)(2,1)S(1)} %arrange.1.panel_ref, bf16[1024,512]{1,0:T(8,128)(2,1)S(1)} %join.4.refs_0_, bf16[1024,512]{1,0:T(8,128)(2,1)S(1)} %join.5.refs_1_, bf16[1024,512]{1,0:T(8,128)(2,1)S(1)} %collective-permute-done.28.refs_2_, ...), custom_call_target="tpu_custom_call" | custom-call | tf_op jit(solution)/shard_map/begin/pallas_call | solution.py:123
  115.4 1.7 %collective-permute-done.34.refs_0_ = bf16[512,512]{1,0:T(8,128)(2,1)S(1)} collective-permute-done((bf16[512,512]{1,0:T(8,128)(2,1)S(1)}, bf16[512,512]{1,0:T(8,128)(2,1)S(1)}, u32[]{:S(2)}, u32[]{:S(2)}) %collective-permute-start.34) | collective-permute-done | bytes 524320 | tf_op jit(solution)/shard_map/ppermute | solution.py:42
  117.1 0.4 more.3.sum_ref
  117.6 1.2 last.1
  (30 shorter events, 0.3 us)
Async XLA Ops:
  0.1 1.0 copy-start
  1.2 0.7 copy-start.1
  2.2 11.6 %collective-permute-start.1 = (bf16[512,512]{1,0:T(8,128)(2,1)S(1)}, bf16[512,512]{1,0:T(8,128)(2,1)S(1)}, u32[]{:S(2)}, u32[]{:S(2)}) collective-permute-start(bf16[512,512]{1,0:T(8,128)(2,1)S(1)} %get-tuple-element.32.refs_0_), channel_id=1, source_target_pairs={{0,1},{1,0},{2,3},{3,2},{4,5},{5,4},{6,7},{7,6},{8,9},{9,8},{10,11... | collective-permute-start | bytes 1572872 | tf_op jit(solution)/shard_map/ppermute | solution.py:42
  5.6 10.0 %collective-permute-start = (bf16[512,512]{1,0:T(8,128)(2,1)S(1)}, bf16[512,512]{1,0:T(8,128)(2,1)S(1)}, u32[]{:S(2)}, u32[]{:S(2)}) collective-permute-start(bf16[512,512]{1,0:T(8,128)(2,1)S(1)} %get-tuple-element.32.refs_0_), channel_id=1, source_target_pairs={{0,2},{1,15},{2,4},{3,1},{4,6},{5,3},{6,8},{7,5},{8,10},{9,7},{10,... | collective-permute-start | bytes 1572872 | tf_op jit(solution)/shard_map/ppermute | solution.py:42
  9.4 9.6 %collective-permute-start.3 = (bf16[512,512]{1,0:T(8,128)(2,1)S(1)}, bf16[512,512]{1,0:T(8,128)(2,1)S(1)}, u32[]{:S(2)}, u32[]{:S(2)}) collective-permute-start(bf16[512,512]{1,0:T(8,128)(2,1)S(1)} %get-tuple-element.32.refs_0_), channel_id=1, source_target_pairs={{0,16},{1,65},{2,18},{3,67},{4,20},{5,69},{6,22},{7,71},{8,24},{9,... | collective-permute-start | bytes 1572872 | tf_op jit(solution)/shard_map/ppermute | solution.py:42
  10.7 8.3 %collective-permute-start.4 = (bf16[512,512]{1,0:T(8,128)(2,1)S(1)}, bf16[512,512]{1,0:T(8,128)(2,1)S(1)}, u32[]{:S(2)}, u32[]{:S(2)}) collective-permute-start(bf16[512,512]{1,0:T(8,128)(2,1)S(1)} %get-tuple-element.32.refs_0_), channel_id=1, source_target_pairs={{0,48},{1,193},{2,50},{3,195},{4,52},{5,197},{6,54},{7,199},{8,56}... | collective-permute-start | bytes 1572872 | tf_op jit(solution)/shard_map/ppermute | solution.py:42
  12.1 13.4 %collective-permute-start.5 = (bf16[512,512]{1,0:T(8,128)(2,1)S(1)}, bf16[512,512]{1,0:T(8,128)(2,1)S(1)}, u32[]{:S(2)}, u32[]{:S(2)}) collective-permute-start(bf16[512,512]{1,0:T(8,128)(2,1)S(1)} %get-tuple-element.32.refs_0_), channel_id=1, source_target_pairs={{0,32},{1,129},{2,34},{3,131},{4,36},{5,133},{6,38},{7,135},{8,40}... | collective-permute-start | bytes 1572872 | tf_op jit(solution)/shard_map/ppermute | solution.py:42
  13.8 11.7 %collective-permute-start.2 = (bf16[512,512]{1,0:T(8,128)(2,1)S(1)}, bf16[512,512]{1,0:T(8,128)(2,1)S(1)}, u32[]{:S(2)}, u32[]{:S(2)}) collective-permute-start(bf16[512,512]{1,0:T(8,128)(2,1)S(1)} %collective-permute-done.1.refs_5_), channel_id=1, source_target_pairs={{0,2},{1,15},{2,4},{3,1},{4,6},{5,3},{6,8},{7,5},{8,10},{9,7},{10,... | collective-permute-start | bytes 1572872 | tf_op jit(solution)/shard_map/ppermute | solution.py:42
  25.7 26.5 %collective-permute-start.18 = (bf16[2048,512]{1,0:T(8,128)(2,1)S(1)}, bf16[2048,512]{1,0:T(8,128)(2,1)S(1)}, u32[]{:S(2)}, u32[]{:S(2)}) collective-permute-start(bf16[2048,512]{1,0:T(8,128)(2,1)S(1)} %join.3.refs_0_), channel_id=1, source_target_pairs={{0,64},{1,17},{2,66},{3,19},{4,68},{5,21},{6,70},{7,23},{8,72},{9,... | collective-permute-start | bytes 6291464 | tf_op jit(solution)/shard_map/ppermute | solution.py:42
  26.9 25.3 %collective-permute-start.19 = (bf16[2048,512]{1,0:T(8,128)(2,1)S(1)}, bf16[2048,512]{1,0:T(8,128)(2,1)S(1)}, u32[]{:S(2)}, u32[]{:S(2)}) collective-permute-start(bf16[2048,512]{1,0:T(8,128)(2,1)S(1)} %join.3.refs_0_), channel_id=1, source_target_pairs={{0,192},{1,49},{2,194},{3,51},{4,196},{5,53},{6,198},{7,55},{8,200... | collective-permute-start | bytes 6291464 | tf_op jit(solution)/shard_map/ppermute | solution.py:42
  28.4 8.3 %collective-permute-start.6 = (bf16[512,512]{1,0:T(8,128)(2,1)S(1)}, bf16[512,512]{1,0:T(8,128)(2,1)S(1)}, u32[]{:S(2)}, u32[]{:S(2)}) collective-permute-start(bf16[512,512]{1,0:T(8,128)(2,1)S(1)} %collective-permute-done.refs_1_), channel_id=1, source_target_pairs={{0,2},{1,15},{2,4},{3,1},{4,6},{5,3},{6,8},{7,5},{8,10},{9,7},{10,... | collective-permute-start | bytes 1572872 | tf_op jit(solution)/shard_map/ppermute | solution.py:42
  29.1 8.3 %collective-permute-start.7 = (bf16[512,512]{1,0:T(8,128)(2,1)S(1)}, bf16[512,512]{1,0:T(8,128)(2,1)S(1)}, u32[]{:S(2)}, u32[]{:S(2)}) collective-permute-start(bf16[512,512]{1,0:T(8,128)(2,1)S(1)} %collective-permute-done.refs_1_), channel_id=1, source_target_pairs={{0,1},{1,0},{2,3},{3,2},{4,5},{5,4},{6,7},{7,6},{8,9},{9,8},{10,11... | collective-permute-start | bytes 1572872 | tf_op jit(solution)/shard_map/ppermute | solution.py:42
  29.1 13.2 %collective-permute-start.11 = (bf16[512,512]{1,0:T(8,128)(2,1)S(1)}, bf16[512,512]{1,0:T(8,128)(2,1)S(1)}, u32[]{:S(2)}, u32[]{:S(2)}) collective-permute-start(bf16[512,512]{1,0:T(8,128)(2,1)S(1)} %collective-permute-done.2.refs_6_), channel_id=1, source_target_pairs={{0,2},{1,15},{2,4},{3,1},{4,6},{5,3},{6,8},{7,5},{8,10},{9,7},{10,... | collective-permute-start | bytes 1572872 | tf_op jit(solution)/shard_map/ppermute | solution.py:42
  36.7 6.4 %collective-permute-start.12 = (bf16[512,512]{1,0:T(8,128)(2,1)S(1)}, bf16[512,512]{1,0:T(8,128)(2,1)S(1)}, u32[]{:S(2)}, u32[]{:S(2)}) collective-permute-start(bf16[512,512]{1,0:T(8,128)(2,1)S(1)} %collective-permute-done.2.refs_6_), channel_id=1, source_target_pairs={{0,1},{1,0},{2,3},{3,2},{4,5},{5,4},{6,7},{7,6},{8,9},{9,8},{10,11... | collective-permute-start | bytes 1572872 | tf_op jit(solution)/shard_map/ppermute | solution.py:42
  37.5 10.5 %collective-permute-start.8 = (bf16[512,512]{1,0:T(8,128)(2,1)S(1)}, bf16[512,512]{1,0:T(8,128)(2,1)S(1)}, u32[]{:S(2)}, u32[]{:S(2)}) collective-permute-start(bf16[512,512]{1,0:T(8,128)(2,1)S(1)} %collective-permute-done.6.refs_2_), channel_id=1, source_target_pairs={{0,2},{1,15},{2,4},{3,1},{4,6},{5,3},{6,8},{7,5},{8,10},{9,7},{10,... | collective-permute-start | bytes 1572872 | tf_op jit(solution)/shard_map/ppermute | solution.py:42
  42.4 6.4 %collective-permute-start.9 = (bf16[512,512]{1,0:T(8,128)(2,1)S(1)}, bf16[512,512]{1,0:T(8,128)(2,1)S(1)}, u32[]{:S(2)}, u32[]{:S(2)}) collective-permute-start(bf16[512,512]{1,0:T(8,128)(2,1)S(1)} %collective-permute-done.6.refs_2_), channel_id=1, source_target_pairs={{0,1},{1,0},{2,3},{3,2},{4,5},{5,4},{6,7},{7,6},{8,9},{9,8},{10,11... | collective-permute-start | bytes 1572872 | tf_op jit(solution)/shard_map/ppermute | solution.py:42
  43.1 12.0 %collective-permute-start.13 = (bf16[512,512]{1,0:T(8,128)(2,1)S(1)}, bf16[512,512]{1,0:T(8,128)(2,1)S(1)}, u32[]{:S(2)}, u32[]{:S(2)}) collective-permute-start(bf16[512,512]{1,0:T(8,128)(2,1)S(1)} %collective-permute-done.11.refs_7_), channel_id=1, source_target_pairs={{0,2},{1,15},{2,4},{3,1},{4,6},{5,3},{6,8},{7,5},{8,10},{9,7},{10,... | collective-permute-start | bytes 1572872 | tf_op jit(solution)/shard_map/ppermute | solution.py:42
  48.0 7.1 %collective-permute-start.16 = (bf16[512,512]{1,0:T(8,128)(2,1)S(1)}, bf16[512,512]{1,0:T(8,128)(2,1)S(1)}, u32[]{:S(2)}, u32[]{:S(2)}) collective-permute-start(bf16[512,512]{1,0:T(8,128)(2,1)S(1)} %collective-permute-done.11.refs_7_), channel_id=1, source_target_pairs={{0,1},{1,0},{2,3},{3,2},{4,5},{5,4},{6,7},{7,6},{8,9},{9,8},{10,11... | collective-permute-start | bytes 1572872 | tf_op jit(solution)/shard_map/ppermute | solution.py:42
  48.7 10.5 %collective-permute-start.10 = (bf16[512,512]{1,0:T(8,128)(2,1)S(1)}, bf16[512,512]{1,0:T(8,128)(2,1)S(1)}, u32[]{:S(2)}, u32[]{:S(2)}) collective-permute-start(bf16[512,512]{1,0:T(8,128)(2,1)S(1)} %collective-permute-done.8.refs_3_), channel_id=1, source_target_pairs={{0,2},{1,15},{2,4},{3,1},{4,6},{5,3},{6,8},{7,5},{8,10},{9,7},{10,... | collective-permute-start | bytes 1572872 | tf_op jit(solution)/shard_map/ppermute | solution.py:42
  52.2 14.9 %collective-permute-start.20 = (bf16[1024,512]{1,0:T(8,128)(2,1)S(1)}, bf16[1024,512]{1,0:T(8,128)(2,1)S(1)}, u32[]{:S(2)}, u32[]{:S(2)}) collective-permute-start(bf16[1024,512]{1,0:T(8,128)(2,1)S(1)} %slice.24), channel_id=1, source_target_pairs={{0,64},{1,17},{2,66},{3,19},{4,68},{5,21},{6,70},{7,23},{8,72},{9,... | collective-permute-start | bytes 3145736 | tf_op jit(solution)/shard_map/ppermute | solution.py:42
  52.4 16.1 %collective-permute-start.21 = (bf16[1024,512]{1,0:T(8,128)(2,1)S(1)}, bf16[1024,512]{1,0:T(8,128)(2,1)S(1)}, u32[]{:S(2)}, u32[]{:S(2)}) collective-permute-start(bf16[1024,512]{1,0:T(8,128)(2,1)S(1)} %slice.25), channel_id=1, source_target_pairs={{0,192},{1,49},{2,194},{3,51},{4,196},{5,53},{6,198},{7,55},{8,200... | collective-permute-start | bytes 3145736 | tf_op jit(solution)/shard_map/ppermute | solution.py:42
  55.1 4.9 %collective-permute-start.14 = (bf16[512,512]{1,0:T(8,128)(2,1)S(1)}, bf16[512,512]{1,0:T(8,128)(2,1)S(1)}, u32[]{:S(2)}, u32[]{:S(2)}) collective-permute-start(bf16[512,512]{1,0:T(8,128)(2,1)S(1)} %collective-permute-done.8.refs_3_), channel_id=1, source_target_pairs={{0,1},{1,0},{2,3},{3,2},{4,5},{5,4},{6,7},{7,6},{8,9},{9,8},{10,11... | collective-permute-start | bytes 1572872 | tf_op jit(solution)/shard_map/ppermute | solution.py:42
  55.1 4.8 %collective-permute-start.17 = (bf16[512,512]{1,0:T(8,128)(2,1)S(1)}, bf16[512,512]{1,0:T(8,128)(2,1)S(1)}, u32[]{:S(2)}, u32[]{:S(2)}) collective-permute-start(bf16[512,512]{1,0:T(8,128)(2,1)S(1)} %collective-permute-done.13.refs_8_), channel_id=1, source_target_pairs={{0,1},{1,0},{2,3},{3,2},{4,5},{5,4},{6,7},{7,6},{8,9},{9,8},{10,11... | collective-permute-start | bytes 1572872 | tf_op jit(solution)/shard_map/ppermute | solution.py:42
  59.2 2.3 %collective-permute-start.15 = (bf16[512,512]{1,0:T(8,128)(2,1)S(1)}, bf16[512,512]{1,0:T(8,128)(2,1)S(1)}, u32[]{:S(2)}, u32[]{:S(2)}) collective-permute-start(bf16[512,512]{1,0:T(8,128)(2,1)S(1)} %collective-permute-done.10.refs_4_), channel_id=1, source_target_pairs={{0,1},{1,0},{2,3},{3,2},{4,5},{5,4},{6,7},{7,6},{8,9},{9,8},{10,11... | collective-permute-start | bytes 1572872 | tf_op jit(solution)/shard_map/ppermute | solution.py:42
  69.2 6.6 %collective-permute-start.22 = (bf16[256,512]{1,0:T(8,128)(2,1)S(1)}, bf16[256,512]{1,0:T(8,128)(2,1)S(1)}, u32[]{:S(2)}, u32[]{:S(2)}) collective-permute-start(bf16[256,512]{1,0:T(8,128)(2,1)S(1)} %get-tuple-element.49.refs_0_), channel_id=1, source_target_pairs={{0,16},{1,65},{2,18},{3,67},{4,20},{5,69},{6,22},{7,71},{8,24},{9,... | collective-permute-start | bytes 786440 | tf_op jit(solution)/shard_map/ppermute | solution.py:42
  70.2 5.7 %collective-permute-start.25 = (bf16[256,512]{1,0:T(8,128)(2,1)S(1)}, bf16[256,512]{1,0:T(8,128)(2,1)S(1)}, u32[]{:S(2)}, u32[]{:S(2)}) collective-permute-start(bf16[256,512]{1,0:T(8,128)(2,1)S(1)} %get-tuple-element.50.refs_1_), channel_id=1, source_target_pairs={{0,48},{1,193},{2,50},{3,195},{4,52},{5,197},{6,54},{7,199},{8,56}... | collective-permute-start | bytes 786440 | tf_op jit(solution)/shard_map/ppermute | solution.py:42
  72.0 6.9 %collective-permute-start.23 = (bf16[256,512]{1,0:T(8,128)(2,1)S(1)}, bf16[256,512]{1,0:T(8,128)(2,1)S(1)}, u32[]{:S(2)}, u32[]{:S(2)}) collective-permute-start(bf16[256,512]{1,0:T(8,128)(2,1)S(1)} %get-tuple-element.50.refs_1_), channel_id=1, source_target_pairs={{0,16},{1,65},{2,18},{3,67},{4,20},{5,69},{6,22},{7,71},{8,24},{9,... | collective-permute-start | bytes 786440 | tf_op jit(solution)/shard_map/ppermute | solution.py:42
  72.0 9.7 %collective-permute-start.24 = (bf16[256,512]{1,0:T(8,128)(2,1)S(1)}, bf16[256,512]{1,0:T(8,128)(2,1)S(1)}, u32[]{:S(2)}, u32[]{:S(2)}) collective-permute-start(bf16[256,512]{1,0:T(8,128)(2,1)S(1)} %get-tuple-element.49.refs_0_), channel_id=1, source_target_pairs={{0,48},{1,193},{2,50},{3,195},{4,52},{5,197},{6,54},{7,199},{8,56}... | collective-permute-start | bytes 786440 | tf_op jit(solution)/shard_map/ppermute | solution.py:42
  75.8 6.7 %collective-permute-start.26 = (bf16[256,512]{1,0:T(8,128)(2,1)S(1)}, bf16[256,512]{1,0:T(8,128)(2,1)S(1)}, u32[]{:S(2)}, u32[]{:S(2)}) collective-permute-start(bf16[256,512]{1,0:T(8,128)(2,1)S(1)} %collective-permute-done.22.refs_2_), channel_id=1, source_target_pairs={{0,16},{1,65},{2,18},{3,67},{4,20},{5,69},{6,22},{7,71},{8,24},{9,... | collective-permute-start | bytes 786440 | tf_op jit(solution)/shard_map/ppermute | solution.py:42
  75.8 6.7 %collective-permute-start.27 = (bf16[256,512]{1,0:T(8,128)(2,1)S(1)}, bf16[256,512]{1,0:T(8,128)(2,1)S(1)}, u32[]{:S(2)}, u32[]{:S(2)}) collective-permute-start(bf16[256,512]{1,0:T(8,128)(2,1)S(1)} %collective-permute-done.25.refs_1_), channel_id=1, source_target_pairs={{0,48},{1,193},{2,50},{3,195},{4,52},{5,197},{6,54},{7,199},{8,56}... | collective-permute-start | bytes 786440 | tf_op jit(solution)/shard_map/ppermute | solution.py:42
  78.9 15.7 %collective-permute-start.28 = (bf16[1024,512]{1,0:T(8,128)(2,1)S(1)}, bf16[1024,512]{1,0:T(8,128)(2,1)S(1)}, u32[]{:S(2)}, u32[]{:S(2)}) collective-permute-start(bf16[1024,512]{1,0:T(8,128)(2,1)S(1)} %join.4.refs_0_), channel_id=1, source_target_pairs={{0,64},{1,17},{2,66},{3,19},{4,68},{5,21},{6,70},{7,23},{8,72},{9,... | collective-permute-start | bytes 3145736 | tf_op jit(solution)/shard_map/ppermute | solution.py:42
  79.0 15.7 %collective-permute-start.29 = (bf16[1024,512]{1,0:T(8,128)(2,1)S(1)}, bf16[1024,512]{1,0:T(8,128)(2,1)S(1)}, u32[]{:S(2)}, u32[]{:S(2)}) collective-permute-start(bf16[1024,512]{1,0:T(8,128)(2,1)S(1)} %join.4.refs_0_), channel_id=1, source_target_pairs={{0,192},{1,49},{2,194},{3,51},{4,196},{5,53},{6,198},{7,55},{8,200... | collective-permute-start | bytes 3145736 | tf_op jit(solution)/shard_map/ppermute | solution.py:42
  82.6 23.2 %collective-permute-start.30 = (bf16[1024,512]{1,0:T(8,128)(2,1)S(1)}, bf16[1024,512]{1,0:T(8,128)(2,1)S(1)}, u32[]{:S(2)}, u32[]{:S(2)}) collective-permute-start(bf16[1024,512]{1,0:T(8,128)(2,1)S(1)} %join.5.refs_1_), channel_id=1, source_target_pairs={{0,64},{1,17},{2,66},{3,19},{4,68},{5,21},{6,70},{7,23},{8,72},{9,... | collective-permute-start | bytes 3145736 | tf_op jit(solution)/shard_map/ppermute | solution.py:42
  82.7 23.2 %collective-permute-start.31 = (bf16[1024,512]{1,0:T(8,128)(2,1)S(1)}, bf16[1024,512]{1,0:T(8,128)(2,1)S(1)}, u32[]{:S(2)}, u32[]{:S(2)}) collective-permute-start(bf16[1024,512]{1,0:T(8,128)(2,1)S(1)} %join.5.refs_1_), channel_id=1, source_target_pairs={{0,192},{1,49},{2,194},{3,51},{4,196},{5,53},{6,198},{7,55},{8,200... | collective-permute-start | bytes 3145736 | tf_op jit(solution)/shard_map/ppermute | solution.py:42
  94.7 16.8 %collective-permute-start.32 = (bf16[512,512]{1,0:T(8,128)(2,1)S(1)}, bf16[512,512]{1,0:T(8,128)(2,1)S(1)}, u32[]{:S(2)}, u32[]{:S(2)}) collective-permute-start(bf16[512,512]{1,0:T(8,128)(2,1)S(1)} %slice.20), channel_id=1, source_target_pairs={{0,64},{1,17},{2,66},{3,19},{4,68},{5,21},{6,70},{7,23},{8,72},{9,... | collective-permute-start | bytes 1572872 | tf_op jit(solution)/shard_map/ppermute | solution.py:42
  94.8 16.7 %collective-permute-start.33 = (bf16[512,512]{1,0:T(8,128)(2,1)S(1)}, bf16[512,512]{1,0:T(8,128)(2,1)S(1)}, u32[]{:S(2)}, u32[]{:S(2)}) collective-permute-start(bf16[512,512]{1,0:T(8,128)(2,1)S(1)} %slice.21), channel_id=1, source_target_pairs={{0,192},{1,49},{2,194},{3,51},{4,196},{5,53},{6,198},{7,55},{8,200... | collective-permute-start | bytes 1572872 | tf_op jit(solution)/shard_map/ppermute | solution.py:42
  105.9 11.2 %collective-permute-start.34 = (bf16[512,512]{1,0:T(8,128)(2,1)S(1)}, bf16[512,512]{1,0:T(8,128)(2,1)S(1)}, u32[]{:S(2)}, u32[]{:S(2)}) collective-permute-start(bf16[512,512]{1,0:T(8,128)(2,1)S(1)} %slice.22), channel_id=1, source_target_pairs={{0,64},{1,17},{2,66},{3,19},{4,68},{5,21},{6,70},{7,23},{8,72},{9,... | collective-permute-start | bytes 1572872 | tf_op jit(solution)/shard_map/ppermute | solution.py:42
  106.1 11.5 %collective-permute-start.35 = (bf16[512,512]{1,0:T(8,128)(2,1)S(1)}, bf16[512,512]{1,0:T(8,128)(2,1)S(1)}, u32[]{:S(2)}, u32[]{:S(2)}) collective-permute-start(bf16[512,512]{1,0:T(8,128)(2,1)S(1)} %slice.23), channel_id=1, source_target_pairs={{0,192},{1,49},{2,194},{3,51},{4,196},{5,53},{6,198},{7,55},{8,200... | collective-permute-start | bytes 1572872 | tf_op jit(solution)/shard_map/ppermute | solution.py:42

commit v8 on v7

--- a/solution.py
+++ b/solution.py
@@ -11,6 +11,7 @@
 SIDE = 4
 DEEP = 8
 TILES = 16
+STORES = 4
 AXES = ("row", "col")
 F32 = jnp.float32
 BF16 = jnp.bfloat16
@@ -174,10 +175,10 @@
 
 def last_kernel(places, panel_ref, sum_ref, *refs):
     rights, keep_ref, out_hbm, out_ref, sems = refs[:-4], refs[-4], refs[-3], refs[-2], refs[-1]
-    half = out_ref.shape[0] // 2
+    part = out_ref.shape[0] // STORES
     stores = []
-    for k in range(2):
-        rows = pl.ds(k * half, half)
+    for k in range(STORES):
+        rows = pl.ds(k * part, part)
         total = sum_ref[rows, :] + total_of(panel_ref.at[:, rows, :], rights, places)
         out_ref[rows, :] = (keep_ref[rows, :].astype(F32) * total).astype(BF16)
         stores.append(pltpu.make_async_copy(out_ref.at[rows], out_hbm.at[rows], sems.at[k]))
@@ -191,7 +192,7 @@
         functools.partial(last_kernel, places),
         in_specs=[VMEM] * (3 + len(rights)), out_specs=ANY,
         out_shape=jax.ShapeDtypeStruct(keep.shape, BF16),
-        scratch_shapes=[pltpu.VMEM(keep.shape, BF16), pltpu.SemaphoreType.DMA((2,))],
+        scratch_shapes=[pltpu.VMEM(keep.shape, BF16), pltpu.SemaphoreType.DMA((STORES,))],
         compiler_params=LARGE, cost_estimate=cost(2, panel, rights[0]), name="last",
     )(panel, begun, *rights, keep)
 

time: 120 us -> 120 us (level)
  no operation moved by 1% of the time
where the time goes in v8:
time: 120 us; the launch traced here: 119 us
  waiting for transfers between devices  55.2 us (46%)
  starting transfers between devices  48.3 us (40%)
  Pallas kernels  12.9 us (11%)
  local copies, waits for them, and re-layouts  2.11 us (2%)
    ppermute x36, waiting for transfers between devices, send(): return lax.ppermute(block, AXES, pairs)  55.2 us
    ppermute x36, starting transfers between devices, send(): return lax.ppermute(block, AXES, pairs)  48.3 us
    pallas_call x2, Pallas kernels, begin(): pl.pallas_call(functools.partial(begin_kernel, places), in_specs=[VMEM] *...  7.34 us
  transfers between devices with their start and end apart: 36, of which 17 were waited for; matrix products, arithmetic and copies ran while one was open for 0% of the time, Pallas kernels for 9%

profile of v8, /device:TPU:1, one launch (start us, length us, event | category | flops | bytes accessed | tf_op | source)
XLA Modules:
  0.0 118.9 jit_solution(1856028153221885450)
XLA Ops:
  0.0 0.1 stack.135.where_ref
  0.1 1.0 copy-done
  1.2 0.7 copy-done.1
  1.8 0.4 mask.1
  2.2 3.3 %collective-permute-start.1 = (bf16[512,512]{1,0:T(8,128)(2,1)S(1)}, bf16[512,512]{1,0:T(8,128)(2,1)S(1)}, u32[]{:S(2)}, u32[]{:S(2)}) collective-permute-start(bf16[512,512]{1,0:T(8,128)(2,1)S(1)} %get-tuple-element.32.refs_0_), channel_id=1, source_target_pairs={{0,1},{1,0},{2,3},{3,2},{4,5},{5,4},{6,7},{7,6},{8,9},{9,8},{10,11... | collective-permute-start | bytes 1572872 | tf_op jit(solution)/shard_map/ppermute | solution.py:43
  5.6 3.8 %collective-permute-start = (bf16[512,512]{1,0:T(8,128)(2,1)S(1)}, bf16[512,512]{1,0:T(8,128)(2,1)S(1)}, u32[]{:S(2)}, u32[]{:S(2)}) collective-permute-start(bf16[512,512]{1,0:T(8,128)(2,1)S(1)} %get-tuple-element.32.refs_0_), channel_id=1, source_target_pairs={{0,2},{1,15},{2,4},{3,1},{4,6},{5,3},{6,8},{7,5},{8,10},{9,7},{10,... | collective-permute-start | bytes 1572872 | tf_op jit(solution)/shard_map/ppermute | solution.py:43
  9.4 1.3 %collective-permute-start.3 = (bf16[512,512]{1,0:T(8,128)(2,1)S(1)}, bf16[512,512]{1,0:T(8,128)(2,1)S(1)}, u32[]{:S(2)}, u32[]{:S(2)}) collective-permute-start(bf16[512,512]{1,0:T(8,128)(2,1)S(1)} %get-tuple-element.32.refs_0_), channel_id=1, source_target_pairs={{0,16},{1,65},{2,18},{3,67},{4,20},{5,69},{6,22},{7,71},{8,24},{9,... | collective-permute-start | bytes 1572872 | tf_op jit(solution)/shard_map/ppermute | solution.py:43
  10.7 1.4 %collective-permute-start.4 = (bf16[512,512]{1,0:T(8,128)(2,1)S(1)}, bf16[512,512]{1,0:T(8,128)(2,1)S(1)}, u32[]{:S(2)}, u32[]{:S(2)}) collective-permute-start(bf16[512,512]{1,0:T(8,128)(2,1)S(1)} %get-tuple-element.32.refs_0_), channel_id=1, source_target_pairs={{0,48},{1,193},{2,50},{3,195},{4,52},{5,197},{6,54},{7,199},{8,56}... | collective-permute-start | bytes 1572872 | tf_op jit(solution)/shard_map/ppermute | solution.py:43
  12.1 1.6 %collective-permute-start.5 = (bf16[512,512]{1,0:T(8,128)(2,1)S(1)}, bf16[512,512]{1,0:T(8,128)(2,1)S(1)}, u32[]{:S(2)}, u32[]{:S(2)}) collective-permute-start(bf16[512,512]{1,0:T(8,128)(2,1)S(1)} %get-tuple-element.32.refs_0_), channel_id=1, source_target_pairs={{0,32},{1,129},{2,34},{3,131},{4,36},{5,133},{6,38},{7,135},{8,40}... | collective-permute-start | bytes 1572872 | tf_op jit(solution)/shard_map/ppermute | solution.py:43
  13.8 0.7 collective-permute-start.2
  14.5 1.0 collective-permute-done.refs_1_
  15.5 3.5 %collective-permute-done.3.refs_1_ = bf16[512,512]{1,0:T(8,128)(2,1)S(1)} collective-permute-done((bf16[512,512]{1,0:T(8,128)(2,1)S(1)}, bf16[512,512]{1,0:T(8,128)(2,1)S(1)}, u32[]{:S(2)}, u32[]{:S(2)}) %collective-permute-start.3) | collective-permute-done | bytes 524320 | tf_op jit(solution)/shard_map/ppermute | solution.py:43
  19.0 6.5 %collective-permute-done.5.refs_3_ = bf16[512,512]{1,0:T(8,128)(2,1)S(1)} collective-permute-done((bf16[512,512]{1,0:T(8,128)(2,1)S(1)}, bf16[512,512]{1,0:T(8,128)(2,1)S(1)}, u32[]{:S(2)}, u32[]{:S(2)}) %collective-permute-start.5) | collective-permute-done | bytes 524320 | tf_op jit(solution)/shard_map/ppermute | solution.py:43
  25.5 0.1 join.3.refs_0_
  25.7 1.3 %collective-permute-start.18 = (bf16[2048,512]{1,0:T(8,128)(2,1)S(1)}, bf16[2048,512]{1,0:T(8,128)(2,1)S(1)}, u32[]{:S(2)}, u32[]{:S(2)}) collective-permute-start(bf16[2048,512]{1,0:T(8,128)(2,1)S(1)} %join.3.refs_0_), channel_id=1, source_target_pairs={{0,64},{1,17},{2,66},{3,19},{4,68},{5,21},{6,70},{7,23},{8,72},{9,... | collective-permute-start | bytes 6291464 | tf_op jit(solution)/shard_map/ppermute | solution.py:43
  26.9 1.5 %collective-permute-start.19 = (bf16[2048,512]{1,0:T(8,128)(2,1)S(1)}, bf16[2048,512]{1,0:T(8,128)(2,1)S(1)}, u32[]{:S(2)}, u32[]{:S(2)}) collective-permute-start(bf16[2048,512]{1,0:T(8,128)(2,1)S(1)} %join.3.refs_0_), channel_id=1, source_target_pairs={{0,192},{1,49},{2,194},{3,51},{4,196},{5,53},{6,198},{7,55},{8,200... | collective-permute-start | bytes 6291464 | tf_op jit(solution)/shard_map/ppermute | solution.py:43
  28.4 0.7 collective-permute-start.6
  29.1 1.0 collective-permute-start.11
  30.2 6.6 %collective-permute-done.6.refs_2_ = bf16[512,512]{1,0:T(8,128)(2,1)S(1)} collective-permute-done((bf16[512,512]{1,0:T(8,128)(2,1)S(1)}, bf16[512,512]{1,0:T(8,128)(2,1)S(1)}, u32[]{:S(2)}, u32[]{:S(2)}) %collective-permute-start.6) | collective-permute-done | bytes 524320 | tf_op jit(solution)/shard_map/ppermute | solution.py:43
  36.7 0.7 collective-permute-start.12
  37.5 1.7 %collective-permute-start.8 = (bf16[512,512]{1,0:T(8,128)(2,1)S(1)}, bf16[512,512]{1,0:T(8,128)(2,1)S(1)}, u32[]{:S(2)}, u32[]{:S(2)}) collective-permute-start(bf16[512,512]{1,0:T(8,128)(2,1)S(1)} %collective-permute-done.6.refs_2_), channel_id=1, source_target_pairs={{0,2},{1,15},{2,4},{3,1},{4,6},{5,3},{6,8},{7,5},{8,10},{9,7},{10,... | collective-permute-start | bytes 1572872 | tf_op jit(solution)/shard_map/ppermute | solution.py:43
  39.2 3.1 %collective-permute-done.11.refs_7_ = bf16[512,512]{1,0:T(8,128)(2,1)S(1)} collective-permute-done((bf16[512,512]{1,0:T(8,128)(2,1)S(1)}, bf16[512,512]{1,0:T(8,128)(2,1)S(1)}, u32[]{:S(2)}, u32[]{:S(2)}) %collective-permute-start.11) | collective-permute-done | bytes 524320 | tf_op jit(solution)/shard_map/ppermute | solution.py:43
  42.4 0.7 collective-permute-start.9
  43.1 1.7 %collective-permute-start.13 = (bf16[512,512]{1,0:T(8,128)(2,1)S(1)}, bf16[512,512]{1,0:T(8,128)(2,1)S(1)}, u32[]{:S(2)}, u32[]{:S(2)}) collective-permute-start(bf16[512,512]{1,0:T(8,128)(2,1)S(1)} %collective-permute-done.11.refs_7_), channel_id=1, source_target_pairs={{0,2},{1,15},{2,4},{3,1},{4,6},{5,3},{6,8},{7,5},{8,10},{9,7},{10,... | collective-permute-start | bytes 1572872 | tf_op jit(solution)/shard_map/ppermute | solution.py:43
  44.8 3.1 %collective-permute-done.8.refs_3_ = bf16[512,512]{1,0:T(8,128)(2,1)S(1)} collective-permute-done((bf16[512,512]{1,0:T(8,128)(2,1)S(1)}, bf16[512,512]{1,0:T(8,128)(2,1)S(1)}, u32[]{:S(2)}, u32[]{:S(2)}) %collective-permute-start.8) | collective-permute-done | bytes 524320 | tf_op jit(solution)/shard_map/ppermute | solution.py:43
  48.0 0.7 collective-permute-start.16
  48.7 1.7 %collective-permute-start.10 = (bf16[512,512]{1,0:T(8,128)(2,1)S(1)}, bf16[512,512]{1,0:T(8,128)(2,1)S(1)}, u32[]{:S(2)}, u32[]{:S(2)}) collective-permute-start(bf16[512,512]{1,0:T(8,128)(2,1)S(1)} %collective-permute-done.8.refs_3_), channel_id=1, source_target_pairs={{0,2},{1,15},{2,4},{3,1},{4,6},{5,3},{6,8},{7,5},{8,10},{9,7},{10,... | collective-permute-start | bytes 1572872 | tf_op jit(solution)/shard_map/ppermute | solution.py:43
  50.5 1.7 %collective-permute-done.18.refs_1_ = bf16[2048,512]{1,0:T(8,128)(2,1)S(1)} collective-permute-done((bf16[2048,512]{1,0:T(8,128)(2,1)S(1)}, bf16[2048,512]{1,0:T(8,128)(2,1)S(1)}, u32[]{:S(2)}, u32[]{:S(2)}) %collective-permute-start.18) | collective-permute-done | bytes 2097184 | tf_op jit(solution)/shard_map/ppermute | solution.py:43
  52.1 0.1 slice.24
  52.2 0.1 collective-permute-start.20
  52.3 0.1 slice.25
  52.4 2.7 %collective-permute-start.21 = (bf16[1024,512]{1,0:T(8,128)(2,1)S(1)}, bf16[1024,512]{1,0:T(8,128)(2,1)S(1)}, u32[]{:S(2)}, u32[]{:S(2)}) collective-permute-start(bf16[1024,512]{1,0:T(8,128)(2,1)S(1)} %slice.25), channel_id=1, source_target_pairs={{0,192},{1,49},{2,194},{3,51},{4,196},{5,53},{6,198},{7,55},{8,200... | collective-permute-start | bytes 3145736 | tf_op jit(solution)/shard_map/ppermute | solution.py:43
  55.1 0.5 collective-permute-start.17
  55.6 3.6 %collective-permute-done.10.refs_4_ = bf16[512,512]{1,0:T(8,128)(2,1)S(1)} collective-permute-done((bf16[512,512]{1,0:T(8,128)(2,1)S(1)}, bf16[512,512]{1,0:T(8,128)(2,1)S(1)}, u32[]{:S(2)}, u32[]{:S(2)}) %collective-permute-start.10) | collective-permute-done | bytes 524320 | tf_op jit(solution)/shard_map/ppermute | solution.py:43
  59.2 0.7 collective-permute-start.15
  60.0 1.5 %collective-permute-done.15.refs_12_ = bf16[512,512]{1,0:T(8,128)(2,1)S(1)} collective-permute-done((bf16[512,512]{1,0:T(8,128)(2,1)S(1)}, bf16[512,512]{1,0:T(8,128)(2,1)S(1)}, u32[]{:S(2)}, u32[]{:S(2)}) %collective-permute-start.15) | collective-permute-done | bytes 524320 | tf_op jit(solution)/shard_map/ppermute | solution.py:43
  61.5 1.2 %arrange.1.panel_ref = bf16[8,512,1024]{2,1,0:T(8,128)(2,1)S(1)} custom-call(s32[33]{0:T(128)S(1)} %stack.135.where_ref, bf16[512,512]{1,0:T(8,128)(2,1)S(1)} %get-tuple-element.32.refs_0_, bf16[512,512]{1,0:T(8,128)(2,1)S(1)} %collective-permute-done.refs_1_, bf16[512,512]{1,0:T(8,128)(2,1)S(1)} %collective-permute-done.6.refs_2_, ...), custom_call_target="tpu_custom_call" | custom-call | tf_op jit(solution)/shard_map/arrange/pallas_call | solution.py:94
  62.7 3.4 %begin.2.sum_ref = f32[512,512]{1,0:T(8,128)S(1)} custom-call(bf16[8,512,1024]{2,1,0:T(8,128)(2,1)S(1)} %arrange.1.panel_ref, bf16[2048,512]{1,0:T(8,128)(2,1)S(1)} %join.3.refs_0_, bf16[2048,512]{1,0:T(8,128)(2,1)S(1)} %collective-permute-done.18.refs_1_, bf16[2048,512]{1,0:T(8,128)(2,1)S(1)} %collective-permute-done.19.refs_2_), custom_call_target="tpu_custom_call" | custom-call | tf_op jit(solution)/shard_map/begin/pallas_call | solution.py:124
  66.1 1.0 collective-permute-done.20.part_ref
  67.1 1.3 %more.2.base_ref = f32[512,512]{1,0:T(8,128)S(1)} custom-call(s32[33]{0:T(128)S(1)} %stack.135.where_ref, bf16[8,512,1024]{2,1,0:T(8,128)(2,1)S(1)} %arrange.1.panel_ref, f32[512,512]{1,0:T(8,128)S(1)} %begin.2.sum_ref, bf16[512,512]{1,0:T(8,128)(2,1)S(1)} %get-tuple-element.45.keep_ref.refs_1_, bf16[1024,512]{1,0:T(8,128)(2,1)S(1)} %collective-permute-done.20.part_ref), custom_call_target="tpu_custom_call" | custom-call | tf_op jit(solution)/shard_map/more/pallas_call | solution.py:151
  68.5 0.7 middle.1
  69.2 0.9 collective-permute-start.22
  70.2 1.8 %collective-permute-start.25 = (bf16[256,512]{1,0:T(8,128)(2,1)S(1)}, bf16[256,512]{1,0:T(8,128)(2,1)S(1)}, u32[]{:S(2)}, u32[]{:S(2)}) collective-permute-start(bf16[256,512]{1,0:T(8,128)(2,1)S(1)} %get-tuple-element.50.refs_1_), channel_id=1, source_target_pairs={{0,48},{1,193},{2,50},{3,195},{4,52},{5,197},{6,54},{7,199},{8,56}... | collective-permute-start | bytes 786440 | tf_op jit(solution)/shard_map/ppermute | solution.py:43
  72.0 2.7 %collective-permute-start.24 = (bf16[256,512]{1,0:T(8,128)(2,1)S(1)}, bf16[256,512]{1,0:T(8,128)(2,1)S(1)}, u32[]{:S(2)}, u32[]{:S(2)}) collective-permute-start(bf16[256,512]{1,0:T(8,128)(2,1)S(1)} %get-tuple-element.49.refs_0_), channel_id=1, source_target_pairs={{0,48},{1,193},{2,50},{3,195},{4,52},{5,197},{6,54},{7,199},{8,56}... | collective-permute-start | bytes 786440 | tf_op jit(solution)/shard_map/ppermute | solution.py:43
  74.7 1.2 collective-permute-done.22.refs_2_
  75.8 2.9 %collective-permute-start.27 = (bf16[256,512]{1,0:T(8,128)(2,1)S(1)}, bf16[256,512]{1,0:T(8,128)(2,1)S(1)}, u32[]{:S(2)}, u32[]{:S(2)}) collective-permute-start(bf16[256,512]{1,0:T(8,128)(2,1)S(1)} %collective-permute-done.25.refs_1_), channel_id=1, source_target_pairs={{0,48},{1,193},{2,50},{3,195},{4,52},{5,197},{6,54},{7,199},{8,56}... | collective-permute-start | bytes 786440 | tf_op jit(solution)/shard_map/ppermute | solution.py:43
  78.7 0.1 collective-permute-done.23.refs_3_
  78.8 0.1 join.4.refs_0_
  78.9 0.1 collective-permute-start.28
  79.0 2.7 %collective-permute-start.29 = (bf16[1024,512]{1,0:T(8,128)(2,1)S(1)}, bf16[1024,512]{1,0:T(8,128)(2,1)S(1)}, u32[]{:S(2)}, u32[]{:S(2)}) collective-permute-start(bf16[1024,512]{1,0:T(8,128)(2,1)S(1)} %join.4.refs_0_), channel_id=1, source_target_pairs={{0,192},{1,49},{2,194},{3,51},{4,196},{5,53},{6,198},{7,55},{8,200... | collective-permute-start | bytes 3145736 | tf_op jit(solution)/shard_map/ppermute | solution.py:43
  81.7 0.9 collective-permute-done.26.refs_2_
  82.6 0.1 collective-permute-start.30
  82.7 2.7 %collective-permute-start.31 = (bf16[1024,512]{1,0:T(8,128)(2,1)S(1)}, bf16[1024,512]{1,0:T(8,128)(2,1)S(1)}, u32[]{:S(2)}, u32[]{:S(2)}) collective-permute-start(bf16[1024,512]{1,0:T(8,128)(2,1)S(1)} %join.5.refs_1_), channel_id=1, source_target_pairs={{0,192},{1,49},{2,194},{3,51},{4,196},{5,53},{6,198},{7,55},{8,200... | collective-permute-start | bytes 3145736 | tf_op jit(solution)/shard_map/ppermute | solution.py:43
  85.4 9.3 %collective-permute-done.28.refs_2_ = bf16[1024,512]{1,0:T(8,128)(2,1)S(1)} collective-permute-done((bf16[1024,512]{1,0:T(8,128)(2,1)S(1)}, bf16[1024,512]{1,0:T(8,128)(2,1)S(1)}, u32[]{:S(2)}, u32[]{:S(2)}) %collective-permute-start.28) | collective-permute-done | bytes 1048608 | tf_op jit(solution)/shard_map/ppermute | solution.py:43
  94.7 0.1 collective-permute-start.32
  94.8 3.0 %collective-permute-start.33 = (bf16[512,512]{1,0:T(8,128)(2,1)S(1)}, bf16[512,512]{1,0:T(8,128)(2,1)S(1)}, u32[]{:S(2)}, u32[]{:S(2)}) collective-permute-start(bf16[512,512]{1,0:T(8,128)(2,1)S(1)} %slice.21), channel_id=1, source_target_pairs={{0,192},{1,49},{2,194},{3,51},{4,196},{5,53},{6,198},{7,55},{8,200... | collective-permute-start | bytes 1572872 | tf_op jit(solution)/shard_map/ppermute | solution.py:43
  97.9 8.0 %collective-permute-done.30.refs_3_ = bf16[1024,512]{1,0:T(8,128)(2,1)S(1)} collective-permute-done((bf16[1024,512]{1,0:T(8,128)(2,1)S(1)}, bf16[1024,512]{1,0:T(8,128)(2,1)S(1)}, u32[]{:S(2)}, u32[]{:S(2)}) %collective-permute-start.30) | collective-permute-done | bytes 1048608 | tf_op jit(solution)/shard_map/ppermute | solution.py:43
  105.9 0.1 collective-permute-start.34
  106.1 3.0 %collective-permute-start.35 = (bf16[512,512]{1,0:T(8,128)(2,1)S(1)}, bf16[512,512]{1,0:T(8,128)(2,1)S(1)}, u32[]{:S(2)}, u32[]{:S(2)}) collective-permute-start(bf16[512,512]{1,0:T(8,128)(2,1)S(1)} %slice.23), channel_id=1, source_target_pairs={{0,192},{1,49},{2,194},{3,51},{4,196},{5,53},{6,198},{7,55},{8,200... | collective-permute-start | bytes 1572872 | tf_op jit(solution)/shard_map/ppermute | solution.py:43
  109.1 2.4 %collective-permute-done.32.refs_6_ = bf16[512,512]{1,0:T(8,128)(2,1)S(1)} collective-permute-done((bf16[512,512]{1,0:T(8,128)(2,1)S(1)}, bf16[512,512]{1,0:T(8,128)(2,1)S(1)}, u32[]{:S(2)}, u32[]{:S(2)}) %collective-permute-start.32) | collective-permute-done | bytes 524320 | tf_op jit(solution)/shard_map/ppermute | solution.py:43
  111.5 3.9 %begin.3.sum_ref = f32[512,512]{1,0:T(8,128)S(1)} custom-call(bf16[8,512,1024]{2,1,0:T(8,128)(2,1)S(1)} %arrange.1.panel_ref, bf16[1024,512]{1,0:T(8,128)(2,1)S(1)} %join.4.refs_0_, bf16[1024,512]{1,0:T(8,128)(2,1)S(1)} %join.5.refs_1_, bf16[1024,512]{1,0:T(8,128)(2,1)S(1)} %collective-permute-done.28.refs_2_, ...), custom_call_target="tpu_custom_call" | custom-call | tf_op jit(solution)/shard_map/begin/pallas_call | solution.py:124
  115.4 1.7 %collective-permute-done.34.refs_0_ = bf16[512,512]{1,0:T(8,128)(2,1)S(1)} collective-permute-done((bf16[512,512]{1,0:T(8,128)(2,1)S(1)}, bf16[512,512]{1,0:T(8,128)(2,1)S(1)}, u32[]{:S(2)}, u32[]{:S(2)}) %collective-permute-start.34) | collective-permute-done | bytes 524320 | tf_op jit(solution)/shard_map/ppermute | solution.py:43
  117.1 0.4 more.3.sum_ref
  117.6 1.2 last.1
  (30 shorter events, 0.3 us)
Async XLA Ops:
  0.1 1.0 copy-start
  1.2 0.7 copy-start.1
  2.2 11.6 %collective-permute-start.1 = (bf16[512,512]{1,0:T(8,128)(2,1)S(1)}, bf16[512,512]{1,0:T(8,128)(2,1)S(1)}, u32[]{:S(2)}, u32[]{:S(2)}) collective-permute-start(bf16[512,512]{1,0:T(8,128)(2,1)S(1)} %get-tuple-element.32.refs_0_), channel_id=1, source_target_pairs={{0,1},{1,0},{2,3},{3,2},{4,5},{5,4},{6,7},{7,6},{8,9},{9,8},{10,11... | collective-permute-start | bytes 1572872 | tf_op jit(solution)/shard_map/ppermute | solution.py:43
  5.6 10.0 %collective-permute-start = (bf16[512,512]{1,0:T(8,128)(2,1)S(1)}, bf16[512,512]{1,0:T(8,128)(2,1)S(1)}, u32[]{:S(2)}, u32[]{:S(2)}) collective-permute-start(bf16[512,512]{1,0:T(8,128)(2,1)S(1)} %get-tuple-element.32.refs_0_), channel_id=1, source_target_pairs={{0,2},{1,15},{2,4},{3,1},{4,6},{5,3},{6,8},{7,5},{8,10},{9,7},{10,... | collective-permute-start | bytes 1572872 | tf_op jit(solution)/shard_map/ppermute | solution.py:43
  9.4 9.6 %collective-permute-start.3 = (bf16[512,512]{1,0:T(8,128)(2,1)S(1)}, bf16[512,512]{1,0:T(8,128)(2,1)S(1)}, u32[]{:S(2)}, u32[]{:S(2)}) collective-permute-start(bf16[512,512]{1,0:T(8,128)(2,1)S(1)} %get-tuple-element.32.refs_0_), channel_id=1, source_target_pairs={{0,16},{1,65},{2,18},{3,67},{4,20},{5,69},{6,22},{7,71},{8,24},{9,... | collective-permute-start | bytes 1572872 | tf_op jit(solution)/shard_map/ppermute | solution.py:43
  10.7 8.3 %collective-permute-start.4 = (bf16[512,512]{1,0:T(8,128)(2,1)S(1)}, bf16[512,512]{1,0:T(8,128)(2,1)S(1)}, u32[]{:S(2)}, u32[]{:S(2)}) collective-permute-start(bf16[512,512]{1,0:T(8,128)(2,1)S(1)} %get-tuple-element.32.refs_0_), channel_id=1, source_target_pairs={{0,48},{1,193},{2,50},{3,195},{4,52},{5,197},{6,54},{7,199},{8,56}... | collective-permute-start | bytes 1572872 | tf_op jit(solution)/shard_map/ppermute | solution.py:43
  12.1 13.4 %collective-permute-start.5 = (bf16[512,512]{1,0:T(8,128)(2,1)S(1)}, bf16[512,512]{1,0:T(8,128)(2,1)S(1)}, u32[]{:S(2)}, u32[]{:S(2)}) collective-permute-start(bf16[512,512]{1,0:T(8,128)(2,1)S(1)} %get-tuple-element.32.refs_0_), channel_id=1, source_target_pairs={{0,32},{1,129},{2,34},{3,131},{4,36},{5,133},{6,38},{7,135},{8,40}... | collective-permute-start | bytes 1572872 | tf_op jit(solution)/shard_map/ppermute | solution.py:43
  13.8 11.7 %collective-permute-start.2 = (bf16[512,512]{1,0:T(8,128)(2,1)S(1)}, bf16[512,512]{1,0:T(8,128)(2,1)S(1)}, u32[]{:S(2)}, u32[]{:S(2)}) collective-permute-start(bf16[512,512]{1,0:T(8,128)(2,1)S(1)} %collective-permute-done.1.refs_5_), channel_id=1, source_target_pairs={{0,2},{1,15},{2,4},{3,1},{4,6},{5,3},{6,8},{7,5},{8,10},{9,7},{10,... | collective-permute-start | bytes 1572872 | tf_op jit(solution)/shard_map/ppermute | solution.py:43
  25.7 26.5 %collective-permute-start.18 = (bf16[2048,512]{1,0:T(8,128)(2,1)S(1)}, bf16[2048,512]{1,0:T(8,128)(2,1)S(1)}, u32[]{:S(2)}, u32[]{:S(2)}) collective-permute-start(bf16[2048,512]{1,0:T(8,128)(2,1)S(1)} %join.3.refs_0_), channel_id=1, source_target_pairs={{0,64},{1,17},{2,66},{3,19},{4,68},{5,21},{6,70},{7,23},{8,72},{9,... | collective-permute-start | bytes 6291464 | tf_op jit(solution)/shard_map/ppermute | solution.py:43
  26.9 25.3 %collective-permute-start.19 = (bf16[2048,512]{1,0:T(8,128)(2,1)S(1)}, bf16[2048,512]{1,0:T(8,128)(2,1)S(1)}, u32[]{:S(2)}, u32[]{:S(2)}) collective-permute-start(bf16[2048,512]{1,0:T(8,128)(2,1)S(1)} %join.3.refs_0_), channel_id=1, source_target_pairs={{0,192},{1,49},{2,194},{3,51},{4,196},{5,53},{6,198},{7,55},{8,200... | collective-permute-start | bytes 6291464 | tf_op jit(solution)/shard_map/ppermute | solution.py:43
  28.4 8.3 %collective-permute-start.6 = (bf16[512,512]{1,0:T(8,128)(2,1)S(1)}, bf16[512,512]{1,0:T(8,128)(2,1)S(1)}, u32[]{:S(2)}, u32[]{:S(2)}) collective-permute-start(bf16[512,512]{1,0:T(8,128)(2,1)S(1)} %collective-permute-done.refs_1_), channel_id=1, source_target_pairs={{0,2},{1,15},{2,4},{3,1},{4,6},{5,3},{6,8},{7,5},{8,10},{9,7},{10,... | collective-permute-start | bytes 1572872 | tf_op jit(solution)/shard_map/ppermute | solution.py:43
  29.1 8.3 %collective-permute-start.7 = (bf16[512,512]{1,0:T(8,128)(2,1)S(1)}, bf16[512,512]{1,0:T(8,128)(2,1)S(1)}, u32[]{:S(2)}, u32[]{:S(2)}) collective-permute-start(bf16[512,512]{1,0:T(8,128)(2,1)S(1)} %collective-permute-done.refs_1_), channel_id=1, source_target_pairs={{0,1},{1,0},{2,3},{3,2},{4,5},{5,4},{6,7},{7,6},{8,9},{9,8},{10,11... | collective-permute-start | bytes 1572872 | tf_op jit(solution)/shard_map/ppermute | solution.py:43
  29.1 13.2 %collective-permute-start.11 = (bf16[512,512]{1,0:T(8,128)(2,1)S(1)}, bf16[512,512]{1,0:T(8,128)(2,1)S(1)}, u32[]{:S(2)}, u32[]{:S(2)}) collective-permute-start(bf16[512,512]{1,0:T(8,128)(2,1)S(1)} %collective-permute-done.2.refs_6_), channel_id=1, source_target_pairs={{0,2},{1,15},{2,4},{3,1},{4,6},{5,3},{6,8},{7,5},{8,10},{9,7},{10,... | collective-permute-start | bytes 1572872 | tf_op jit(solution)/shard_map/ppermute | solution.py:43
  36.7 6.4 %collective-permute-start.12 = (bf16[512,512]{1,0:T(8,128)(2,1)S(1)}, bf16[512,512]{1,0:T(8,128)(2,1)S(1)}, u32[]{:S(2)}, u32[]{:S(2)}) collective-permute-start(bf16[512,512]{1,0:T(8,128)(2,1)S(1)} %collective-permute-done.2.refs_6_), channel_id=1, source_target_pairs={{0,1},{1,0},{2,3},{3,2},{4,5},{5,4},{6,7},{7,6},{8,9},{9,8},{10,11... | collective-permute-start | bytes 1572872 | tf_op jit(solution)/shard_map/ppermute | solution.py:43
  37.5 10.5 %collective-permute-start.8 = (bf16[512,512]{1,0:T(8,128)(2,1)S(1)}, bf16[512,512]{1,0:T(8,128)(2,1)S(1)}, u32[]{:S(2)}, u32[]{:S(2)}) collective-permute-start(bf16[512,512]{1,0:T(8,128)(2,1)S(1)} %collective-permute-done.6.refs_2_), channel_id=1, source_target_pairs={{0,2},{1,15},{2,4},{3,1},{4,6},{5,3},{6,8},{7,5},{8,10},{9,7},{10,... | collective-permute-start | bytes 1572872 | tf_op jit(solution)/shard_map/ppermute | solution.py:43
  42.4 6.4 %collective-permute-start.9 = (bf16[512,512]{1,0:T(8,128)(2,1)S(1)}, bf16[512,512]{1,0:T(8,128)(2,1)S(1)}, u32[]{:S(2)}, u32[]{:S(2)}) collective-permute-start(bf16[512,512]{1,0:T(8,128)(2,1)S(1)} %collective-permute-done.6.refs_2_), channel_id=1, source_target_pairs={{0,1},{1,0},{2,3},{3,2},{4,5},{5,4},{6,7},{7,6},{8,9},{9,8},{10,11... | collective-permute-start | bytes 1572872 | tf_op jit(solution)/shard_map/ppermute | solution.py:43
  43.1 12.0 %collective-permute-start.13 = (bf16[512,512]{1,0:T(8,128)(2,1)S(1)}, bf16[512,512]{1,0:T(8,128)(2,1)S(1)}, u32[]{:S(2)}, u32[]{:S(2)}) collective-permute-start(bf16[512,512]{1,0:T(8,128)(2,1)S(1)} %collective-permute-done.11.refs_7_), channel_id=1, source_target_pairs={{0,2},{1,15},{2,4},{3,1},{4,6},{5,3},{6,8},{7,5},{8,10},{9,7},{10,... | collective-permute-start | bytes 1572872 | tf_op jit(solution)/shard_map/ppermute | solution.py:43
  48.0 7.1 %collective-permute-start.16 = (bf16[512,512]{1,0:T(8,128)(2,1)S(1)}, bf16[512,512]{1,0:T(8,128)(2,1)S(1)}, u32[]{:S(2)}, u32[]{:S(2)}) collective-permute-start(bf16[512,512]{1,0:T(8,128)(2,1)S(1)} %collective-permute-done.11.refs_7_), channel_id=1, source_target_pairs={{0,1},{1,0},{2,3},{3,2},{4,5},{5,4},{6,7},{7,6},{8,9},{9,8},{10,11... | collective-permute-start | bytes 1572872 | tf_op jit(solution)/shard_map/ppermute | solution.py:43
  48.7 10.5 %collective-permute-start.10 = (bf16[512,512]{1,0:T(8,128)(2,1)S(1)}, bf16[512,512]{1,0:T(8,128)(2,1)S(1)}, u32[]{:S(2)}, u32[]{:S(2)}) collective-permute-start(bf16[512,512]{1,0:T(8,128)(2,1)S(1)} %collective-permute-done.8.refs_3_), channel_id=1, source_target_pairs={{0,2},{1,15},{2,4},{3,1},{4,6},{5,3},{6,8},{7,5},{8,10},{9,7},{10,... | collective-permute-start | bytes 1572872 | tf_op jit(solution)/shard_map/ppermute | solution.py:43
  52.2 14.9 %collective-permute-start.20 = (bf16[1024,512]{1,0:T(8,128)(2,1)S(1)}, bf16[1024,512]{1,0:T(8,128)(2,1)S(1)}, u32[]{:S(2)}, u32[]{:S(2)}) collective-permute-start(bf16[1024,512]{1,0:T(8,128)(2,1)S(1)} %slice.24), channel_id=1, source_target_pairs={{0,64},{1,17},{2,66},{3,19},{4,68},{5,21},{6,70},{7,23},{8,72},{9,... | collective-permute-start | bytes 3145736 | tf_op jit(solution)/shard_map/ppermute | solution.py:43
  52.4 16.1 %collective-permute-start.21 = (bf16[1024,512]{1,0:T(8,128)(2,1)S(1)}, bf16[1024,512]{1,0:T(8,128)(2,1)S(1)}, u32[]{:S(2)}, u32[]{:S(2)}) collective-permute-start(bf16[1024,512]{1,0:T(8,128)(2,1)S(1)} %slice.25), channel_id=1, source_target_pairs={{0,192},{1,49},{2,194},{3,51},{4,196},{5,53},{6,198},{7,55},{8,200... | collective-permute-start | bytes 3145736 | tf_op jit(solution)/shard_map/ppermute | solution.py:43
  55.1 4.9 %collective-permute-start.14 = (bf16[512,512]{1,0:T(8,128)(2,1)S(1)}, bf16[512,512]{1,0:T(8,128)(2,1)S(1)}, u32[]{:S(2)}, u32[]{:S(2)}) collective-permute-start(bf16[512,512]{1,0:T(8,128)(2,1)S(1)} %collective-permute-done.8.refs_3_), channel_id=1, source_target_pairs={{0,1},{1,0},{2,3},{3,2},{4,5},{5,4},{6,7},{7,6},{8,9},{9,8},{10,11... | collective-permute-start | bytes 1572872 | tf_op jit(solution)/shard_map/ppermute | solution.py:43
  55.1 4.8 %collective-permute-start.17 = (bf16[512,512]{1,0:T(8,128)(2,1)S(1)}, bf16[512,512]{1,0:T(8,128)(2,1)S(1)}, u32[]{:S(2)}, u32[]{:S(2)}) collective-permute-start(bf16[512,512]{1,0:T(8,128)(2,1)S(1)} %collective-permute-done.13.refs_8_), channel_id=1, source_target_pairs={{0,1},{1,0},{2,3},{3,2},{4,5},{5,4},{6,7},{7,6},{8,9},{9,8},{10,11... | collective-permute-start | bytes 1572872 | tf_op jit(solution)/shard_map/ppermute | solution.py:43
  59.2 2.3 %collective-permute-start.15 = (bf16[512,512]{1,0:T(8,128)(2,1)S(1)}, bf16[512,512]{1,0:T(8,128)(2,1)S(1)}, u32[]{:S(2)}, u32[]{:S(2)}) collective-permute-start(bf16[512,512]{1,0:T(8,128)(2,1)S(1)} %collective-permute-done.10.refs_4_), channel_id=1, source_target_pairs={{0,1},{1,0},{2,3},{3,2},{4,5},{5,4},{6,7},{7,6},{8,9},{9,8},{10,11... | collective-permute-start | bytes 1572872 | tf_op jit(solution)/shard_map/ppermute | solution.py:43
  69.2 6.6 %collective-permute-start.22 = (bf16[256,512]{1,0:T(8,128)(2,1)S(1)}, bf16[256,512]{1,0:T(8,128)(2,1)S(1)}, u32[]{:S(2)}, u32[]{:S(2)}) collective-permute-start(bf16[256,512]{1,0:T(8,128)(2,1)S(1)} %get-tuple-element.49.refs_0_), channel_id=1, source_target_pairs={{0,16},{1,65},{2,18},{3,67},{4,20},{5,69},{6,22},{7,71},{8,24},{9,... | collective-permute-start | bytes 786440 | tf_op jit(solution)/shard_map/ppermute | solution.py:43
  70.2 5.7 %collective-permute-start.25 = (bf16[256,512]{1,0:T(8,128)(2,1)S(1)}, bf16[256,512]{1,0:T(8,128)(2,1)S(1)}, u32[]{:S(2)}, u32[]{:S(2)}) collective-permute-start(bf16[256,512]{1,0:T(8,128)(2,1)S(1)} %get-tuple-element.50.refs_1_), channel_id=1, source_target_pairs={{0,48},{1,193},{2,50},{3,195},{4,52},{5,197},{6,54},{7,199},{8,56}... | collective-permute-start | bytes 786440 | tf_op jit(solution)/shard_map/ppermute | solution.py:43
  72.0 6.9 %collective-permute-start.23 = (bf16[256,512]{1,0:T(8,128)(2,1)S(1)}, bf16[256,512]{1,0:T(8,128)(2,1)S(1)}, u32[]{:S(2)}, u32[]{:S(2)}) collective-permute-start(bf16[256,512]{1,0:T(8,128)(2,1)S(1)} %get-tuple-element.50.refs_1_), channel_id=1, source_target_pairs={{0,16},{1,65},{2,18},{3,67},{4,20},{5,69},{6,22},{7,71},{8,24},{9,... | collective-permute-start | bytes 786440 | tf_op jit(solution)/shard_map/ppermute | solution.py:43
  72.0 9.7 %collective-permute-start.24 = (bf16[256,512]{1,0:T(8,128)(2,1)S(1)}, bf16[256,512]{1,0:T(8,128)(2,1)S(1)}, u32[]{:S(2)}, u32[]{:S(2)}) collective-permute-start(bf16[256,512]{1,0:T(8,128)(2,1)S(1)} %get-tuple-element.49.refs_0_), channel_id=1, source_target_pairs={{0,48},{1,193},{2,50},{3,195},{4,52},{5,197},{6,54},{7,199},{8,56}... | collective-permute-start | bytes 786440 | tf_op jit(solution)/shard_map/ppermute | solution.py:43
  75.8 6.7 %collective-permute-start.26 = (bf16[256,512]{1,0:T(8,128)(2,1)S(1)}, bf16[256,512]{1,0:T(8,128)(2,1)S(1)}, u32[]{:S(2)}, u32[]{:S(2)}) collective-permute-start(bf16[256,512]{1,0:T(8,128)(2,1)S(1)} %collective-permute-done.22.refs_2_), channel_id=1, source_target_pairs={{0,16},{1,65},{2,18},{3,67},{4,20},{5,69},{6,22},{7,71},{8,24},{9,... | collective-permute-start | bytes 786440 | tf_op jit(solution)/shard_map/ppermute | solution.py:43
  75.8 6.7 %collective-permute-start.27 = (bf16[256,512]{1,0:T(8,128)(2,1)S(1)}, bf16[256,512]{1,0:T(8,128)(2,1)S(1)}, u32[]{:S(2)}, u32[]{:S(2)}) collective-permute-start(bf16[256,512]{1,0:T(8,128)(2,1)S(1)} %collective-permute-done.25.refs_1_), channel_id=1, source_target_pairs={{0,48},{1,193},{2,50},{3,195},{4,52},{5,197},{6,54},{7,199},{8,56}... | collective-permute-start | bytes 786440 | tf_op jit(solution)/shard_map/ppermute | solution.py:43
  78.9 15.7 %collective-permute-start.28 = (bf16[1024,512]{1,0:T(8,128)(2,1)S(1)}, bf16[1024,512]{1,0:T(8,128)(2,1)S(1)}, u32[]{:S(2)}, u32[]{:S(2)}) collective-permute-start(bf16[1024,512]{1,0:T(8,128)(2,1)S(1)} %join.4.refs_0_), channel_id=1, source_target_pairs={{0,64},{1,17},{2,66},{3,19},{4,68},{5,21},{6,70},{7,23},{8,72},{9,... | collective-permute-start | bytes 3145736 | tf_op jit(solution)/shard_map/ppermute | solution.py:43
  79.0 15.7 %collective-permute-start.29 = (bf16[1024,512]{1,0:T(8,128)(2,1)S(1)}, bf16[1024,512]{1,0:T(8,128)(2,1)S(1)}, u32[]{:S(2)}, u32[]{:S(2)}) collective-permute-start(bf16[1024,512]{1,0:T(8,128)(2,1)S(1)} %join.4.refs_0_), channel_id=1, source_target_pairs={{0,192},{1,49},{2,194},{3,51},{4,196},{5,53},{6,198},{7,55},{8,200... | collective-permute-start | bytes 3145736 | tf_op jit(solution)/shard_map/ppermute | solution.py:43
  82.6 23.2 %collective-permute-start.30 = (bf16[1024,512]{1,0:T(8,128)(2,1)S(1)}, bf16[1024,512]{1,0:T(8,128)(2,1)S(1)}, u32[]{:S(2)}, u32[]{:S(2)}) collective-permute-start(bf16[1024,512]{1,0:T(8,128)(2,1)S(1)} %join.5.refs_1_), channel_id=1, source_target_pairs={{0,64},{1,17},{2,66},{3,19},{4,68},{5,21},{6,70},{7,23},{8,72},{9,... | collective-permute-start | bytes 3145736 | tf_op jit(solution)/shard_map/ppermute | solution.py:43
  82.7 23.2 %collective-permute-start.31 = (bf16[1024,512]{1,0:T(8,128)(2,1)S(1)}, bf16[1024,512]{1,0:T(8,128)(2,1)S(1)}, u32[]{:S(2)}, u32[]{:S(2)}) collective-permute-start(bf16[1024,512]{1,0:T(8,128)(2,1)S(1)} %join.5.refs_1_), channel_id=1, source_target_pairs={{0,192},{1,49},{2,194},{3,51},{4,196},{5,53},{6,198},{7,55},{8,200... | collective-permute-start | bytes 3145736 | tf_op jit(solution)/shard_map/ppermute | solution.py:43
  94.7 16.8 %collective-permute-start.32 = (bf16[512,512]{1,0:T(8,128)(2,1)S(1)}, bf16[512,512]{1,0:T(8,128)(2,1)S(1)}, u32[]{:S(2)}, u32[]{:S(2)}) collective-permute-start(bf16[512,512]{1,0:T(8,128)(2,1)S(1)} %slice.20), channel_id=1, source_target_pairs={{0,64},{1,17},{2,66},{3,19},{4,68},{5,21},{6,70},{7,23},{8,72},{9,... | collective-permute-start | bytes 1572872 | tf_op jit(solution)/shard_map/ppermute | solution.py:43
  94.8 16.7 %collective-permute-start.33 = (bf16[512,512]{1,0:T(8,128)(2,1)S(1)}, bf16[512,512]{1,0:T(8,128)(2,1)S(1)}, u32[]{:S(2)}, u32[]{:S(2)}) collective-permute-start(bf16[512,512]{1,0:T(8,128)(2,1)S(1)} %slice.21), channel_id=1, source_target_pairs={{0,192},{1,49},{2,194},{3,51},{4,196},{5,53},{6,198},{7,55},{8,200... | collective-permute-start | bytes 1572872 | tf_op jit(solution)/shard_map/ppermute | solution.py:43
  105.9 11.2 %collective-permute-start.34 = (bf16[512,512]{1,0:T(8,128)(2,1)S(1)}, bf16[512,512]{1,0:T(8,128)(2,1)S(1)}, u32[]{:S(2)}, u32[]{:S(2)}) collective-permute-start(bf16[512,512]{1,0:T(8,128)(2,1)S(1)} %slice.22), channel_id=1, source_target_pairs={{0,64},{1,17},{2,66},{3,19},{4,68},{5,21},{6,70},{7,23},{8,72},{9,... | collective-permute-start | bytes 1572872 | tf_op jit(solution)/shard_map/ppermute | solution.py:43
  106.1 11.5 %collective-permute-start.35 = (bf16[512,512]{1,0:T(8,128)(2,1)S(1)}, bf16[512,512]{1,0:T(8,128)(2,1)S(1)}, u32[]{:S(2)}, u32[]{:S(2)}) collective-permute-start(bf16[512,512]{1,0:T(8,128)(2,1)S(1)} %slice.23), channel_id=1, source_target_pairs={{0,192},{1,49},{2,194},{3,51},{4,196},{5,53},{6,198},{7,55},{8,200... | collective-permute-start | bytes 1572872 | tf_op jit(solution)/shard_map/ppermute | solution.py:43
